TPU v7x, 256 devices: a whole 4x4x8 slice. The times are simulated.
256 devices in a mesh: gx: 32 (over y, z), gy: 8 (over x, core).
Axes of the slice: x: 4, y: 4, z: 8, core: 2. Of those that a mesh axis runs over, the one named last changes fastest.
Arguments:
- velocities: float32 [3, 32, 8, 20480], P(None, 'gx', 'gy'), may hold values from -6 to 6
- bins: int32 [3, 2, 32, 8, 20480], P(None, None, 'gx', 'gy'), may hold values from 0 to 511, as said below
- offsets: int32 [2, 3], replicated, may hold values from 1 to 3
- axes: int32 [2, 64, 128, 128], P(None, 'gx', 'gy'), may hold values from 0 to 63
- live: int32 [32, 8], P('gx', 'gy'), may hold values from 5120 to 20480, as said below
Outputs:
- new_velocities: float32 [3, 32, 8, 20480], P(None, 'gx', 'gy')
Inputs may be any that keep to these rules, and one draw needn't show every extreme that they name: bins[0] lies in 0 .. 7, bins[1] in 0 .. 63, bins[2] in 0 .. 511, uniform over the brick, also in dead slots. `live`: bricks at either x wall are full (20480); occupancy falls towards the middle of the channel to about a third.
All inputs are finite; a program needn't handle non-finite values.
Results may differ from a plain program's by a relative error of at most 0.0001.
Values sent between devices are 32-bit elements; how exact they have to be, the bound alone decides.
No kernel may reach another device: no remote copies, remote signals or barrier semaphores. Data moves between devices by JAX's collectives and lax.ppermute only.
A program may use at most 64 MiB of HBM per device.

v0:
```python
import functools
import math

import jax
import jax.numpy as jnp
import numpy as np
from jax import lax
from jax.experimental import pallas as pl
from jax.experimental.pallas import tpu as pltpu
from jax.sharding import PartitionSpec as P

FINE = 4
NAXES = 64
STEPS = 2
SLOTS = 20480
LANES = 128
ROWS = SLOTS // LANES
DEPTH = 128
CELLS_X = 2
CELLS_Y = 16
PAIRS = 9
QUADS = 3 * PAIRS
FACE = 8 * PAIRS
SUMS = 3 * FACE
WIDE = 224
AXROWS = STEPS * CELLS_Y
BLOCK = 16
VMEM_LIMIT = 48 * 1024 * 1024

turn_cos = math.cos(130.0 * math.pi / 180.0)
turn_sin = math.sin(130.0 * math.pi / 180.0)
golden = math.pi * (3.0 - math.sqrt(5.0))


def axis_table():
    index = np.arange(NAXES).astype(np.float32)
    height = (np.float32(1.0) - (np.float32(2.0) * index + np.float32(1.0)) / np.float32(NAXES)).astype(np.float32)
    radius = np.sqrt(np.float32(1.0) - height * height).astype(np.float32)
    angle = (index * np.float32(golden)).astype(np.float64)
    rows = np.stack([radius * np.cos(angle), radius * np.sin(angle), height]).astype(np.float32)
    padded = np.zeros((3, 1, LANES), np.float32)
    padded[:, 0, :NAXES] = rows
    return np.broadcast_to(padded, (3, 8, LANES)).copy()


def row_ids(shape):
    return lax.broadcasted_iota(jnp.int32, shape, 0)


def fill_keys(step, bins_ref, offsets_ref, info_ref, key_ref, quad_ref):
    live = info_ref[0]
    at_wall = info_ref[1]
    shape = (ROWS, LANES)
    cell_x = (bins_ref[0, step] + offsets_ref[step, 0]) >> 2
    cell_x = jnp.where(at_wall > 0, jnp.minimum(cell_x, CELLS_X - 1), cell_x)
    cell_y = (bins_ref[1, step] + offsets_ref[step, 1]) >> 2
    cell_z = ((bins_ref[2, step] + offsets_ref[step, 2]) >> 2) & (DEPTH - 1)
    slot = jnp.where(cell_x == 1, 2, cell_x >> 1)
    particle = row_ids(shape) * LANES + lax.broadcasted_iota(jnp.int32, shape, 1)
    quad = slot * PAIRS + (cell_y >> 1)
    key_ref[...] = ((cell_y & 1) * DEPTH + cell_z).astype(jnp.float32)
    quad_ref[...] = jnp.where(particle < live, quad, 100).astype(jnp.float32)


def hot_block(key_ref, base, count):
    ids = [(row_ids((16, LANES)) + 16 * t).astype(jnp.float32).astype(jnp.bfloat16) for t in range(16)]
    one = jnp.ones((16, LANES), jnp.bfloat16)
    zero = jnp.zeros((16, LANES), jnp.bfloat16)
    cols = []
    for r in range(count):
        key = jnp.broadcast_to(key_ref[pl.ds(base + r, 1), :], (16, LANES)).astype(jnp.bfloat16)
        cols.append(jnp.concatenate([jnp.where(key == ids[t], one, zero) for t in range(16)], axis=0))
    return jnp.concatenate(cols, axis=1)


def spread_block(vel_ref, quad_ref, base, count):
    sub = row_ids((8, LANES))
    half = row_ids((16, LANES)) >> 3
    ids = [(half + 2 * t).astype(jnp.float32).astype(jnp.bfloat16) for t in range(WIDE // 16)]
    zero = jnp.zeros((16, LANES), jnp.bfloat16)
    cols = []
    for r in range(count):
        row = pl.ds(base + r, 1)
        part = [jnp.broadcast_to(vel_ref[c, row, :], (8, LANES)) for c in range(3)]
        full = jnp.where((sub == 0) | (sub == 3), part[0], jnp.where((sub == 1) | (sub == 4), part[1], part[2]))
        high = full.astype(jnp.bfloat16).astype(jnp.float32)
        data = jnp.where(sub < 3, high, jnp.where(sub < 6, full - high, jnp.where(sub == 6, 1.0, 0.0)))
        data = jnp.concatenate([data, data], axis=0).astype(jnp.bfloat16)
        quad = jnp.broadcast_to(quad_ref[pl.ds(base + r, 1), :], (16, LANES)).astype(jnp.bfloat16)
        cols.append(jnp.concatenate([jnp.where(quad == ids[t], data, zero) for t in range(WIDE // 16)], axis=0))
    return jnp.concatenate(cols, axis=1)


def add_block(acc_ref, spread, hot):
    acc_ref[...] += lax.dot_general(spread, hot, (((1,), (1,)), ((), ())), preferred_element_type=jnp.float32)


def finish_sums(acc_ref, sums_ref):
    sub = row_ids((8, LANES))
    for q in range(QUADS):
        halves = []
        for parity in range(2):
            part = acc_ref[8 * q:8 * q + 8, parity * DEPTH:(parity + 1) * DEPTH]
            moved = pltpu.roll(part, 5, 0)
            halves.append(jnp.where(sub < 3, part + moved, moved))
        sums_ref[8 * q:8 * q + 8, :] = jnp.where(sub < 4, halves[0], pltpu.roll(halves[1], 4, 0))


def write_faces(info_ref, sums_ref, a_ref, b_ref):
    odd = info_ref[2] > 0
    low = sums_ref[0:FACE, :]
    high = sums_ref[FACE:2 * FACE, :]
    a_ref[0:FACE, :] = jnp.where(odd, high, low)
    b_ref[0:FACE, :] = jnp.where(odd, low, high)


def scatter_kernel(offsets_ref, info_ref, vel_ref, bins_ref, axes_ref, sums_ref, a_ref, b_ref, key_ref, quad_ref, acc_ref):
    fill_keys(0, bins_ref, offsets_ref, info_ref, key_ref, quad_ref)
    acc_ref[...] = jnp.zeros_like(acc_ref)

    def body(turn, carry):
        base = pl.multiple_of(turn * BLOCK, BLOCK)
        add_block(acc_ref, spread_block(vel_ref, quad_ref, base, BLOCK), hot_block(key_ref, base, BLOCK))
        return carry

    lax.fori_loop(0, ROWS // BLOCK, body, 0)
    finish_sums(acc_ref, sums_ref)
    write_faces(info_ref, sums_ref, a_ref, b_ref)
    for step in range(STEPS):
        own = axes_ref[step, 0].astype(jnp.float32)
        a_ref[FACE + step * CELLS_Y:FACE + (step + 1) * CELLS_Y, :] = own
        b_ref[FACE + step * CELLS_Y:FACE + (step + 1) * CELLS_Y, :] = own


def fill_fields(step, info_ref, axes_ref, sums_ref, low_x_ref, high_x_ref, low_y_ref, high_y_ref, axes_x_ref, axes_y_ref, field_ref):
    sub = row_ids((8, LANES))
    field_ref[...] = jnp.zeros_like(field_ref)
    is_count = (sub == 3) | (sub == 7)
    for slot in range(3):
        for pair in range(PAIRS):
            q = slot * PAIRS + pair
            total = sums_ref[8 * q:8 * q + 8, :]
            if slot == 0:
                total = total + low_x_ref[8 * pair:8 * pair + 8, :]
            if slot == 1:
                total = total + high_x_ref[8 * pair:8 * pair + 8, :]
            if pair == 0:
                total = total + jnp.where(sub < 4, low_y_ref[8 * slot:8 * slot + 8, :], 0.0)
            if pair == PAIRS - 1:
                total = total + jnp.where(sub < 4, high_y_ref[8 * slot:8 * slot + 8, :], 0.0)
            count = jnp.where(is_count, total, 0.0)
            count = count + pltpu.roll(count, 7, 0)
            count = count + pltpu.roll(count, 6, 0)
            mean = total / jnp.maximum(count, 1.0)
            high = mean.astype(jnp.bfloat16).astype(jnp.float32)
            rest = mean - high
            index = []
            for parity in range(2):
                column = 2 * pair + parity
                if column == CELLS_Y:
                    row = axes_y_ref[slot:slot + 1, :]
                elif column > CELLS_Y:
                    row = jnp.zeros((1, LANES), jnp.float32)
                elif slot == 1:
                    row = axes_x_ref[column:column + 1, :]
                else:
                    row = axes_ref[step, slot // 2, column:column + 1, :].astype(jnp.float32)
                index.append(jnp.broadcast_to(row, (8, LANES)))
            even = jnp.where(sub < 3, high, jnp.where(sub < 6, pltpu.roll(rest, 3, 0), jnp.where(sub == 6, index[0], 0.0)))
            odd = jnp.where(sub < 3, pltpu.roll(high, 4, 0), jnp.where(sub < 6, pltpu.roll(rest, 7, 0), jnp.where(sub == 6, index[1], 0.0)))
            field_ref[8 * q:8 * q + 8, 0:DEPTH] = even
            field_ref[8 * q:8 * q + 8, DEPTH:2 * DEPTH] = odd


def pick_block(picked, quad_ref, got_ref, base, count):
    for r in range(count):
        quad = jnp.broadcast_to(quad_ref[pl.ds(base + r, 1), :], (8, LANES))
        got = jnp.zeros((8, LANES), jnp.float32)
        for q in range(QUADS):
            got = jnp.where(quad == float(q), picked[8 * q:8 * q + 8, r * LANES:(r + 1) * LANES], got)
        got_ref[8 * r:8 * r + 8, :] = got


def turn_block(vel_ref, out_ref, quad_ref, got_ref, table_ref, base, count):
    for g in range(count // 8):
        rows = pl.ds(pl.multiple_of(base + 8 * g, 8), 8)
        chan = [got_ref[pl.ds(64 * g + k, 8, stride=8), :] for k in range(7)]
        mean = [chan[c] + chan[3 + c] for c in range(3)]
        index = chan[6].astype(jnp.int32)
        axis = [jnp.take_along_axis(table_ref[c], index, axis=1, mode="promise_in_bounds") for c in range(3)]
        vel = [vel_ref[c, rows, :] for c in range(3)]
        rel = [vel[c] - mean[c] for c in range(3)]
        along = (1.0 - turn_cos) * (axis[0] * rel[0] + axis[1] * rel[1] + axis[2] * rel[2])
        alive = quad_ref[rows, :] < 64.0
        for c in range(3):
            d, e = (c + 1) % 3, (c + 2) % 3
            cross = axis[d] * rel[e] - axis[e] * rel[d]
            turned = mean[c] + turn_cos * rel[c] + turn_sin * cross + along * axis[c]
            out_ref[c, rows, :] = jnp.where(alive, turned, vel[c])


def gather_block(field, hot):
    return lax.dot_general(field, hot, (((1,), (0,)), ((), ())), preferred_element_type=jnp.float32)


def turn_kernel(step, offsets_ref, info_ref, vel_ref, bins_ref, axes_ref, table_ref, sums_ref, low_x_ref, high_x_ref,
                low_y_ref, high_y_ref, axes_x_ref, axes_y_ref, *rest):
    last = step == STEPS - 1
    if last:
        out_ref, key_ref, quad_ref, field_ref, got_ref = rest
    else:
        out_ref, next_ref, a_ref, b_ref, key_ref, quad_ref, field_ref, got_ref, key2_ref, quad2_ref, acc_ref = rest
        fill_keys(step + 1, bins_ref, offsets_ref, info_ref, key2_ref, quad2_ref)
        acc_ref[...] = jnp.zeros_like(acc_ref)
    fill_keys(step, bins_ref, offsets_ref, info_ref, key_ref, quad_ref)
    fill_fields(step, info_ref, axes_ref, sums_ref, low_x_ref, high_x_ref, low_y_ref, high_y_ref, axes_x_ref, axes_y_ref, field_ref)

    def body(turn, carry):
        base = pl.multiple_of(turn * BLOCK, BLOCK)
        field = field_ref[...].astype(jnp.bfloat16)
        picked = gather_block(field, hot_block(key_ref, base, BLOCK))
        pick_block(picked, quad_ref, got_ref, base, BLOCK)
        turn_block(vel_ref, out_ref, quad_ref, got_ref, table_ref, base, BLOCK)
        if not last:
            add_block(acc_ref, spread_block(out_ref, quad2_ref, base, BLOCK), hot_block(key2_ref, base, BLOCK))
        return carry

    lax.fori_loop(0, ROWS // BLOCK, body, 0)
    if not last:
        finish_sums(acc_ref, next_ref)
        write_faces(info_ref, next_ref, a_ref, b_ref)


SMEM = pl.BlockSpec(memory_space=pltpu.SMEM)
VMEM = pl.BlockSpec(memory_space=pltpu.VMEM)


def f32(*shape):
    return jax.ShapeDtypeStruct(shape, jnp.float32)


def particle_scratch():
    return [pltpu.VMEM((ROWS, LANES), jnp.float32), pltpu.VMEM((ROWS, LANES), jnp.float32)]


def scatter_call(offsets, info, vel, bins, axes):
    face = f32(FACE + AXROWS, LANES)
    return pl.pallas_call(
        scatter_kernel,
        out_shape=(f32(SUMS, LANES), face, face),
        in_specs=[SMEM, SMEM, VMEM, VMEM, VMEM],
        out_specs=(VMEM, VMEM, VMEM),
        scratch_shapes=particle_scratch() + [pltpu.VMEM((WIDE, 2 * DEPTH), jnp.float32)],
        compiler_params=pltpu.CompilerParams(vmem_limit_bytes=VMEM_LIMIT),
        name="scatter",
    )(offsets, info, vel, bins, axes)


def turn_call(step, offsets, info, vel, bins, axes, table, *exchanged):
    last = step == STEPS - 1
    out_shape = [f32(3, ROWS, LANES)]
    scratch = particle_scratch() + [
        pltpu.VMEM((WIDE, 2 * DEPTH), jnp.float32),
        pltpu.VMEM((8 * BLOCK, LANES), jnp.float32),
    ]
    if not last:
        out_shape += [f32(SUMS, LANES), f32(FACE, LANES), f32(FACE, LANES)]
        scratch += particle_scratch() + [pltpu.VMEM((WIDE, 2 * DEPTH), jnp.float32)]
    return pl.pallas_call(
        functools.partial(turn_kernel, step),
        out_shape=tuple(out_shape),
        in_specs=[SMEM, SMEM] + [VMEM] * (4 + len(exchanged)),
        out_specs=tuple([VMEM] * len(out_shape)),
        scratch_shapes=scratch,
        compiler_params=pltpu.CompilerParams(vmem_limit_bytes=VMEM_LIMIT),
        name="turn",
    )(offsets, info, vel, bins, axes, table, *exchanged)


def swaps(count_x, count_y):
    x_odd, x_even, y_odd, y_even = [], [], [], []
    for i in range(count_x):
        for j in range(count_y):
            here = i * count_y + j
            up = i + 1 if i % 2 == 1 else i - 1
            x_odd.append((here, up * count_y + j if 0 <= up < count_x else i * count_y + (j ^ 1)))
            x_even.append((here, (i ^ 1) * count_y + j))
            y_odd.append((here, i * count_y + ((j + 1 if j % 2 == 1 else j - 1) % count_y)))
            y_even.append((here, i * count_y + (j ^ 1)))
    return x_odd, x_even, y_odd, y_even


def per_device(perms, velocities, bins, offsets, axes, live):
    names = ("gx", "gy")
    x_odd, x_even, y_odd, y_even = perms
    i, j = lax.axis_index("gx"), lax.axis_index("gy")
    last_i = lax.axis_size("gx") - 1
    odd_x, odd_y = i % 2 == 1, j % 2 == 1
    vel = velocities.reshape(3, ROWS, LANES)
    bins = bins.reshape(3, STEPS, ROWS, LANES)
    info = jnp.stack([live.reshape(()), (i == last_i).astype(jnp.int32), odd_x.astype(jnp.int32), odd_y.astype(jnp.int32)])
    table = jnp.asarray(axis_table())
    sums, a, b = scatter_call(offsets, info, vel, bins, axes)
    axes_x = axes_y = None
    for step in range(STEPS):
        got_b = lax.ppermute(b, names, x_even)
        got_a = lax.ppermute(a, names, x_odd)
        from_low = jnp.where(odd_x, got_b, got_a)
        from_high = jnp.where(odd_x, got_a, got_b)
        low_x = jnp.where(i > 0, from_low[:FACE], 0.0)
        high_x = jnp.where(i < last_i, from_high[:FACE], 0.0)
        if step == 0:
            axes_x = [from_high[FACE + s * CELLS_Y:FACE + (s + 1) * CELLS_Y] for s in range(STEPS)]
        plane_0 = sums[0:FACE] + low_x
        plane_2 = sums[FACE:2 * FACE] + high_x
        plane_1 = sums[2 * FACE:]
        bottom = [p[0:4] for p in (plane_0, plane_2, plane_1)]
        top = [p[4 * CELLS_Y:4 * CELLS_Y + 4] for p in (plane_0, plane_2, plane_1)]
        if step == 0:
            own = axes.astype(jnp.float32)
            for s in range(STEPS):
                rows = [own[s, 0, 0:1], axes_x[s][0:1], own[s, 1, 0:1], jnp.zeros((1, LANES), jnp.float32)]
                bottom += rows
                top += rows
        bottom, top = jnp.concatenate(bottom), jnp.concatenate(top)
        got_d = lax.ppermute(jnp.where(odd_y, bottom, top), names, y_even)
        got_c = lax.ppermute(jnp.where(odd_y, top, bottom), names, y_odd)
        from_low = jnp.where(odd_y, got_d, got_c)
        from_high = jnp.where(odd_y, got_c, got_d)
        if step == 0:
            axes_y = [from_high[12 + 4 * s:16 + 4 * s] for s in range(STEPS)]
        low_y = jnp.pad(from_low[:12].reshape(3, 4, LANES), ((0, 0), (0, 4), (0, 0))).reshape(24, LANES)
        high_y = jnp.pad(from_high[:12].reshape(3, 4, LANES), ((0, 0), (0, 4), (0, 0))).reshape(24, LANES)
        done = turn_call(step, offsets, info, vel, bins, axes, table, sums, low_x, high_x, low_y, high_y, axes_x[step], axes_y[step])
        if step < STEPS - 1:
            vel, sums, a, b = done
        else:
            vel = done[0]
    return vel.reshape(velocities.shape)


def solution(mesh):
    placed = (
        P(None, "gx", "gy", None),
        P(None, None, "gx", "gy", None),
        P(),
        P(None, "gx", "gy", None),
        P("gx", "gy"),
    )
    perms = swaps(mesh.shape["gx"], mesh.shape["gy"])
    return jax.shard_map(
        functools.partial(per_device, perms), mesh=mesh, in_specs=placed, out_specs=P(None, "gx", "gy", None), check_vma=False
    )
```

profile of v0, /device:TPU:24, one launch (start us, length us, event | category | flops | bytes accessed | tf_op | source)
XLA Modules:
  0.0 52.3 jit_solution(2893452706933607536)
XLA Ops:
  0.0 0.0 copy-start.4
  0.7 0.1 pad_add_fusion.info_ref
  0.7 0.0 copy-start.6
  0.7 0.0 copy-done.4
  0.8 0.6 %copy-done.6 = s32[2,3]{1,0:T(2,128)S(1)} copy-done((s32[2,3]{1,0:T(2,128)S(1)}, s32[2,3]{1,0:T(2,128)}, u32[]{:S(2)}) %copy-start.6) | copy-done | bytes 48
  1.4 0.0 copy-start
  1.4 1.0 %copy-done = s32[3,2,1,1,20480]{4,3,2,1,0:T(1,128)S(1)} copy-done((s32[3,2,1,1,20480]{4,3,2,1,0:T(1,128)S(1)}, s32[3,2,1,1,20480]{4,3,2,1,0:T(1,128)}, u32[]{:S(2)}) %copy-start) | copy-done | bytes 491544
  2.5 0.0 copy-start.2
  2.5 0.9 %copy-done.2 = f32[3,1,1,20480]{3,2,1,0:T(1,128)S(1)} copy-done((f32[3,1,1,20480]{3,2,1,0:T(1,128)S(1)}, f32[3,1,1,20480]{3,2,1,0:T(1,128)}, u32[]{:S(2)}) %copy-start.2) | copy-done | bytes 245784
  3.4 5.7 %scatter.1 = (f32[216,128]{1,0:T(8,128)S(1)}, f32[104,128]{1,0:T(8,128)S(1)}, f32[104,128]{1,0:T(8,128)S(1)}) custom-call(s32[2,3]{1,0:T(2,128)S(1)} %copy-done.6, s32[4]{0:T(128)S(1)} %pad_add_fusion.info_ref, f32[3,160,128]{2,1,0:T(8,128)S(1)} %bitcast.27, s32[3,2,160,128]{3,2,1,0:T(8,128)S(1)} %bitcast.24, s32[2,2,16,128]{3,2,1,0:T(8,128)S(1)} %copy-done.4), custom_call_target="tpu_custom_call" | custom-call | tf_op jit(solution)/shard_map/scatter/pallas_call | solution.py:248
  9.1 0.0 copy-start.1
  9.1 2.0 %collective-permute-start = (f32[104,128]{1,0:T(8,128)S(1)}, f32[104,128]{1,0:T(8,128)S(1)}, u32[]{:S(2)}, u32[]{:S(2)}) collective-permute-start(f32[104,128]{1,0:T(8,128)S(1)} %get-tuple-element.13), channel_id=1, source_target_pairs={{0,8},{1,9},{2,10},{3,11},{4,12},{5,13},{6,14},{7,15},{8,0},{9,1},... | collective-permute-start | bytes 159752 | tf_op jit(solution)/shard_map/ppermute | solution.py:306
  11.1 5.1 %collective-permute-start.1 = (f32[104,128]{1,0:T(8,128)S(1)}, f32[104,128]{1,0:T(8,128)S(1)}, u32[]{:S(2)}, u32[]{:S(2)}) collective-permute-start(f32[104,128]{1,0:T(8,128)S(1)} %get-tuple-element.14), channel_id=1, source_target_pairs={{0,1},{1,0},{2,3},{3,2},{4,5},{5,4},{6,7},{7,6},{8,16},{9,17},{10,... | collective-permute-start | bytes 159752 | tf_op jit(solution)/shard_map/ppermute | solution.py:307
  16.3 0.0 collective-permute-done
  16.3 2.1 %collective-permute-done.1 = f32[104,128]{1,0:T(8,128)S(1)} collective-permute-done((f32[104,128]{1,0:T(8,128)S(1)}, f32[104,128]{1,0:T(8,128)S(1)}, u32[]{:S(2)}, u32[]{:S(2)}) %collective-permute-start.1) | collective-permute-done | bytes 53280 | tf_op jit(solution)/shard_map/ppermute | solution.py:307
  18.4 0.0 copy-start.3
  18.4 0.1 concatenate.12
  18.5 0.1 concatenate.13
  18.6 0.1 collective-permute-start.2
  18.7 2.9 %collective-permute-start.3 = (f32[20,128]{1,0:T(8,128)S(1)}, f32[20,128]{1,0:T(8,128)S(1)}, u32[]{:S(2)}, u32[]{:S(2)}) collective-permute-start(f32[20,128]{1,0:T(8,128)S(1)} %get-tuple-element.52), channel_id=1, source_target_pairs={{0,7},{1,2},{2,1},{3,4},{4,3},{5,6},{6,5},{7,0},{8,15},{9,10},{10,... | collective-permute-start | bytes 30728 | tf_op jit(solution)/shard_map/ppermute | solution.py:327
  21.6 0.0 collective-permute-done.2
  21.6 1.5 %collective-permute-done.3 = f32[20,128]{1,0:T(8,128)S(1)} collective-permute-done((f32[20,128]{1,0:T(8,128)S(1)}, f32[20,128]{1,0:T(8,128)S(1)}, u32[]{:S(2)}, u32[]{:S(2)}) %collective-permute-start.3) | collective-permute-done | bytes 10272 | tf_op jit(solution)/shard_map/ppermute | solution.py:327
  23.1 0.0 copy-start.7
  23.1 0.6 %copy-done.7 = f32[20,128]{1,0:T(8,128)} copy-done((f32[20,128]{1,0:T(8,128)}, f32[20,128]{1,0:T(8,128)S(1)}, u32[]{:S(2)}) %copy-start.7) | copy-done | bytes 10264
  23.7 0.0 slice-start
  23.7 0.7 %slice-done = f32[12,128]{1,0:T(8,128)S(1)} async-done(((f32[20,128]{1,0:T(8,128)}), f32[12,128]{1,0:T(8,128)S(1)}, s32[]{:S(2)}) %slice-start) | async-done | bytes 6168 | tf_op jit(solution)/shard_map/slice | solution.py:333
  24.4 0.0 copy-start.5
  24.4 0.0 copy-done.1
  24.4 0.0 copy-done.3
  24.4 0.7 %copy-done.5 = f32[3,8,128]{2,1,0:T(8,128)S(1)} copy-done((f32[3,8,128]{2,1,0:T(8,128)S(1)}, f32[3,8,128]{2,1,0:T(8,128)}, u32[]{:S(2)}) %copy-start.5) | copy-done | bytes 12312
  25.1 9.9 %turn.2 = (f32[3,160,128]{2,1,0:T(8,128)S(1)}, f32[216,128]{1,0:T(8,128)S(1)}, f32[72,128]{1,0:T(8,128)S(1)}, f32[72,128]{1,0:T(8,128)S(1)}) custom-call(s32[2,3]{1,0:T(2,128)S(1)} %copy-done.6, s32[4]{0:T(128)S(1)} %pad_add_fusion.info_ref, f32[3,160,128]{2,1,0:T(8,128)S(1)} %bitcast.28, s32[3,2,160,128]{3,2,1,0:T(8,128)S(1)} %bitcast.25, ...), custom_call_target="tpu_custom_call" | custom-call | tf_op jit(solution)/shard_map/turn/pallas_call | solution.py:269
  35.1 0.1 collective-permute-start.4
  35.2 4.2 %collective-permute-start.5 = (f32[72,128]{1,0:T(8,128)S(1)}, f32[72,128]{1,0:T(8,128)S(1)}, u32[]{:S(2)}, u32[]{:S(2)}) collective-permute-start(f32[72,128]{1,0:T(8,128)S(1)} %get-tuple-element.18), channel_id=1, source_target_pairs={{0,1},{1,0},{2,3},{3,2},{4,5},{5,4},{6,7},{7,6},{8,16},{9,17},{10,... | collective-permute-start | bytes 110600 | tf_op jit(solution)/shard_map/ppermute | solution.py:307
  39.4 0.0 collective-permute-done.4
  39.4 1.9 %collective-permute-done.5 = f32[72,128]{1,0:T(8,128)S(1)} collective-permute-done((f32[72,128]{1,0:T(8,128)S(1)}, f32[72,128]{1,0:T(8,128)S(1)}, u32[]{:S(2)}, u32[]{:S(2)}) %collective-permute-start.5) | collective-permute-done | bytes 36896 | tf_op jit(solution)/shard_map/ppermute | solution.py:307
  41.4 2.0 %collective-permute-start.7 = (f32[12,128]{1,0:T(8,128)S(1)}, f32[12,128]{1,0:T(8,128)S(1)}, u32[]{:S(2)}, u32[]{:S(2)}) collective-permute-start(f32[12,128]{1,0:T(8,128)S(1)} %get-tuple-element.57), channel_id=1, source_target_pairs={{0,7},{1,2},{2,1},{3,4},{4,3},{5,6},{6,5},{7,0},{8,15},{9,10},{10,... | collective-permute-start | bytes 18440 | tf_op jit(solution)/shard_map/ppermute | solution.py:327
  43.4 0.0 collective-permute-start.6
  43.4 2.4 %collective-permute-done.7 = f32[12,128]{1,0:T(8,128)S(1)} collective-permute-done((f32[12,128]{1,0:T(8,128)S(1)}, f32[12,128]{1,0:T(8,128)S(1)}, u32[]{:S(2)}, u32[]{:S(2)}) %collective-permute-start.7) | collective-permute-done | bytes 6176 | tf_op jit(solution)/shard_map/ppermute | solution.py:327
  45.8 0.0 collective-permute-done.6
  45.8 6.5 %turn.3 = f32[3,160,128]{2,1,0:T(8,128)} custom-call(s32[2,3]{1,0:T(2,128)S(1)} %copy-done.6, s32[4]{0:T(128)S(1)} %pad_add_fusion.info_ref, f32[3,160,128]{2,1,0:T(8,128)S(1)} %get-tuple-element.15.vel_ref, s32[3,2,160,128]{3,2,1,0:T(8,128)S(1)} %bitcast.26, s32[2,2,16,128]{3,2,1,0:T(8,128)S(1)} %copy-done.4, f32[3,8,128]{2,1,0:T(8,128)S(1)} %copy-done.5, ...), custom_call_target="tpu_custom_call" | custom-call | tf_op jit(solution)/shard_map/turn/pallas_call | solution.py:269
  (27 shorter events, 0.2 us)
Async XLA Ops:
  0.0 0.8 %copy-start.4 = (s32[2,2,16,128]{3,2,1,0:T(8,128)S(1)}, s32[2,2,16,128]{3,2,1,0:T(8,128)}, u32[]{:S(2)}) copy-start(s32[2,2,16,128]{3,2,1,0:T(8,128)} %axes_ref.5) | copy-start | bytes 98308
  0.7 0.7 %copy-start.6 = (s32[2,3]{1,0:T(2,128)S(1)}, s32[2,3]{1,0:T(2,128)}, u32[]{:S(2)}) copy-start(s32[2,3]{1,0:T(2,128)} %offsets_ref.5) | copy-start | bytes 76
  1.4 1.0 %copy-start = (s32[3,2,1,1,20480]{4,3,2,1,0:T(1,128)S(1)}, s32[3,2,1,1,20480]{4,3,2,1,0:T(1,128)}, u32[]{:S(2)}) copy-start(s32[3,2,1,1,20480]{4,3,2,1,0:T(1,128)} %param.7) | copy-start | bytes 1474564
  2.5 0.9 %copy-start.2 = (f32[3,1,1,20480]{3,2,1,0:T(1,128)S(1)}, f32[3,1,1,20480]{3,2,1,0:T(1,128)}, u32[]{:S(2)}) copy-start(f32[3,1,1,20480]{3,2,1,0:T(1,128)} %param.6) | copy-start | bytes 737284
  9.1 15.3 %copy-start.1 = (s32[3,2,1,1,20480]{4,3,2,1,0:T(1,128)S(1)}, s32[3,2,1,1,20480]{4,3,2,1,0:T(1,128)}, u32[]{:S(2)}) copy-start(s32[3,2,1,1,20480]{4,3,2,1,0:T(1,128)} %param.7) | copy-start | bytes 1474564
  9.1 7.1 %collective-permute-start = (f32[104,128]{1,0:T(8,128)S(1)}, f32[104,128]{1,0:T(8,128)S(1)}, u32[]{:S(2)}, u32[]{:S(2)}) collective-permute-start(f32[104,128]{1,0:T(8,128)S(1)} %get-tuple-element.13), channel_id=1, source_target_pairs={{0,8},{1,9},{2,10},{3,11},{4,12},{5,13},{6,14},{7,15},{8,0},{9,1},... | collective-permute-start | bytes 159752 | tf_op jit(solution)/shard_map/ppermute | solution.py:306
  11.1 7.2 %collective-permute-start.1 = (f32[104,128]{1,0:T(8,128)S(1)}, f32[104,128]{1,0:T(8,128)S(1)}, u32[]{:S(2)}, u32[]{:S(2)}) collective-permute-start(f32[104,128]{1,0:T(8,128)S(1)} %get-tuple-element.14), channel_id=1, source_target_pairs={{0,1},{1,0},{2,3},{3,2},{4,5},{5,4},{6,7},{7,6},{8,16},{9,17},{10,... | collective-permute-start | bytes 159752 | tf_op jit(solution)/shard_map/ppermute | solution.py:307
  18.4 6.0 %copy-start.3 = (f32[3,1,1,20480]{3,2,1,0:T(1,128)S(1)}, f32[3,1,1,20480]{3,2,1,0:T(1,128)}, u32[]{:S(2)}) copy-start(f32[3,1,1,20480]{3,2,1,0:T(1,128)} %param.6) | copy-start | bytes 737284
  18.6 3.0 %collective-permute-start.2 = (f32[20,128]{1,0:T(8,128)S(1)}, f32[20,128]{1,0:T(8,128)S(1)}, u32[]{:S(2)}, u32[]{:S(2)}) collective-permute-start(f32[20,128]{1,0:T(8,128)S(1)} %get-tuple-element.51), channel_id=1, source_target_pairs={{0,1},{1,0},{2,3},{3,2},{4,5},{5,4},{6,7},{7,6},{8,9},{9,8},{10,11... | collective-permute-start | bytes 30728 | tf_op jit(solution)/shard_map/ppermute | solution.py:326
  18.7 4.4 %collective-permute-start.3 = (f32[20,128]{1,0:T(8,128)S(1)}, f32[20,128]{1,0:T(8,128)S(1)}, u32[]{:S(2)}, u32[]{:S(2)}) collective-permute-start(f32[20,128]{1,0:T(8,128)S(1)} %get-tuple-element.52), channel_id=1, source_target_pairs={{0,7},{1,2},{2,1},{3,4},{4,3},{5,6},{6,5},{7,0},{8,15},{9,10},{10,... | collective-permute-start | bytes 30728 | tf_op jit(solution)/shard_map/ppermute | solution.py:327
  23.1 0.6 %copy-start.7 = (f32[20,128]{1,0:T(8,128)}, f32[20,128]{1,0:T(8,128)S(1)}, u32[]{:S(2)}) copy-start(f32[20,128]{1,0:T(8,128)S(1)} %broadcast_select_fusion.1) | copy-start | bytes 30724
  23.7 0.7 %slice-start = ((f32[20,128]{1,0:T(8,128)}), f32[12,128]{1,0:T(8,128)S(1)}, s32[]{:S(2)}) async-start(f32[20,128]{1,0:T(8,128)} %copy-done.7), calls=%async_computation | async-start | bytes 16384 | tf_op jit(solution)/shard_map/slice | solution.py:333
  24.4 0.7 %copy-start.5 = (f32[3,8,128]{2,1,0:T(8,128)S(1)}, f32[3,8,128]{2,1,0:T(8,128)}, u32[]{:S(2)}) copy-start(f32[3,8,128]{2,1,0:T(8,128)} %constant.36.clone.table_ref) | copy-start | bytes 36868
  35.1 4.3 %collective-permute-start.4 = (f32[72,128]{1,0:T(8,128)S(1)}, f32[72,128]{1,0:T(8,128)S(1)}, u32[]{:S(2)}, u32[]{:S(2)}) collective-permute-start(f32[72,128]{1,0:T(8,128)S(1)} %get-tuple-element.17), channel_id=1, source_target_pairs={{0,8},{1,9},{2,10},{3,11},{4,12},{5,13},{6,14},{7,15},{8,0},{9,1},... | collective-permute-start | bytes 110600 | tf_op jit(solution)/shard_map/ppermute | solution.py:306
  35.2 6.2 %collective-permute-start.5 = (f32[72,128]{1,0:T(8,128)S(1)}, f32[72,128]{1,0:T(8,128)S(1)}, u32[]{:S(2)}, u32[]{:S(2)}) collective-permute-start(f32[72,128]{1,0:T(8,128)S(1)} %get-tuple-element.18), channel_id=1, source_target_pairs={{0,1},{1,0},{2,3},{3,2},{4,5},{5,4},{6,7},{7,6},{8,16},{9,17},{10,... | collective-permute-start | bytes 110600 | tf_op jit(solution)/shard_map/ppermute | solution.py:307
  41.4 4.4 %collective-permute-start.7 = (f32[12,128]{1,0:T(8,128)S(1)}, f32[12,128]{1,0:T(8,128)S(1)}, u32[]{:S(2)}, u32[]{:S(2)}) collective-permute-start(f32[12,128]{1,0:T(8,128)S(1)} %get-tuple-element.57), channel_id=1, source_target_pairs={{0,7},{1,2},{2,1},{3,4},{4,3},{5,6},{6,5},{7,0},{8,15},{9,10},{10,... | collective-permute-start | bytes 18440 | tf_op jit(solution)/shard_map/ppermute | solution.py:327
  43.4 2.4 %collective-permute-start.6 = (f32[12,128]{1,0:T(8,128)S(1)}, f32[12,128]{1,0:T(8,128)S(1)}, u32[]{:S(2)}, u32[]{:S(2)}) collective-permute-start(f32[12,128]{1,0:T(8,128)S(1)} %get-tuple-element.58), channel_id=1, source_target_pairs={{0,1},{1,0},{2,3},{3,2},{4,5},{5,4},{6,7},{7,6},{8,9},{9,8},{10,11... | collective-permute-start | bytes 18440 | tf_op jit(solution)/shard_map/ppermute | solution.py:326
where the time goes:
time: 52.6 us; the launch traced here: 52.3 us
  Pallas kernels  22.1 us (42%)
  starting transfers between devices  16.4 us (31%)
  waiting for transfers between devices  7.93 us (15%)
  local copies, waits for them, and re-layouts  4.85 us (9%)
  between operations  0.84 us (2%)
    pallas_call x2, Pallas kernels, turn_call(): pl.pallas_call(functools.partial(turn_kernel, step), out_shape=tuple(out_...  16.4 us
    ppermute x2, starting transfers between devices, per_device(): got_a = lax.ppermute(a, names, x_odd)  9.32 us
    pallas_call x1, Pallas kernels, scatter_call(): pl.pallas_call(scatter_kernel, out_shape=(f32(SUMS, LANES), face, face),...  5.71 us
    ppermute x2, starting transfers between devices, per_device(): got_c = lax.ppermute(jnp.where(odd_y, top, bottom), names, y_odd)  4.88 us
    ppermute x2, waiting for transfers between devices, per_device(): got_a = lax.ppermute(a, names, x_odd)  4.02 us
    unnamed x16, local copies, waits for them, and re-layouts  3.94 us
    ppermute x2, waiting for transfers between devices, per_device(): got_c = lax.ppermute(jnp.where(odd_y, top, bottom), names, y_odd)  3.9 us
    ppermute x2, starting transfers between devices, per_device(): got_b = lax.ppermute(b, names, x_even)  2.09 us
  transfers between devices with their start and end apart: 8, of which 4 were waited for; matrix products, arithmetic and copies ran while one was open for 0% of the time, Pallas kernels for 0%

commit v1 on v0

v1 whole, which is shorter than its diff:
```python
import functools
import math

import jax
import jax.numpy as jnp
import numpy as np
from jax import lax
from jax.experimental import pallas as pl
from jax.experimental.pallas import tpu as pltpu
from jax.sharding import PartitionSpec as P

NAXES = 64
STEPS = 2
SLOTS = 20480
LANES = 128
ROWS = SLOTS // LANES
DEPTH = 128
CELLS_X = 2
CELLS_Y = 16
PLANE = 18
COLUMNS = 3 * PLANE
PAIRS = COLUMNS // 2
GROUPS = 7
FACE = 4 * PLANE
SUMS = 32 * GROUPS
WIDE = 8 * 28
AXROWS = STEPS * CELLS_Y
BLOCK = 32
DEAD = 64 * DEPTH
VMEM_LIMIT = 40 * 1024 * 1024

turn_cos = math.cos(130.0 * math.pi / 180.0)
turn_sin = math.sin(130.0 * math.pi / 180.0)
golden = math.pi * (3.0 - math.sqrt(5.0))


def axis_table():
    index = np.arange(NAXES).astype(np.float32)
    height = (np.float32(1.0) - (np.float32(2.0) * index + np.float32(1.0)) / np.float32(NAXES)).astype(np.float32)
    radius = np.sqrt(np.float32(1.0) - height * height).astype(np.float32)
    angle = (index * np.float32(golden)).astype(np.float64)
    rows = np.stack([radius * np.cos(angle), radius * np.sin(angle), height]).astype(np.float32)
    padded = np.zeros((3, 1, LANES), np.float32)
    padded[:, 0, :NAXES] = rows
    return np.broadcast_to(padded, (3, 8, LANES)).copy()


def row_ids(shape):
    return lax.broadcasted_iota(jnp.int32, shape, 0)


def cell_code(bins_ref, step, offsets_ref, live, at_wall):
    shape = (ROWS, LANES)
    cell_x = (bins_ref[0] + offsets_ref[step, 0]) >> 2
    cell_x = jnp.where(at_wall, jnp.minimum(cell_x, CELLS_X - 1), cell_x)
    cell_y = (bins_ref[1] + offsets_ref[step, 1]) >> 2
    cell_z = ((bins_ref[2] + offsets_ref[step, 2]) >> 2) & (DEPTH - 1)
    plane = jnp.where(cell_x == 1, 2, cell_x >> 1)
    particle = row_ids(shape) * LANES + lax.broadcasted_iota(jnp.int32, shape, 1)
    code = (plane * PLANE + cell_y) * DEPTH + cell_z
    return jnp.where(particle < live, code, code + DEAD)


def fill_keys(code, key_ref, pair_ref):
    key_ref[...] = (code & 255).astype(jnp.float32)
    pair_ref[...] = (code >> 8).astype(jnp.float32)


def hot_row(key_ref, row):
    key = jnp.broadcast_to(key_ref[row, :], (16, LANES)).astype(jnp.bfloat16)
    one = jnp.ones((16, LANES), jnp.bfloat16)
    zero = jnp.zeros((16, LANES), jnp.bfloat16)
    ids = [(row_ids((16, LANES)) + 16 * t).astype(jnp.float32).astype(jnp.bfloat16) for t in range(16)]
    return jnp.concatenate([jnp.where(key == ids[t], one, zero) for t in range(16)], axis=0)


def spread_row(vel_ref, pair_ref, row):
    sub = row_ids((8, LANES))
    half = row_ids((16, LANES)) >> 3
    zero = jnp.zeros((16, LANES), jnp.bfloat16)
    part = [jnp.broadcast_to(vel_ref[c, row, :], (8, LANES)) for c in range(3)]
    full = jnp.where((sub == 0) | (sub == 3), part[0], jnp.where((sub == 1) | (sub == 4), part[1], part[2]))
    high = full.astype(jnp.bfloat16).astype(jnp.float32)
    data = jnp.where(sub < 3, high, jnp.where(sub < 6, full - high, jnp.where(sub == 6, 1.0, 0.0)))
    data = jnp.concatenate([data, data], axis=0).astype(jnp.bfloat16)
    pair = jnp.broadcast_to(pair_ref[row, :], (16, LANES)).astype(jnp.bfloat16)
    ids = [(half + 2 * t).astype(jnp.float32).astype(jnp.bfloat16) for t in range(WIDE // 16)]
    return jnp.concatenate([jnp.where(pair == ids[t], data, zero) for t in range(WIDE // 16)], axis=0)


def scatter_rows(acc_ref, vel_ref, key_ref, pair_ref, base, count):
    rows = [pl.ds(base + r, 1) for r in range(count)]
    spread = jnp.concatenate([spread_row(vel_ref, pair_ref, row) for row in rows], axis=1)
    hot = jnp.concatenate([hot_row(key_ref, row) for row in rows], axis=1)
    acc_ref[...] += lax.dot_general(spread, hot, (((1,), (1,)), ((), ())), preferred_element_type=jnp.float32)


def finish_sums(acc_ref, sums_ref):
    sub = row_ids((8, LANES))
    for q in range(SUMS // 8):
        halves = []
        for parity in range(2):
            part = acc_ref[8 * q:8 * q + 8, parity * DEPTH:(parity + 1) * DEPTH]
            moved = pltpu.roll(part, 5, 0)
            halves.append(jnp.where(sub < 3, part + moved, moved))
        sums_ref[8 * q:8 * q + 8, :] = jnp.where(sub < 4, halves[0], pltpu.roll(halves[1], 4, 0))


def write_faces(sums_ref, a_ref, b_ref):
    odd = lax.axis_index("gx") % 2 == 1
    low = sums_ref[0:FACE, :]
    high = sums_ref[FACE:2 * FACE, :]
    a_ref[0:FACE, :] = jnp.where(odd, high, low)
    b_ref[0:FACE, :] = jnp.where(odd, low, high)


def scatter_kernel(offsets_hbm, live_hbm, vel_hbm, bins_hbm, axes_hbm, table_hbm,
                   vel_ref, code_ref, axes_ref, table_ref, sums_ref, a_ref, b_ref,
                   bins_ref, key_ref, pair_ref, acc_ref, offsets_ref, live_ref, sems):
    copies = [
        pltpu.make_async_copy(offsets_hbm, offsets_ref, sems.at[0]),
        pltpu.make_async_copy(live_hbm, live_ref, sems.at[1]),
        pltpu.make_async_copy(bins_hbm.at[:, 0], bins_ref.at[0], sems.at[2]),
        pltpu.make_async_copy(vel_hbm, vel_ref, sems.at[3]),
        pltpu.make_async_copy(bins_hbm.at[:, 1], bins_ref.at[1], sems.at[4]),
        pltpu.make_async_copy(axes_hbm, axes_ref, sems.at[5]),
        pltpu.make_async_copy(table_hbm, table_ref, sems.at[6]),
    ]
    for copy in copies:
        copy.start()
    acc_ref[...] = jnp.zeros_like(acc_ref)
    at_wall = lax.axis_index("gx") == lax.axis_size("gx") - 1
    for copy in copies[:3]:
        copy.wait()
    live = live_ref[0, 0]
    code = cell_code(bins_ref.at[0], 0, offsets_ref, live, at_wall)
    code_ref[0] = code
    fill_keys(code, key_ref, pair_ref)
    copies[3].wait()

    def body(turn, carry):
        scatter_rows(acc_ref, vel_ref, key_ref, pair_ref, pl.multiple_of(turn * BLOCK, BLOCK), BLOCK)
        return carry

    lax.fori_loop(0, ROWS // BLOCK, body, 0)
    finish_sums(acc_ref, sums_ref)
    write_faces(sums_ref, a_ref, b_ref)
    for copy in copies[4:]:
        copy.wait()
    code_ref[1] = cell_code(bins_ref.at[1], 1, offsets_ref, live, at_wall)
    for step in range(STEPS):
        own = axes_ref[step, 0].astype(jnp.float32)
        a_ref[FACE + step * CELLS_Y:FACE + (step + 1) * CELLS_Y, :] = own
        b_ref[FACE + step * CELLS_Y:FACE + (step + 1) * CELLS_Y, :] = own


def fill_fields(step, axes_ref, sums_ref, a_ref, b_ref, c_ref, d_ref, first, total_ref, index_ref, packed_ref, mean_ref):
    i, j = lax.axis_index("gx"), lax.axis_index("gy")
    odd_x, odd_y = i % 2 == 1, j % 2 == 1
    first_a, first_b, first_c, first_d = first
    low_x = jnp.where(odd_x, b_ref[0:FACE, :], a_ref[0:FACE, :])
    high_x = jnp.where(odd_x, a_ref[0:FACE, :], b_ref[0:FACE, :])
    total_ref[0:FACE, :] = sums_ref[0:FACE, :] + jnp.where(i > 0, low_x, 0.0)
    total_ref[FACE:2 * FACE, :] = sums_ref[FACE:2 * FACE, :] + jnp.where(i < lax.axis_size("gx") - 1, high_x, 0.0)
    total_ref[2 * FACE:, :] = sums_ref[2 * FACE:, :]
    low_y = jnp.where(odd_y, d_ref[...], c_ref[...])
    high_y = jnp.where(odd_y, c_ref[...], d_ref[...])
    index_ref[...] = jnp.zeros_like(index_ref)
    rows = slice(FACE + step * CELLS_Y, FACE + (step + 1) * CELLS_Y)
    index_ref[0:CELLS_Y, :] = axes_ref[step, 0]
    index_ref[PLANE:PLANE + CELLS_Y, :] = jnp.where(odd_x, first_a[rows, :], first_b[rows, :]).astype(jnp.int32)
    index_ref[2 * PLANE:2 * PLANE + CELLS_Y, :] = axes_ref[step, 1]
    rows = slice(12 + 4 * step, 15 + 4 * step)
    index_y = jnp.where(odd_y, first_c[rows, :], first_d[rows, :]).astype(jnp.int32)
    for plane in range(3):
        top = 4 * (plane * PLANE + CELLS_Y)
        total_ref[plane * FACE:plane * FACE + 4, :] += low_y[4 * plane:4 * plane + 4, :]
        total_ref[top:top + 4, :] += high_y[4 * plane:4 * plane + 4, :]
        index_ref[plane * PLANE + CELLS_Y:plane * PLANE + CELLS_Y + 1, :] = index_y[plane:plane + 1, :]
    first_mean = []
    for g in range(GROUPS):
        count = jnp.maximum(total_ref[pl.ds(32 * g + 3, 8, stride=4), :], 1.0)
        mean = [total_ref[pl.ds(32 * g + c, 8, stride=4), :] / count for c in range(3)]
        first_mean.append(mean[0])
        mean_ref[0, 8 * g:8 * g + 8, :] = mean[1]
        mean_ref[1, 8 * g:8 * g + 8, :] = mean[2]
    largest = functools.reduce(jnp.maximum, [jnp.abs(m) for m in first_mean])
    largest = jnp.maximum(jnp.max(largest, axis=(0, 1), keepdims=True), 1e-30)
    scale = jnp.broadcast_to(2.0 ** 24 / largest, (8, LANES))
    for g in range(GROUPS):
        whole = (first_mean[g] * scale).astype(jnp.int32)
        packed_ref[8 * g:8 * g + 8, :] = whole * NAXES + index_ref[8 * g:8 * g + 8, :]
    return jnp.broadcast_to(largest * 2.0 ** -24, (8, LANES))


def pick(table, index):
    return jnp.take_along_axis(table, index, axis=1, mode="promise_in_bounds")


def turn_rows(vel_ref, out_ref, code_ref, packed_ref, mean_ref, table_ref, unit, got_packed, got_mean, base, count):
    for r in range(count):
        code = jnp.broadcast_to(code_ref[pl.ds(base + r, 1), :], (8, LANES))
        z = code & (DEPTH - 1)
        group = code >> 10
        for g in range(GROUPS):
            rows = slice(8 * g, 8 * g + 8)
            found = [pick(packed_ref[rows, :], z), pick(mean_ref[0, rows, :], z), pick(mean_ref[1, rows, :], z)]
            if g == 0:
                got = found
            else:
                here = group == g
                got = [jnp.where(here, new, old) for new, old in zip(found, got)]
        got_packed[8 * r:8 * r + 8, :] = got[0]
        got_mean[0, 8 * r:8 * r + 8, :] = got[1]
        got_mean[1, 8 * r:8 * r + 8, :] = got[2]
    for b in range(count // 8):
        rows = pl.ds(pl.multiple_of(base + 8 * b, 8), 8)
        code = code_ref[rows, :]
        sub = (code >> 7) & 7
        masks = [sub == k for k in range(8)]

        def choose(ref):
            value = ref[pl.ds(64 * b, 8, stride=8), :]
            for k in range(1, 8):
                value = jnp.where(masks[k], ref[pl.ds(64 * b + k, 8, stride=8), :], value)
            return value

        packed = choose(got_packed)
        index = packed & (NAXES - 1)
        mean = [(packed >> 6).astype(jnp.float32) * unit, choose(got_mean.at[0]), choose(got_mean.at[1])]
        axis = [pick(table_ref[c], index) for c in range(3)]
        vel = [vel_ref[c, rows, :] for c in range(3)]
        rel = [vel[c] - mean[c] for c in range(3)]
        along = (1.0 - turn_cos) * (axis[0] * rel[0] + axis[1] * rel[1] + axis[2] * rel[2])
        for c in range(3):
            d, e = (c + 1) % 3, (c + 2) % 3
            cross = axis[d] * rel[e] - axis[e] * rel[d]
            turned = mean[c] + turn_cos * rel[c] + turn_sin * cross + along * axis[c]
            out_ref[c, rows, :] = jnp.where(code < DEAD, turned, vel[c])


def turn_kernel(step, vel_ref, code_ref, axes_ref, table_ref, sums_ref, a_ref, b_ref, c_ref, d_ref, *rest):
    last = step == STEPS - 1
    if last:
        first = rest[:4]
        out_ref, total_ref, index_ref, packed_ref, mean_ref, got_packed, got_mean = rest[4:]
    else:
        first = (a_ref, b_ref, c_ref, d_ref)
        out_ref, next_ref, na_ref, nb_ref, total_ref, index_ref, packed_ref, mean_ref, got_packed, got_mean, key_ref, pair_ref, acc_ref = rest
        fill_keys(code_ref[step + 1], key_ref, pair_ref)
        acc_ref[...] = jnp.zeros_like(acc_ref)
    unit = fill_fields(step, axes_ref, sums_ref, a_ref, b_ref, c_ref, d_ref, first, total_ref, index_ref, packed_ref, mean_ref)

    def body(turn, carry):
        base = pl.multiple_of(turn * BLOCK, BLOCK)
        turn_rows(vel_ref, out_ref, code_ref.at[step], packed_ref, mean_ref, table_ref, unit, got_packed, got_mean, base, BLOCK)
        if not last:
            scatter_rows(acc_ref, out_ref, key_ref, pair_ref, base, BLOCK)
        return carry

    lax.fori_loop(0, ROWS // BLOCK, body, 0)
    if not last:
        finish_sums(acc_ref, next_ref)
        write_faces(next_ref, na_ref, nb_ref)


HBM = pl.BlockSpec(memory_space=pltpu.HBM)
VMEM = pl.BlockSpec(memory_space=pltpu.VMEM)


def f32(*shape):
    return jax.ShapeDtypeStruct(shape, jnp.float32)


def i32(*shape):
    return jax.ShapeDtypeStruct(shape, jnp.int32)


def scatter_scratch():
    return [
        pltpu.VMEM((ROWS, LANES), jnp.float32),
        pltpu.VMEM((ROWS, LANES), jnp.float32),
        pltpu.VMEM((WIDE, 2 * DEPTH), jnp.float32),
    ]


def scatter_call(offsets, live, vel, bins, axes, table):
    face = f32(FACE + AXROWS, LANES)
    out_shape = (f32(3, ROWS, LANES), i32(STEPS, ROWS, LANES), i32(*axes.shape), f32(3, 8, LANES), f32(SUMS, LANES), face, face)
    return pl.pallas_call(
        scatter_kernel,
        out_shape=out_shape,
        in_specs=[HBM] * 6,
        out_specs=tuple([VMEM] * len(out_shape)),
        scratch_shapes=[pltpu.VMEM((STEPS, 3, ROWS, LANES), jnp.int32)] + scatter_scratch() + [
            pltpu.SMEM((STEPS, 3), jnp.int32),
            pltpu.SMEM((1, 1), jnp.int32),
            pltpu.SemaphoreType.DMA((7,)),
        ],
        compiler_params=pltpu.CompilerParams(vmem_limit_bytes=VMEM_LIMIT),
        name="scatter",
    )(offsets, live, vel, bins, axes, table)


def turn_call(step, *args):
    last = step == STEPS - 1
    out_shape = [f32(3, ROWS, LANES)]
    scratch = [
        pltpu.VMEM((SUMS, LANES), jnp.float32),
        pltpu.VMEM((8 * GROUPS, LANES), jnp.int32),
        pltpu.VMEM((8 * GROUPS, LANES), jnp.int32),
        pltpu.VMEM((2, 8 * GROUPS, LANES), jnp.float32),
        pltpu.VMEM((8 * BLOCK, LANES), jnp.int32),
        pltpu.VMEM((2, 8 * BLOCK, LANES), jnp.float32),
    ]
    if not last:
        out_shape += [f32(SUMS, LANES), f32(FACE, LANES), f32(FACE, LANES)]
        scratch += scatter_scratch()
    return pl.pallas_call(
        functools.partial(turn_kernel, step),
        out_shape=tuple(out_shape),
        in_specs=[VMEM] * len(args),
        out_specs=tuple([VMEM] * len(out_shape)),
        scratch_shapes=scratch,
        compiler_params=pltpu.CompilerParams(vmem_limit_bytes=VMEM_LIMIT),
        name="turn",
    )(*args)


def swaps(count_x, count_y):
    x_odd, x_even, y_odd, y_even = [], [], [], []
    for i in range(count_x):
        for j in range(count_y):
            here = i * count_y + j
            up = i + 1 if i % 2 == 1 else i - 1
            x_odd.append((here, up * count_y + j if 0 <= up < count_x else i * count_y + (j ^ 1)))
            x_even.append((here, (i ^ 1) * count_y + j))
            y_odd.append((here, i * count_y + ((j + 1 if j % 2 == 1 else j - 1) % count_y)))
            y_even.append((here, i * count_y + (j ^ 1)))
    return x_odd, x_even, y_odd, y_even


def y_messages(step, axes, sums, got_a, got_b):
    i = lax.axis_index("gx")
    odd_x = i % 2 == 1
    low_x = jnp.where(odd_x, got_b, got_a)
    high_x = jnp.where(odd_x, got_a, got_b)
    has_low, has_high = i > 0, i < lax.axis_size("gx") - 1
    ends = []
    for start in (0, 4 * CELLS_Y):
        rows = slice(start, start + 4)
        ends.append([
            sums[0:FACE][rows] + jnp.where(has_low, low_x[:FACE][rows], 0.0),
            sums[FACE:2 * FACE][rows] + jnp.where(has_high, high_x[:FACE][rows], 0.0),
            sums[2 * FACE:3 * FACE][rows],
        ])
    if step == 0:
        for s in range(STEPS):
            own = axes[s, :, 0].astype(jnp.float32)
            rows = [own[0:1], high_x[FACE + s * CELLS_Y:FACE + s * CELLS_Y + 1], own[1:2], own[1:2]]
            ends = [end + rows for end in ends]
    return [jnp.concatenate(end) for end in ends]


def per_device(perms, velocities, bins, offsets, axes, live):
    names = ("gx", "gy")
    x_odd, x_even, y_odd, y_even = perms
    odd_y = lax.axis_index("gy") % 2 == 1
    vel, code, axes, table, sums, a, b = scatter_call(
        offsets, live, velocities.reshape(3, ROWS, LANES), bins.reshape(3, STEPS, ROWS, LANES), axes, jnp.asarray(axis_table()))
    first = ()
    for step in range(STEPS):
        got_b = lax.ppermute(b, names, x_even)
        got_a = lax.ppermute(a, names, x_odd)
        bottom, top = y_messages(step, axes, sums, got_a, got_b)
        got_d = lax.ppermute(jnp.where(odd_y, bottom, top), names, y_even)
        got_c = lax.ppermute(jnp.where(odd_y, top, bottom), names, y_odd)
        got = (got_a, got_b, got_c, got_d)
        done = turn_call(step, vel, code, axes, table, sums, *got, *first)
        if step < STEPS - 1:
            vel, sums, a, b = done
            first = got
        else:
            vel = done[0]
    return vel.reshape(velocities.shape)


def solution(mesh):
    placed = (
        P(None, "gx", "gy", None),
        P(None, None, "gx", "gy", None),
        P(),
        P(None, "gx", "gy", None),
        P("gx", "gy"),
    )
    perms = swaps(mesh.shape["gx"], mesh.shape["gy"])
    return jax.shard_map(
        functools.partial(per_device, perms), mesh=mesh, in_specs=placed, out_specs=P(None, "gx", "gy", None), check_vma=False
    )
```

time: 52.6 us -> 50.1 us (0.952)
  waiting for transfers between devices: 7.93 us -> 12.2 us
  starting transfers between devices: 16.4 us -> 13.1 us
  Pallas kernels: 22.1 us -> 20.1 us
  local copies, waits for them, and re-layouts: 4.85 us -> 3.54 us
    ppermute x2, starting transfers between devices: 2.09 us -> 0.01 us  [per_device(): got_b = lax.ppermute(b, names, x_even)]
    ppermute x2, waiting for transfers between devices: 0.01 us -> 2.02 us  [per_device(): got_b = lax.ppermute(b, names, x_even)]
    ppermute x2, waiting for transfers between devices: 4.02 us -> 6.03 us  [per_device(): got_a = lax.ppermute(a, names, x_odd)]
    pallas_call x2, Pallas kernels: 16.4 us -> 15.2 us  [turn_call(): pl.pallas_call(functools.partial(turn_kernel, step), out_shape=tuple(out_...]
    ppermute x2, starting transfers between devices: 9.32 us -> 8.33 us  [per_device(): got_a = lax.ppermute(a, names, x_odd)]
    pallas_call x1, Pallas kernels: 5.71 us -> 4.87 us  [scatter_call(): pl.pallas_call(scatter_kernel, out_shape=out_shape, in_specs=[HBM] * 6, o...]
    slice x10 -> x2, local copies, waits for them, and re-layouts: 0.71 us -> 0.01 us  [the longest x1 0.01 us: y_messages(): own[1:2]]
    unnamed x16 -> x10, local copies, waits for them, and re-layouts: 3.94 us -> 3.4 us
  transfers between devices with their start and end apart: 8 -> 8, of which waited for: 4 -> 5; matrix products, arithmetic and copies ran while one was open for 0% -> 0% of each run, Pallas kernels for 0% -> 0%
where the time goes in v1:
time: 50.1 us; the launch traced here: 49.8 us
  Pallas kernels  20.1 us (40%)
  starting transfers between devices  13.1 us (26%)
  waiting for transfers between devices  12.2 us (24%)
  local copies, waits for them, and re-layouts  3.54 us (7%)
  between operations  0.78 us (2%)
    pallas_call x2, Pallas kernels, turn_call(): pl.pallas_call(functools.partial(turn_kernel, step), out_shape=tuple(out_...  15.2 us
    ppermute x2, starting transfers between devices, per_device(): got_a = lax.ppermute(a, names, x_odd)  8.33 us
    ppermute x2, waiting for transfers between devices, per_device(): got_a = lax.ppermute(a, names, x_odd)  6.03 us
    pallas_call x1, Pallas kernels, scatter_call(): pl.pallas_call(scatter_kernel, out_shape=out_shape, in_specs=[HBM] * 6, o...  4.87 us
    ppermute x2, starting transfers between devices, per_device(): got_c = lax.ppermute(jnp.where(odd_y, top, bottom), names, y_odd)  4.63 us
    ppermute x2, waiting for transfers between devices, per_device(): got_c = lax.ppermute(jnp.where(odd_y, top, bottom), names, y_odd)  4.15 us
    unnamed x10, local copies, waits for them, and re-layouts  3.4 us
    ppermute x2, waiting for transfers between devices, per_device(): got_b = lax.ppermute(b, names, x_even)  2.02 us
  transfers between devices with their start and end apart: 8, of which 5 were waited for; matrix products, arithmetic and copies ran while one was open for 0% of the time, Pallas kernels for 0%

profile of v1, /device:TPU:24, one launch (start us, length us, event | category | flops | bytes accessed | tf_op | source)
XLA Modules:
  0.0 49.8 jit_solution(1631055303834531039)
XLA Ops:
  0.0 0.0 copy-start.3
  0.7 0.0 copy-start.4
  0.7 0.0 copy-done.3
  0.7 0.6 %copy-done.4 = s32[2,3]{1,0:T(2,128)S(1)} copy-done((s32[2,3]{1,0:T(2,128)S(1)}, s32[2,3]{1,0:T(2,128)}, u32[]{:S(2)}) %copy-start.4) | copy-done | bytes 48
  1.3 0.0 copy-start
  1.4 1.0 %copy-done = s32[3,2,1,1,20480]{4,3,2,1,0:T(1,128)S(1)} copy-done((s32[3,2,1,1,20480]{4,3,2,1,0:T(1,128)S(1)}, s32[3,2,1,1,20480]{4,3,2,1,0:T(1,128)}, u32[]{:S(2)}) %copy-start) | copy-done | bytes 491544
  2.4 0.0 copy-start.1
  2.4 0.9 %copy-done.1 = f32[3,1,1,20480]{3,2,1,0:T(1,128)S(1)} copy-done((f32[3,1,1,20480]{3,2,1,0:T(1,128)S(1)}, f32[3,1,1,20480]{3,2,1,0:T(1,128)}, u32[]{:S(2)}) %copy-start.1) | copy-done | bytes 245784
  3.3 0.0 copy-start.2
  3.3 0.8 %copy-done.2 = s32[2,2,16,128]{3,2,1,0:T(8,128)S(1)} copy-done((s32[2,2,16,128]{3,2,1,0:T(8,128)S(1)}, s32[2,2,16,128]{3,2,1,0:T(8,128)}, u32[]{:S(2)}) %copy-start.2) | copy-done | bytes 32792
  4.1 4.9 %scatter.1 = (f32[3,160,128]{2,1,0:T(8,128)S(1)}, s32[2,160,128]{2,1,0:T(8,128)S(1)}, s32[2,2,16,128]{3,2,1,0:T(8,128)S(1)}, f32[3,8,128]{2,1,0:T(8,128)S(1)}, f...) custom-call(s32[2,3]{1,0:T(2,128)S(1)} %copy-done.4, s32[1,1]{1,0:T(1,128)S(6)} %copy.9.live_hbm, ...), custom_call_target="tpu_custom_call" | custom-call | tf_op jit(solution)/shard_map/scatter/pallas_call | solution.py:290
  9.0 6.1 %collective-permute-start = (f32[104,128]{1,0:T(8,128)S(1)}, f32[104,128]{1,0:T(8,128)S(1)}, u32[]{:S(2)}, u32[]{:S(2)}) collective-permute-start(f32[104,128]{1,0:T(8,128)S(1)} %get-tuple-element.21), channel_id=1, source_target_pairs={{0,1},{1,0},{2,3},{3,2},{4,5},{5,4},{6,7},{7,6},{8,16},{9,17},{10,... | collective-permute-start | bytes 159752 | tf_op jit(solution)/shard_map/ppermute | solution.py:374
  15.1 0.0 collective-permute-start.1
  15.1 2.1 %collective-permute-done.a_ref.rest_0_ = f32[104,128]{1,0:T(8,128)S(1)} collective-permute-done((f32[104,128]{1,0:T(8,128)S(1)}, f32[104,128]{1,0:T(8,128)S(1)}, u32[]{:S(2)}, u32[]{:S(2)}) %collective-permute-start) | collective-permute-done | bytes 53280 | tf_op jit(solution)/shard_map/ppermute | solution.py:374
  17.2 2.0 %collective-permute-done.1.b_ref.rest_1_ = f32[104,128]{1,0:T(8,128)S(1)} collective-permute-done((f32[104,128]{1,0:T(8,128)S(1)}, f32[104,128]{1,0:T(8,128)S(1)}, u32[]{:S(2)}, u32[]{:S(2)}) %collective-permute-start.1) | collective-permute-done | bytes 53280 | tf_op jit(solution)/shard_map/ppermute | solution.py:373
  19.3 0.1 concatenate.13
  19.3 0.1 concatenate.12
  19.4 0.1 collective-permute-start.3
  19.5 2.9 %collective-permute-start.2 = (f32[20,128]{1,0:T(8,128)S(1)}, f32[20,128]{1,0:T(8,128)S(1)}, u32[]{:S(2)}, u32[]{:S(2)}) collective-permute-start(f32[20,128]{1,0:T(8,128)S(1)} %get-tuple-element.52), channel_id=1, source_target_pairs={{0,7},{1,2},{2,1},{3,4},{4,3},{5,6},{6,5},{7,0},{8,15},{9,10},{10,... | collective-permute-start | bytes 30728 | tf_op jit(solution)/shard_map/ppermute | solution.py:377
  22.4 0.0 collective-permute-done.3.d_ref.rest_3_
  22.4 1.5 %collective-permute-done.2.c_ref.rest_2_ = f32[20,128]{1,0:T(8,128)S(1)} collective-permute-done((f32[20,128]{1,0:T(8,128)S(1)}, f32[20,128]{1,0:T(8,128)S(1)}, u32[]{:S(2)}, u32[]{:S(2)}) %collective-permute-start.2) | collective-permute-done | bytes 10272 | tf_op jit(solution)/shard_map/ppermute | solution.py:377
  23.9 9.5 %turn.2 = (f32[3,160,128]{2,1,0:T(8,128)S(1)}, f32[224,128]{1,0:T(8,128)S(1)}, f32[72,128]{1,0:T(8,128)S(1)}, f32[72,128]{1,0:T(8,128)S(1)}) custom-call(f32[3,160,128]{2,1,0:T(8,128)S(1)} %get-tuple-element.16.vel_ref, s32[2,160,128]{2,1,0:T(8,128)S(1)} %get-tuple-element.17.code_ref, s32[2,2,16,128]{3,2,1,0:T(8,128)S(1)} %get-tuple-element.18.axes_ref, ...), custom_call_target="tpu_custom_call" | custom-call | tf_op jit(solution)/shard_map/turn/pallas_call | solution.py:319
  33.4 2.2 %collective-permute-start.4 = (f32[72,128]{1,0:T(8,128)S(1)}, f32[72,128]{1,0:T(8,128)S(1)}, u32[]{:S(2)}, u32[]{:S(2)}) collective-permute-start(f32[72,128]{1,0:T(8,128)S(1)} %get-tuple-element.25), channel_id=1, source_target_pairs={{0,1},{1,0},{2,3},{3,2},{4,5},{5,4},{6,7},{7,6},{8,16},{9,17},{10,... | collective-permute-start | bytes 110600 | tf_op jit(solution)/shard_map/ppermute | solution.py:374
  35.6 0.0 collective-permute-start.5
  35.6 4.0 %collective-permute-done.4.a_ref = f32[72,128]{1,0:T(8,128)S(1)} collective-permute-done((f32[72,128]{1,0:T(8,128)S(1)}, f32[72,128]{1,0:T(8,128)S(1)}, u32[]{:S(2)}, u32[]{:S(2)}) %collective-permute-start.4) | collective-permute-done | bytes 36896 | tf_op jit(solution)/shard_map/ppermute | solution.py:374
  39.5 0.0 collective-permute-done.5.b_ref
  39.6 0.1 collective-permute-start.7
  39.7 1.8 %collective-permute-start.6 = (f32[12,128]{1,0:T(8,128)S(1)}, f32[12,128]{1,0:T(8,128)S(1)}, u32[]{:S(2)}, u32[]{:S(2)}) collective-permute-start(f32[12,128]{1,0:T(8,128)S(1)} %get-tuple-element.54), channel_id=1, source_target_pairs={{0,7},{1,2},{2,1},{3,4},{4,3},{5,6},{6,5},{7,0},{8,15},{9,10},{10,... | collective-permute-start | bytes 18440 | tf_op jit(solution)/shard_map/ppermute | solution.py:377
  41.5 0.0 collective-permute-done.7.d_ref
  41.5 2.6 %collective-permute-done.6.c_ref = f32[12,128]{1,0:T(8,128)S(1)} collective-permute-done((f32[12,128]{1,0:T(8,128)S(1)}, f32[12,128]{1,0:T(8,128)S(1)}, u32[]{:S(2)}, u32[]{:S(2)}) %collective-permute-start.6) | collective-permute-done | bytes 6176 | tf_op jit(solution)/shard_map/ppermute | solution.py:377
  44.1 5.7 %turn.3 = f32[3,160,128]{2,1,0:T(8,128)} custom-call(f32[3,160,128]{2,1,0:T(8,128)S(1)} %get-tuple-element.23.vel_ref, s32[2,160,128]{2,1,0:T(8,128)S(1)} %get-tuple-element.17.code_ref, s32[2,2,16,128]{3,2,1,0:T(8,128)S(1)} %get-tuple-element.18.axes_ref, f32[3,8,128]{2,1,0:T(8,128)S(1)} %get-tuple-element.19.table_ref, ...), custom_call_target="tpu_custom_call" | custom-call | tf_op jit(solution)/shard_map/turn/pallas_call | solution.py:319
  (9 shorter events, 0.1 us)
Async XLA Ops:
  0.0 0.7 %copy-start.3 = (f32[3,8,128]{2,1,0:T(8,128)S(1)}, f32[3,8,128]{2,1,0:T(8,128)}, u32[]{:S(2)}) copy-start(f32[3,8,128]{2,1,0:T(8,128)} %constant.36.clone.table_hbm) | copy-start | bytes 36868
  0.7 0.7 %copy-start.4 = (s32[2,3]{1,0:T(2,128)S(1)}, s32[2,3]{1,0:T(2,128)}, u32[]{:S(2)}) copy-start(s32[2,3]{1,0:T(2,128)} %offsets_hbm.1) | copy-start | bytes 76
  1.3 1.0 %copy-start = (s32[3,2,1,1,20480]{4,3,2,1,0:T(1,128)S(1)}, s32[3,2,1,1,20480]{4,3,2,1,0:T(1,128)}, u32[]{:S(2)}) copy-start(s32[3,2,1,1,20480]{4,3,2,1,0:T(1,128)} %param.7) | copy-start | bytes 1474564
  2.4 0.9 %copy-start.1 = (f32[3,1,1,20480]{3,2,1,0:T(1,128)S(1)}, f32[3,1,1,20480]{3,2,1,0:T(1,128)}, u32[]{:S(2)}) copy-start(f32[3,1,1,20480]{3,2,1,0:T(1,128)} %param.6) | copy-start | bytes 737284
  3.3 0.8 %copy-start.2 = (s32[2,2,16,128]{3,2,1,0:T(8,128)S(1)}, s32[2,2,16,128]{3,2,1,0:T(8,128)}, u32[]{:S(2)}) copy-start(s32[2,2,16,128]{3,2,1,0:T(8,128)} %axes_hbm.1) | copy-start | bytes 98308
  9.0 8.2 %collective-permute-start = (f32[104,128]{1,0:T(8,128)S(1)}, f32[104,128]{1,0:T(8,128)S(1)}, u32[]{:S(2)}, u32[]{:S(2)}) collective-permute-start(f32[104,128]{1,0:T(8,128)S(1)} %get-tuple-element.21), channel_id=1, source_target_pairs={{0,1},{1,0},{2,3},{3,2},{4,5},{5,4},{6,7},{7,6},{8,16},{9,17},{10,... | collective-permute-start | bytes 159752 | tf_op jit(solution)/shard_map/ppermute | solution.py:374
  15.1 4.1 %collective-permute-start.1 = (f32[104,128]{1,0:T(8,128)S(1)}, f32[104,128]{1,0:T(8,128)S(1)}, u32[]{:S(2)}, u32[]{:S(2)}) collective-permute-start(f32[104,128]{1,0:T(8,128)S(1)} %get-tuple-element.22), channel_id=1, source_target_pairs={{0,8},{1,9},{2,10},{3,11},{4,12},{5,13},{6,14},{7,15},{8,0},{9,1},... | collective-permute-start | bytes 159752 | tf_op jit(solution)/shard_map/ppermute | solution.py:373
  19.4 3.0 %collective-permute-start.3 = (f32[20,128]{1,0:T(8,128)S(1)}, f32[20,128]{1,0:T(8,128)S(1)}, u32[]{:S(2)}, u32[]{:S(2)}) collective-permute-start(f32[20,128]{1,0:T(8,128)S(1)} %get-tuple-element.51), channel_id=1, source_target_pairs={{0,1},{1,0},{2,3},{3,2},{4,5},{5,4},{6,7},{7,6},{8,9},{9,8},{10,11... | collective-permute-start | bytes 30728 | tf_op jit(solution)/shard_map/ppermute | solution.py:376
  19.5 4.4 %collective-permute-start.2 = (f32[20,128]{1,0:T(8,128)S(1)}, f32[20,128]{1,0:T(8,128)S(1)}, u32[]{:S(2)}, u32[]{:S(2)}) collective-permute-start(f32[20,128]{1,0:T(8,128)S(1)} %get-tuple-element.52), channel_id=1, source_target_pairs={{0,7},{1,2},{2,1},{3,4},{4,3},{5,6},{6,5},{7,0},{8,15},{9,10},{10,... | collective-permute-start | bytes 30728 | tf_op jit(solution)/shard_map/ppermute | solution.py:377
  33.4 6.2 %collective-permute-start.4 = (f32[72,128]{1,0:T(8,128)S(1)}, f32[72,128]{1,0:T(8,128)S(1)}, u32[]{:S(2)}, u32[]{:S(2)}) collective-permute-start(f32[72,128]{1,0:T(8,128)S(1)} %get-tuple-element.25), channel_id=1, source_target_pairs={{0,1},{1,0},{2,3},{3,2},{4,5},{5,4},{6,7},{7,6},{8,16},{9,17},{10,... | collective-permute-start | bytes 110600 | tf_op jit(solution)/shard_map/ppermute | solution.py:374
  35.6 4.0 %collective-permute-start.5 = (f32[72,128]{1,0:T(8,128)S(1)}, f32[72,128]{1,0:T(8,128)S(1)}, u32[]{:S(2)}, u32[]{:S(2)}) collective-permute-start(f32[72,128]{1,0:T(8,128)S(1)} %get-tuple-element.26), channel_id=1, source_target_pairs={{0,8},{1,9},{2,10},{3,11},{4,12},{5,13},{6,14},{7,15},{8,0},{9,1},... | collective-permute-start | bytes 110600 | tf_op jit(solution)/shard_map/ppermute | solution.py:373
  39.6 1.9 %collective-permute-start.7 = (f32[12,128]{1,0:T(8,128)S(1)}, f32[12,128]{1,0:T(8,128)S(1)}, u32[]{:S(2)}, u32[]{:S(2)}) collective-permute-start(f32[12,128]{1,0:T(8,128)S(1)} %get-tuple-element.53), channel_id=1, source_target_pairs={{0,1},{1,0},{2,3},{3,2},{4,5},{5,4},{6,7},{7,6},{8,9},{9,8},{10,11... | collective-permute-start | bytes 18440 | tf_op jit(solution)/shard_map/ppermute | solution.py:376
  39.7 4.4 %collective-permute-start.6 = (f32[12,128]{1,0:T(8,128)S(1)}, f32[12,128]{1,0:T(8,128)S(1)}, u32[]{:S(2)}, u32[]{:S(2)}) collective-permute-start(f32[12,128]{1,0:T(8,128)S(1)} %get-tuple-element.54), channel_id=1, source_target_pairs={{0,7},{1,2},{2,1},{3,4},{4,3},{5,6},{6,5},{7,0},{8,15},{9,10},{10,... | collective-permute-start | bytes 18440 | tf_op jit(solution)/shard_map/ppermute | solution.py:377

commit v2 on v1

--- a/solution.py
+++ b/solution.py
@@ -25,7 +25,8 @@
 SUMS = 32 * GROUPS
 WIDE = 8 * 28
 AXROWS = STEPS * CELLS_Y
-BLOCK = 32
+BLOCK_1 = 160
+BLOCK = 80
 DEAD = 64 * DEPTH
 VMEM_LIMIT = 40 * 1024 * 1024
 
@@ -114,38 +115,37 @@
     b_ref[0:FACE, :] = jnp.where(odd, low, high)
 
 
-def scatter_kernel(offsets_hbm, live_hbm, vel_hbm, bins_hbm, axes_hbm, table_hbm,
+def scatter_kernel(live_ref, offsets_hbm, vel_hbm, bins_hbm, axes_hbm, table_hbm,
                    vel_ref, code_ref, axes_ref, table_ref, sums_ref, a_ref, b_ref,
-                   bins_ref, key_ref, pair_ref, acc_ref, offsets_ref, live_ref, sems):
+                   bins_ref, key_ref, pair_ref, acc_ref, offsets_ref, sems):
     copies = [
         pltpu.make_async_copy(offsets_hbm, offsets_ref, sems.at[0]),
-        pltpu.make_async_copy(live_hbm, live_ref, sems.at[1]),
-        pltpu.make_async_copy(bins_hbm.at[:, 0], bins_ref.at[0], sems.at[2]),
-        pltpu.make_async_copy(vel_hbm, vel_ref, sems.at[3]),
-        pltpu.make_async_copy(bins_hbm.at[:, 1], bins_ref.at[1], sems.at[4]),
-        pltpu.make_async_copy(axes_hbm, axes_ref, sems.at[5]),
-        pltpu.make_async_copy(table_hbm, table_ref, sems.at[6]),
+        pltpu.make_async_copy(bins_hbm.at[:, 0], bins_ref.at[0], sems.at[1]),
+        pltpu.make_async_copy(vel_hbm, vel_ref, sems.at[2]),
+        pltpu.make_async_copy(bins_hbm.at[:, 1], bins_ref.at[1], sems.at[3]),
+        pltpu.make_async_copy(axes_hbm, axes_ref, sems.at[4]),
+        pltpu.make_async_copy(table_hbm, table_ref, sems.at[5]),
     ]
     for copy in copies:
         copy.start()
     acc_ref[...] = jnp.zeros_like(acc_ref)
     at_wall = lax.axis_index("gx") == lax.axis_size("gx") - 1
-    for copy in copies[:3]:
+    for copy in copies[:2]:
         copy.wait()
     live = live_ref[0, 0]
     code = cell_code(bins_ref.at[0], 0, offsets_ref, live, at_wall)
     code_ref[0] = code
     fill_keys(code, key_ref, pair_ref)
-    copies[3].wait()
+    copies[2].wait()
 
     def body(turn, carry):
-        scatter_rows(acc_ref, vel_ref, key_ref, pair_ref, pl.multiple_of(turn * BLOCK, BLOCK), BLOCK)
+        scatter_rows(acc_ref, vel_ref, key_ref, pair_ref, pl.multiple_of(turn * BLOCK_1, BLOCK_1), BLOCK_1)
         return carry
 
-    lax.fori_loop(0, ROWS // BLOCK, body, 0)
+    lax.fori_loop(0, ROWS // BLOCK_1, body, 0)
     finish_sums(acc_ref, sums_ref)
     write_faces(sums_ref, a_ref, b_ref)
-    for copy in copies[4:]:
+    for copy in copies[3:]:
         copy.wait()
     code_ref[1] = cell_code(bins_ref.at[1], 1, offsets_ref, live, at_wall)
     for step in range(STEPS):
@@ -239,10 +239,10 @@
             out_ref[c, rows, :] = jnp.where(code < DEAD, turned, vel[c])
 
 
-def turn_kernel(step, vel_ref, code_ref, axes_ref, table_ref, sums_ref, a_ref, b_ref, c_ref, d_ref, *rest):
+def turn_kernel(step, vel_ref, code_ref, axes_ref, table_ref, sums_ref, b_ref, a_ref, c_ref, d_ref, *rest):
     last = step == STEPS - 1
     if last:
-        first = rest[:4]
+        first = (rest[1], rest[0], rest[2], rest[3])
         out_ref, total_ref, index_ref, packed_ref, mean_ref, got_packed, got_mean = rest[4:]
     else:
         first = (a_ref, b_ref, c_ref, d_ref)
@@ -251,20 +251,26 @@
         acc_ref[...] = jnp.zeros_like(acc_ref)
     unit = fill_fields(step, axes_ref, sums_ref, a_ref, b_ref, c_ref, d_ref, first, total_ref, index_ref, packed_ref, mean_ref)
 
+    def turn_block(base):
+        turn_rows(vel_ref, out_ref, code_ref.at[step], packed_ref, mean_ref, table_ref, unit, got_packed, got_mean, base, BLOCK)
+
     def body(turn, carry):
         base = pl.multiple_of(turn * BLOCK, BLOCK)
-        turn_rows(vel_ref, out_ref, code_ref.at[step], packed_ref, mean_ref, table_ref, unit, got_packed, got_mean, base, BLOCK)
         if not last:
-            scatter_rows(acc_ref, out_ref, key_ref, pair_ref, base, BLOCK)
+            scatter_rows(acc_ref, out_ref, key_ref, pair_ref, base - BLOCK, BLOCK)
+        turn_block(base)
         return carry
 
-    lax.fori_loop(0, ROWS // BLOCK, body, 0)
+    turn_block(0)
+    lax.fori_loop(1, ROWS // BLOCK, body, 0)
     if not last:
+        scatter_rows(acc_ref, out_ref, key_ref, pair_ref, ROWS - BLOCK, BLOCK)
         finish_sums(acc_ref, next_ref)
         write_faces(next_ref, na_ref, nb_ref)
 
 
 HBM = pl.BlockSpec(memory_space=pltpu.HBM)
+SMEM = pl.BlockSpec(memory_space=pltpu.SMEM)
 VMEM = pl.BlockSpec(memory_space=pltpu.VMEM)
 
 
@@ -284,22 +290,21 @@
     ]
 
 
-def scatter_call(offsets, live, vel, bins, axes, table):
+def scatter_call(live, offsets, vel, bins, axes, table):
     face = f32(FACE + AXROWS, LANES)
     out_shape = (f32(3, ROWS, LANES), i32(STEPS, ROWS, LANES), i32(*axes.shape), f32(3, 8, LANES), f32(SUMS, LANES), face, face)
     return pl.pallas_call(
         scatter_kernel,
         out_shape=out_shape,
-        in_specs=[HBM] * 6,
+        in_specs=[SMEM] + [HBM] * 5,
         out_specs=tuple([VMEM] * len(out_shape)),
         scratch_shapes=[pltpu.VMEM((STEPS, 3, ROWS, LANES), jnp.int32)] + scatter_scratch() + [
             pltpu.SMEM((STEPS, 3), jnp.int32),
-            pltpu.SMEM((1, 1), jnp.int32),
-            pltpu.SemaphoreType.DMA((7,)),
+            pltpu.SemaphoreType.DMA((6,)),
         ],
         compiler_params=pltpu.CompilerParams(vmem_limit_bytes=VMEM_LIMIT),
         name="scatter",
-    )(offsets, live, vel, bins, axes, table)
+    )(live, offsets, vel, bins, axes, table)
 
 
 def turn_call(step, *args):
@@ -366,8 +371,8 @@
     names = ("gx", "gy")
     x_odd, x_even, y_odd, y_even = perms
     odd_y = lax.axis_index("gy") % 2 == 1
-    vel, code, axes, table, sums, a, b = scatter_call(
-        offsets, live, velocities.reshape(3, ROWS, LANES), bins.reshape(3, STEPS, ROWS, LANES), axes, jnp.asarray(axis_table()))
+    inputs = (offsets, velocities.reshape(3, ROWS, LANES), bins.reshape(3, STEPS, ROWS, LANES), axes, jnp.asarray(axis_table()))
+    vel, code, axes, table, sums, a, b = scatter_call(live, *[pltpu.with_memory_space_constraint(x, pltpu.HBM) for x in inputs])
     first = ()
     for step in range(STEPS):
         got_b = lax.ppermute(b, names, x_even)
@@ -375,7 +380,7 @@
         bottom, top = y_messages(step, axes, sums, got_a, got_b)
         got_d = lax.ppermute(jnp.where(odd_y, bottom, top), names, y_even)
         got_c = lax.ppermute(jnp.where(odd_y, top, bottom), names, y_odd)
-        got = (got_a, got_b, got_c, got_d)
+        got = (got_b, got_a, got_c, got_d)
         done = turn_call(step, vel, code, axes, table, sums, *got, *first)
         if step < STEPS - 1:
             vel, sums, a, b = done

time: 50.1 us -> 41.2 us (0.82)
  Pallas kernels: 20.1 us -> 15.5 us
  waiting for transfers between devices: 12.2 us -> 7.99 us
  starting transfers between devices: 13.1 us -> 16.6 us
  local copies, waits for them, and re-layouts: 3.54 us -> 0.14 us
    pallas_call x2, Pallas kernels: 15.2 us -> 11.1 us  [turn_call(): pl.pallas_call(functools.partial(turn_kernel, step), out_shape=tuple(out_...]
    unnamed x10 -> x0, local copies, waits for them, and re-layouts: 3.4 us -> none
    ppermute x2, starting transfers between devices: 0.01 us -> 2.09 us  [per_device(): got_b = lax.ppermute(b, names, x_even)]
    ppermute x2, waiting for transfers between devices: 2.02 us -> 0.01 us  [per_device(): got_b = lax.ppermute(b, names, x_even)]
    ppermute x2, waiting for transfers between devices: 6.03 us -> 4.04 us  [per_device(): got_a = lax.ppermute(a, names, x_odd)]
    ppermute x2, starting transfers between devices: 8.33 us -> 9.35 us  [per_device(): got_a = lax.ppermute(a, names, x_odd)]
  transfers between devices with their start and end apart: 8 -> 8, of which waited for: 5 -> 4; matrix products, arithmetic and copies ran while one was open for 0% -> 0% of each run, Pallas kernels for 0% -> 0%
where the time goes in v2:
time: 41.2 us; the launch traced here: 41.1 us
  starting transfers between devices  16.6 us (40%)
  Pallas kernels  15.5 us (38%)
  waiting for transfers between devices  7.99 us (19%)
  between operations  0.74 us (2%)
    pallas_call x2, Pallas kernels, turn_call(): pl.pallas_call(functools.partial(turn_kernel, step), out_shape=tuple(out_...  11.1 us
    ppermute x2, starting transfers between devices, per_device(): got_a = lax.ppermute(a, names, x_odd)  9.35 us
    ppermute x2, starting transfers between devices, per_device(): got_c = lax.ppermute(jnp.where(odd_y, top, bottom), names, y_odd)  5.02 us
    pallas_call x1, Pallas kernels, scatter_call(): pl.pallas_call(scatter_kernel, out_shape=out_shape, in_specs=[SMEM] + [HB...  4.41 us
    ppermute x2, waiting for transfers between devices, per_device(): got_a = lax.ppermute(a, names, x_odd)  4.04 us
    ppermute x2, waiting for transfers between devices, per_device(): got_c = lax.ppermute(jnp.where(odd_y, top, bottom), names, y_odd)  3.95 us
    ppermute x2, starting transfers between devices, per_device(): got_b = lax.ppermute(b, names, x_even)  2.09 us
  transfers between devices with their start and end apart: 8, of which 4 were waited for; matrix products, arithmetic and copies ran while one was open for 0% of the time, Pallas kernels for 0%

profile of v2, /device:TPU:24, one launch (start us, length us, event | category | flops | bytes accessed | tf_op | source)
XLA Modules:
  0.0 41.1 jit_solution(14515771366031169930)
XLA Ops:
  0.7 4.4 %scatter.1 = (f32[3,160,128]{2,1,0:T(8,128)S(1)}, s32[2,160,128]{2,1,0:T(8,128)S(1)}, s32[2,2,16,128]{3,2,1,0:T(8,128)S(1)}, f32[3,8,128]{2,1,0:T(8,128)S(1)}, f...) custom-call(s32[1,1]{1,0:T(1,128)S(6)} %copy.9.live_ref, s32[2,3]{1,0:T(2,128)} %offsets_hbm.1, ...), custom_call_target="tpu_custom_call" | custom-call | tf_op jit(solution)/shard_map/scatter/pallas_call | solution.py:296
  5.1 2.0 %collective-permute-start = (f32[104,128]{1,0:T(8,128)S(1)}, f32[104,128]{1,0:T(8,128)S(1)}, u32[]{:S(2)}, u32[]{:S(2)}) collective-permute-start(f32[104,128]{1,0:T(8,128)S(1)} %get-tuple-element.21), channel_id=1, source_target_pairs={{0,8},{1,9},{2,10},{3,11},{4,12},{5,13},{6,14},{7,15},{8,0},{9,1},... | collective-permute-start | bytes 159752 | tf_op jit(solution)/shard_map/ppermute | solution.py:378
  7.1 5.1 %collective-permute-start.1 = (f32[104,128]{1,0:T(8,128)S(1)}, f32[104,128]{1,0:T(8,128)S(1)}, u32[]{:S(2)}, u32[]{:S(2)}) collective-permute-start(f32[104,128]{1,0:T(8,128)S(1)} %get-tuple-element.22), channel_id=1, source_target_pairs={{0,1},{1,0},{2,3},{3,2},{4,5},{5,4},{6,7},{7,6},{8,16},{9,17},{10,... | collective-permute-start | bytes 159752 | tf_op jit(solution)/shard_map/ppermute | solution.py:379
  12.2 0.0 collective-permute-done.b_ref.rest_0_
  12.2 2.1 %collective-permute-done.1.a_ref.rest_1_ = f32[104,128]{1,0:T(8,128)S(1)} collective-permute-done((f32[104,128]{1,0:T(8,128)S(1)}, f32[104,128]{1,0:T(8,128)S(1)}, u32[]{:S(2)}, u32[]{:S(2)}) %collective-permute-start.1) | collective-permute-done | bytes 53280 | tf_op jit(solution)/shard_map/ppermute | solution.py:379
  14.4 0.1 concatenate.13
  14.4 0.1 concatenate.12
  14.5 0.1 collective-permute-start.3
  14.6 2.9 %collective-permute-start.2 = (f32[20,128]{1,0:T(8,128)S(1)}, f32[20,128]{1,0:T(8,128)S(1)}, u32[]{:S(2)}, u32[]{:S(2)}) collective-permute-start(f32[20,128]{1,0:T(8,128)S(1)} %get-tuple-element.52), channel_id=1, source_target_pairs={{0,7},{1,2},{2,1},{3,4},{4,3},{5,6},{6,5},{7,0},{8,15},{9,10},{10,... | collective-permute-start | bytes 30728 | tf_op jit(solution)/shard_map/ppermute | solution.py:382
  17.4 0.0 collective-permute-done.3.d_ref.rest_3_
  17.4 1.6 %collective-permute-done.2.c_ref.rest_2_ = f32[20,128]{1,0:T(8,128)S(1)} collective-permute-done((f32[20,128]{1,0:T(8,128)S(1)}, f32[20,128]{1,0:T(8,128)S(1)}, u32[]{:S(2)}, u32[]{:S(2)}) %collective-permute-start.2) | collective-permute-done | bytes 10272 | tf_op jit(solution)/shard_map/ppermute | solution.py:382
  19.0 5.9 %turn.2 = (f32[3,160,128]{2,1,0:T(8,128)S(1)}, f32[224,128]{1,0:T(8,128)S(1)}, f32[72,128]{1,0:T(8,128)S(1)}, f32[72,128]{1,0:T(8,128)S(1)}) custom-call(f32[3,160,128]{2,1,0:T(8,128)S(1)} %get-tuple-element.16.vel_ref, s32[2,160,128]{2,1,0:T(8,128)S(1)} %get-tuple-element.17.code_ref, s32[2,2,16,128]{3,2,1,0:T(8,128)S(1)} %get-tuple-element.18.axes_ref, ...), custom_call_target="tpu_custom_call" | custom-call | tf_op jit(solution)/shard_map/turn/pallas_call | solution.py:324
  24.9 0.1 collective-permute-start.4
  25.0 4.2 %collective-permute-start.5 = (f32[72,128]{1,0:T(8,128)S(1)}, f32[72,128]{1,0:T(8,128)S(1)}, u32[]{:S(2)}, u32[]{:S(2)}) collective-permute-start(f32[72,128]{1,0:T(8,128)S(1)} %get-tuple-element.26), channel_id=1, source_target_pairs={{0,1},{1,0},{2,3},{3,2},{4,5},{5,4},{6,7},{7,6},{8,16},{9,17},{10,... | collective-permute-start | bytes 110600 | tf_op jit(solution)/shard_map/ppermute | solution.py:379
  29.3 0.0 collective-permute-done.4.b_ref
  29.3 1.9 %collective-permute-done.5.a_ref = f32[72,128]{1,0:T(8,128)S(1)} collective-permute-done((f32[72,128]{1,0:T(8,128)S(1)}, f32[72,128]{1,0:T(8,128)S(1)}, u32[]{:S(2)}, u32[]{:S(2)}) %collective-permute-start.5) | collective-permute-done | bytes 36896 | tf_op jit(solution)/shard_map/ppermute | solution.py:379
  31.2 0.1 collective-permute-start.7
  31.3 2.2 %collective-permute-start.6 = (f32[12,128]{1,0:T(8,128)S(1)}, f32[12,128]{1,0:T(8,128)S(1)}, u32[]{:S(2)}, u32[]{:S(2)}) collective-permute-start(f32[12,128]{1,0:T(8,128)S(1)} %get-tuple-element.54), channel_id=1, source_target_pairs={{0,7},{1,2},{2,1},{3,4},{4,3},{5,6},{6,5},{7,0},{8,15},{9,10},{10,... | collective-permute-start | bytes 18440 | tf_op jit(solution)/shard_map/ppermute | solution.py:382
  33.5 0.0 collective-permute-done.7.d_ref
  33.5 2.4 %collective-permute-done.6.c_ref = f32[12,128]{1,0:T(8,128)S(1)} collective-permute-done((f32[12,128]{1,0:T(8,128)S(1)}, f32[12,128]{1,0:T(8,128)S(1)}, u32[]{:S(2)}, u32[]{:S(2)}) %collective-permute-start.6) | collective-permute-done | bytes 6176 | tf_op jit(solution)/shard_map/ppermute | solution.py:382
  35.9 5.2 %turn.3 = f32[3,160,128]{2,1,0:T(8,128)} custom-call(f32[3,160,128]{2,1,0:T(8,128)S(1)} %get-tuple-element.23.vel_ref, s32[2,160,128]{2,1,0:T(8,128)S(1)} %get-tuple-element.17.code_ref, s32[2,2,16,128]{3,2,1,0:T(8,128)S(1)} %get-tuple-element.18.axes_ref, f32[3,8,128]{2,1,0:T(8,128)S(1)} %get-tuple-element.19.table_ref, ...), custom_call_target="tpu_custom_call" | custom-call | tf_op jit(solution)/shard_map/turn/pallas_call | solution.py:324
  (9 shorter events, 0.1 us)
Async XLA Ops:
  5.1 7.1 %collective-permute-start = (f32[104,128]{1,0:T(8,128)S(1)}, f32[104,128]{1,0:T(8,128)S(1)}, u32[]{:S(2)}, u32[]{:S(2)}) collective-permute-start(f32[104,128]{1,0:T(8,128)S(1)} %get-tuple-element.21), channel_id=1, source_target_pairs={{0,8},{1,9},{2,10},{3,11},{4,12},{5,13},{6,14},{7,15},{8,0},{9,1},... | collective-permute-start | bytes 159752 | tf_op jit(solution)/shard_map/ppermute | solution.py:378
  7.1 7.2 %collective-permute-start.1 = (f32[104,128]{1,0:T(8,128)S(1)}, f32[104,128]{1,0:T(8,128)S(1)}, u32[]{:S(2)}, u32[]{:S(2)}) collective-permute-start(f32[104,128]{1,0:T(8,128)S(1)} %get-tuple-element.22), channel_id=1, source_target_pairs={{0,1},{1,0},{2,3},{3,2},{4,5},{5,4},{6,7},{7,6},{8,16},{9,17},{10,... | collective-permute-start | bytes 159752 | tf_op jit(solution)/shard_map/ppermute | solution.py:379
  14.5 3.0 %collective-permute-start.3 = (f32[20,128]{1,0:T(8,128)S(1)}, f32[20,128]{1,0:T(8,128)S(1)}, u32[]{:S(2)}, u32[]{:S(2)}) collective-permute-start(f32[20,128]{1,0:T(8,128)S(1)} %get-tuple-element.51), channel_id=1, source_target_pairs={{0,1},{1,0},{2,3},{3,2},{4,5},{5,4},{6,7},{7,6},{8,9},{9,8},{10,11... | collective-permute-start | bytes 30728 | tf_op jit(solution)/shard_map/ppermute | solution.py:381
  14.6 4.4 %collective-permute-start.2 = (f32[20,128]{1,0:T(8,128)S(1)}, f32[20,128]{1,0:T(8,128)S(1)}, u32[]{:S(2)}, u32[]{:S(2)}) collective-permute-start(f32[20,128]{1,0:T(8,128)S(1)} %get-tuple-element.52), channel_id=1, source_target_pairs={{0,7},{1,2},{2,1},{3,4},{4,3},{5,6},{6,5},{7,0},{8,15},{9,10},{10,... | collective-permute-start | bytes 30728 | tf_op jit(solution)/shard_map/ppermute | solution.py:382
  24.9 4.3 %collective-permute-start.4 = (f32[72,128]{1,0:T(8,128)S(1)}, f32[72,128]{1,0:T(8,128)S(1)}, u32[]{:S(2)}, u32[]{:S(2)}) collective-permute-start(f32[72,128]{1,0:T(8,128)S(1)} %get-tuple-element.25), channel_id=1, source_target_pairs={{0,8},{1,9},{2,10},{3,11},{4,12},{5,13},{6,14},{7,15},{8,0},{9,1},... | collective-permute-start | bytes 110600 | tf_op jit(solution)/shard_map/ppermute | solution.py:378
  25.0 6.2 %collective-permute-start.5 = (f32[72,128]{1,0:T(8,128)S(1)}, f32[72,128]{1,0:T(8,128)S(1)}, u32[]{:S(2)}, u32[]{:S(2)}) collective-permute-start(f32[72,128]{1,0:T(8,128)S(1)} %get-tuple-element.26), channel_id=1, source_target_pairs={{0,1},{1,0},{2,3},{3,2},{4,5},{5,4},{6,7},{7,6},{8,16},{9,17},{10,... | collective-permute-start | bytes 110600 | tf_op jit(solution)/shard_map/ppermute | solution.py:379
  31.2 2.3 %collective-permute-start.7 = (f32[12,128]{1,0:T(8,128)S(1)}, f32[12,128]{1,0:T(8,128)S(1)}, u32[]{:S(2)}, u32[]{:S(2)}) collective-permute-start(f32[12,128]{1,0:T(8,128)S(1)} %get-tuple-element.53), channel_id=1, source_target_pairs={{0,1},{1,0},{2,3},{3,2},{4,5},{5,4},{6,7},{7,6},{8,9},{9,8},{10,11... | collective-permute-start | bytes 18440 | tf_op jit(solution)/shard_map/ppermute | solution.py:381
  31.3 4.6 %collective-permute-start.6 = (f32[12,128]{1,0:T(8,128)S(1)}, f32[12,128]{1,0:T(8,128)S(1)}, u32[]{:S(2)}, u32[]{:S(2)}) collective-permute-start(f32[12,128]{1,0:T(8,128)S(1)} %get-tuple-element.54), channel_id=1, source_target_pairs={{0,7},{1,2},{2,1},{3,4},{4,3},{5,6},{6,5},{7,0},{8,15},{9,10},{10,... | collective-permute-start | bytes 18440 | tf_op jit(solution)/shard_map/ppermute | solution.py:382

commit v3 on v2

v3 whole, which is shorter than its diff:
```python
import functools
import math

import jax
import jax.numpy as jnp
import numpy as np
from jax import lax
from jax.experimental import pallas as pl
from jax.experimental.pallas import tpu as pltpu
from jax.sharding import PartitionSpec as P

NAXES = 64
STEPS = 2
SLOTS = 20480
LANES = 128
ROWS = SLOTS // LANES
DEPTH = 128
CELLS_X = 2
CELLS_Y = 16
PLANE = 16
EDGE = 3 * PLANE
GROUPS = 7
FACE = 4 * PLANE + 8
SUMS = 32 * GROUPS
EDGES = 24
WIDE = 8 * 28
AXROWS = STEPS * CELLS_Y
BLOCK = 80
LOWEST = 121
DEAD = 64 * DEPTH
VMEM_LIMIT = 40 * 1024 * 1024

turn_cos = math.cos(130.0 * math.pi / 180.0)
turn_sin = math.sin(130.0 * math.pi / 180.0)
golden = math.pi * (3.0 - math.sqrt(5.0))


def axis_table():
    index = np.arange(NAXES).astype(np.float32)
    height = (np.float32(1.0) - (np.float32(2.0) * index + np.float32(1.0)) / np.float32(NAXES)).astype(np.float32)
    radius = np.sqrt(np.float32(1.0) - height * height).astype(np.float32)
    angle = (index * np.float32(golden)).astype(np.float64)
    rows = np.stack([radius * np.cos(angle), radius * np.sin(angle), height]).astype(np.float32)
    padded = np.zeros((3, 1, LANES), np.float32)
    padded[:, 0, :NAXES] = rows
    return np.broadcast_to(padded, (3, 8, LANES)).copy()


def row_ids(shape):
    return lax.broadcasted_iota(jnp.int32, shape, 0)


def cell_code(bins_ref, step, offsets_ref, live, at_wall):
    shape = (ROWS, LANES)
    cell_x = (bins_ref[0] + offsets_ref[step, 0]) >> 2
    cell_x = jnp.where(at_wall, jnp.minimum(cell_x, CELLS_X - 1), cell_x)
    cell_y = (bins_ref[1] + offsets_ref[step, 1]) >> 2
    cell_z = ((bins_ref[2] + offsets_ref[step, 2]) >> 2) & (DEPTH - 1)
    plane = jnp.where(cell_x == 1, 0, 1 + (cell_x >> 1))
    particle = row_ids(shape) * LANES + lax.broadcasted_iota(jnp.int32, shape, 1)
    at_edge = (cell_y == 0) | (cell_y == CELLS_Y)
    column = jnp.where(at_edge, EDGE + 2 * plane + (cell_y >> 4), PLANE * plane + cell_y - 1)
    code = column * DEPTH + cell_z
    return jnp.where(particle < live, code, code + DEAD)


def fill_keys(code, key_ref, pair_ref):
    key_ref[...] = (code & 255).astype(jnp.float32)
    pair_ref[...] = (code >> 8).astype(jnp.float32)


def hot_row(key_ref, row):
    key = jnp.broadcast_to(key_ref[row, :], (16, LANES)).astype(jnp.bfloat16)
    one = jnp.ones((16, LANES), jnp.bfloat16)
    zero = jnp.zeros((16, LANES), jnp.bfloat16)
    ids = [(row_ids((16, LANES)) + 16 * t).astype(jnp.float32).astype(jnp.bfloat16) for t in range(16)]
    return jnp.concatenate([jnp.where(key == ids[t], one, zero) for t in range(16)], axis=0)


def spread_row(vel_ref, pair_ref, row):
    sub = row_ids((8, LANES))
    half = row_ids((16, LANES)) >> 3
    zero = jnp.zeros((16, LANES), jnp.bfloat16)
    part = [jnp.broadcast_to(vel_ref[c, row, :], (8, LANES)) for c in range(3)]
    full = jnp.where((sub == 0) | (sub == 3), part[0], jnp.where((sub == 1) | (sub == 4), part[1], part[2]))
    high = full.astype(jnp.bfloat16).astype(jnp.float32)
    data = jnp.where(sub < 3, high, jnp.where(sub < 6, full - high, jnp.where(sub == 6, 1.0, 0.0)))
    data = jnp.concatenate([data, data], axis=0).astype(jnp.bfloat16)
    pair = jnp.broadcast_to(pair_ref[row, :], (16, LANES)).astype(jnp.bfloat16)
    ids = [(half + 2 * t).astype(jnp.float32).astype(jnp.bfloat16) for t in range(WIDE // 16)]
    return jnp.concatenate([jnp.where(pair == ids[t], data, zero) for t in range(WIDE // 16)], axis=0)


def scatter_rows(acc_ref, vel_ref, key_ref, pair_ref, base, count):
    rows = [pl.ds(base + r, 1) for r in range(count)]
    spread = jnp.concatenate([spread_row(vel_ref, pair_ref, row) for row in rows], axis=1)
    hot = jnp.concatenate([hot_row(key_ref, row) for row in rows], axis=1)
    acc_ref[...] += lax.dot_general(spread, hot, (((1,), (1,)), ((), ())), preferred_element_type=jnp.float32)


def finish_sums(acc_ref, sums_ref):
    sub = row_ids((8, LANES))
    for q in range(SUMS // 8):
        halves = []
        for parity in range(2):
            part = acc_ref[8 * q:8 * q + 8, parity * DEPTH:(parity + 1) * DEPTH]
            moved = pltpu.roll(part, 5, 0)
            halves.append(jnp.where(sub < 3, part + moved, moved))
        sums_ref[8 * q:8 * q + 8, :] = jnp.where(sub < 4, halves[0], pltpu.roll(halves[1], 4, 0))


def write_faces(sums_ref, a_ref, b_ref):
    odd = lax.axis_index("gx") % 2 == 1
    for rows, low_at, high_at in ((4 * PLANE, 4 * PLANE, 8 * PLANE), (8, 4 * EDGE + 8, 4 * EDGE + 16)):
        start = 0 if rows > 8 else 4 * PLANE
        low = sums_ref[low_at:low_at + rows, :]
        high = sums_ref[high_at:high_at + rows, :]
        a_ref[start:start + rows, :] = jnp.where(odd, high, low)
        b_ref[start:start + rows, :] = jnp.where(odd, low, high)


def scatter_kernel(live_ref, offsets_hbm, vel_hbm, bins_hbm, axes_hbm, table_hbm,
                   vel_ref, code_ref, axes_ref, table_ref, sums_ref, a_ref, b_ref,
                   bins_ref, key_ref, pair_ref, acc_ref, offsets_ref, sems):
    copies = [
        pltpu.make_async_copy(offsets_hbm, offsets_ref, sems.at[0]),
        pltpu.make_async_copy(bins_hbm.at[:, 0], bins_ref.at[0], sems.at[1]),
        pltpu.make_async_copy(vel_hbm, vel_ref, sems.at[2]),
        pltpu.make_async_copy(bins_hbm.at[:, 1], bins_ref.at[1], sems.at[3]),
        pltpu.make_async_copy(axes_hbm, axes_ref, sems.at[4]),
        pltpu.make_async_copy(table_hbm, table_ref, sems.at[5]),
    ]
    for copy in copies:
        copy.start()
    acc_ref[...] = jnp.zeros_like(acc_ref)
    at_wall = lax.axis_index("gx") == lax.axis_size("gx") - 1
    for copy in copies[:2]:
        copy.wait()
    live = live_ref[0, 0]
    code = cell_code(bins_ref.at[0], 0, offsets_ref, live, at_wall)
    code_ref[0] = code
    fill_keys(code, key_ref, pair_ref)
    copies[2].wait()

    scatter_rows(acc_ref, vel_ref, key_ref, pair_ref, 0, ROWS)
    finish_sums(acc_ref, sums_ref)
    write_faces(sums_ref, a_ref, b_ref)
    for copy in copies[3:]:
        copy.wait()
    code_ref[1] = cell_code(bins_ref.at[1], 1, offsets_ref, live, at_wall)
    for step in range(STEPS):
        own = axes_ref[step, 0].astype(jnp.float32)
        a_ref[FACE + step * CELLS_Y:FACE + (step + 1) * CELLS_Y, :] = own
        b_ref[FACE + step * CELLS_Y:FACE + (step + 1) * CELLS_Y, :] = own


def pack_fields(total_ref, index_ref, first_ref, second_ref, start, groups):
    for g in range(groups):
        count = jnp.maximum(total_ref[pl.ds(start + 32 * g + 3, 8, stride=4), :], 1.0)
        mean = [total_ref[pl.ds(start + 32 * g + c, 8, stride=4), :] / count for c in range(3)]
        largest = jnp.maximum(jnp.maximum(jnp.abs(mean[0]), jnp.abs(mean[1])), jnp.abs(mean[2]))
        exponent = jnp.floor(jnp.log2(jnp.maximum(largest, 2.0 ** -120)) + 1.0001)
        scale = jnp.exp2(16.0 - exponent)
        x, y, z = [jnp.floor(m * scale + 0.5).astype(jnp.int32) for m in mean]
        z = z + 65536
        rows = slice(8 * g, 8 * g + 8)
        first_ref[rows, :] = (x << 15) | (index_ref[rows, :] << 9) | (z & 511)
        second_ref[rows, :] = (y << 15) | ((exponent.astype(jnp.int32) + LOWEST) << 8) | (z >> 9)


def unpack_fields(first, second):
    unit = jnp.exp2((((second >> 8) & 127) - (LOWEST + 16)).astype(jnp.float32))
    z = ((first & 511) | ((second & 255) << 9)) - 65536
    mean = [part.astype(jnp.float32) * unit for part in (first >> 15, second >> 15, z)]
    return mean, (first >> 9) & (NAXES - 1)


def pick(table, index):
    return jnp.take_along_axis(table, index, axis=1, mode="promise_in_bounds")


def gather_rows(code_ref, first_ref, second_ref, got_ref, base, count, start, groups):
    for r in range(count):
        code = jnp.broadcast_to(code_ref[pl.ds(base + r, 1), :], (8, LANES))
        z = code & (DEPTH - 1)
        group = code >> 10
        got = None
        for g in range(groups):
            rows = slice(8 * g, 8 * g + 8)
            found = [pick(first_ref[rows, :], z), pick(second_ref[rows, :], z)]
            got = found if got is None else [jnp.where(group == start + g, new, old) for new, old in zip(found, got)]
        got_ref[0, 8 * r:8 * r + 8, :] = got[0]
        got_ref[1, 8 * r:8 * r + 8, :] = got[1]


def choose_rows(code, got_ref, b):
    sub = (code >> 7) & 7
    masks = [sub == k for k in range(8)]
    words = []
    for w in range(2):
        value = got_ref[w, pl.ds(64 * b, 8, stride=8), :]
        for k in range(1, 8):
            value = jnp.where(masks[k], got_ref[w, pl.ds(64 * b + k, 8, stride=8), :], value)
        words.append(value)
    return words


def inner_kernel(step, code_ref, axes_ref, sums_ref, *rest):
    middle = len(rest) == 6
    if middle:
        start, groups = 0, 2
        out_ref, index_ref, first_ref, second_ref, got_ref, total_ref = rest
        index_ref[...] = jnp.zeros_like(index_ref)
        index_ref[0:CELLS_Y - 1, :] = axes_ref[step, 1, 1:CELLS_Y, :]
        total_ref[0:4 * PLANE, :] = sums_ref[0:4 * PLANE, :]
    else:
        start, groups = 2, 4
        b_ref, a_ref, first_b_ref, first_a_ref, before_ref, out_ref, index_ref, first_ref, second_ref, got_ref, total_ref = rest
        i = lax.axis_index("gx")
        odd = i % 2 == 1
        low = jnp.where(odd, b_ref[0:4 * PLANE, :], a_ref[0:4 * PLANE, :])
        high = jnp.where(odd, a_ref[0:4 * PLANE, :], b_ref[0:4 * PLANE, :])
        total_ref[0:4 * PLANE, :] = sums_ref[4 * PLANE:8 * PLANE, :] + jnp.where(i > 0, low, 0.0)
        total_ref[4 * PLANE:8 * PLANE, :] = sums_ref[8 * PLANE:12 * PLANE, :] + jnp.where(i < lax.axis_size("gx") - 1, high, 0.0)
        index_ref[...] = jnp.zeros_like(index_ref)
        index_ref[0:CELLS_Y - 1, :] = axes_ref[step, 0, 1:CELLS_Y, :]
        rows = slice(FACE + step * CELLS_Y + 1, FACE + (step + 1) * CELLS_Y)
        index_ref[PLANE:PLANE + CELLS_Y - 1, :] = jnp.where(odd, first_a_ref[rows, :], first_b_ref[rows, :]).astype(jnp.int32)
    pack_fields(total_ref, index_ref, first_ref, second_ref, 0, groups)

    def body(turn, carry):
        base = pl.multiple_of(turn * BLOCK, BLOCK)
        gather_rows(code_ref.at[step], first_ref, second_ref, got_ref, base, BLOCK, start, groups)
        for b in range(BLOCK // 8):
            rows = pl.ds(pl.multiple_of(base + 8 * b, 8), 8)
            code = code_ref[step, rows, :]
            for w, word in enumerate(choose_rows(code, got_ref, b)):
                out_ref[w, rows, :] = word if middle else jnp.where(code < start * 8 * DEPTH, before_ref[w, rows, :], word)
        return carry

    lax.fori_loop(0, ROWS // BLOCK, body, 0)


def turn_kernel(step, vel_ref, code_ref, axes_ref, table_ref, words_ref, edge_ref, c_ref, d_ref, first_edge_ref, first_c_ref, first_d_ref, *rest):
    last = step == STEPS - 1
    out_ref, total_ref, index_ref, first_ref, second_ref, got_ref = rest[:1] + rest[-8 + 3 * last:][:5]
    if not last:
        next_ref, na_ref, nb_ref = rest[1:4]
        key_ref, pair_ref, acc_ref = rest[-3:]
        fill_keys(code_ref[step + 1], key_ref, pair_ref)
        acc_ref[...] = jnp.zeros_like(acc_ref)
    odd = lax.axis_index("gy") % 2 == 1
    sub = row_ids((8, LANES))
    total_ref[...] = jnp.zeros_like(total_ref)
    index_ref[...] = jnp.zeros_like(index_ref)
    index_rows = slice(EDGES + 4 * step, EDGES + 4 * step + 4)
    index_low = first_edge_ref[index_rows, :].astype(jnp.int32)
    index_high = jnp.where(odd, first_c_ref[index_rows, :], first_d_ref[index_rows, :]).astype(jnp.int32)
    for plane in range(3):
        rows = slice(8 * plane, 8 * plane + 8)
        low = jnp.where(odd, d_ref[rows, :], c_ref[rows, :])
        high = jnp.where(odd, c_ref[rows, :], d_ref[rows, :])
        total_ref[rows, :] = edge_ref[rows, :] + pltpu.roll(jnp.where(sub < 4, high, low), 4, 0)
        index_ref[2 * plane:2 * plane + 1, :] = index_low[plane:plane + 1, :]
        index_ref[2 * plane + 1:2 * plane + 2, :] = index_high[plane:plane + 1, :]
    pack_fields(total_ref, index_ref, first_ref, second_ref, 0, 1)

    def body(turn, carry):
        base = pl.multiple_of(turn * BLOCK, BLOCK)
        gather_rows(code_ref.at[step], first_ref, second_ref, got_ref, base, BLOCK, GROUPS - 1, 1)
        for b in range(BLOCK // 8):
            rows = pl.ds(pl.multiple_of(base + 8 * b, 8), 8)
            code = code_ref[step, rows, :]
            words = [jnp.where(code < EDGE * DEPTH, words_ref[w, rows, :], word) for w, word in enumerate(choose_rows(code, got_ref, b))]
            mean, index = unpack_fields(*words)
            axis = [pick(table_ref[c], index) for c in range(3)]
            vel = [vel_ref[c, rows, :] for c in range(3)]
            rel = [vel[c] - mean[c] for c in range(3)]
            along = (1.0 - turn_cos) * (axis[0] * rel[0] + axis[1] * rel[1] + axis[2] * rel[2])
            for c in range(3):
                d, e = (c + 1) % 3, (c + 2) % 3
                cross = axis[d] * rel[e] - axis[e] * rel[d]
                turned = mean[c] + turn_cos * rel[c] + turn_sin * cross + along * axis[c]
                out_ref[c, rows, :] = jnp.where(code < DEAD, turned, vel[c])
        return carry

    lax.fori_loop(0, ROWS // BLOCK, body, 0)
    if not last:
        scatter_rows(acc_ref, out_ref, key_ref, pair_ref, 0, ROWS)
        finish_sums(acc_ref, next_ref)
        write_faces(next_ref, na_ref, nb_ref)


HBM = pl.BlockSpec(memory_space=pltpu.HBM)
SMEM = pl.BlockSpec(memory_space=pltpu.SMEM)
VMEM = pl.BlockSpec(memory_space=pltpu.VMEM)


def f32(*shape):
    return jax.ShapeDtypeStruct(shape, jnp.float32)


def i32(*shape):
    return jax.ShapeDtypeStruct(shape, jnp.int32)


def scatter_scratch():
    return [
        pltpu.VMEM((ROWS, LANES), jnp.float32),
        pltpu.VMEM((ROWS, LANES), jnp.float32),
        pltpu.VMEM((WIDE, 2 * DEPTH), jnp.float32),
    ]


def scatter_call(live, offsets, vel, bins, axes, table):
    face = f32(FACE + AXROWS, LANES)
    out_shape = (f32(3, ROWS, LANES), i32(STEPS, ROWS, LANES), i32(*axes.shape), f32(3, 8, LANES), f32(SUMS, LANES), face, face)
    return pl.pallas_call(
        scatter_kernel,
        out_shape=out_shape,
        in_specs=[SMEM] + [HBM] * 5,
        out_specs=tuple([VMEM] * len(out_shape)),
        scratch_shapes=[pltpu.VMEM((STEPS, 3, ROWS, LANES), jnp.int32)] + scatter_scratch() + [
            pltpu.SMEM((STEPS, 3), jnp.int32),
            pltpu.SemaphoreType.DMA((6,)),
        ],
        compiler_params=pltpu.CompilerParams(vmem_limit_bytes=VMEM_LIMIT),
        name="scatter",
    )(live, offsets, vel, bins, axes, table)


def field_scratch(groups):
    return [
        pltpu.VMEM((8 * groups, LANES), jnp.int32),
        pltpu.VMEM((8 * groups, LANES), jnp.int32),
        pltpu.VMEM((8 * groups, LANES), jnp.int32),
        pltpu.VMEM((2, 8 * BLOCK, LANES), jnp.int32),
    ]


def inner_call(step, *args):
    groups = 2 if len(args) == 3 else 4
    return pl.pallas_call(
        functools.partial(inner_kernel, step),
        out_shape=i32(2, ROWS, LANES),
        in_specs=[VMEM] * len(args),
        out_specs=VMEM,
        scratch_shapes=field_scratch(groups) + [pltpu.VMEM((32 * groups, LANES), jnp.float32)],
        compiler_params=pltpu.CompilerParams(vmem_limit_bytes=VMEM_LIMIT),
        cost_estimate=pl.CostEstimate(flops=0, bytes_accessed=8000000, transcendentals=0),
        name="inner",
    )(*args)


def turn_call(step, *args):
    last = step == STEPS - 1
    out_shape = [f32(3, ROWS, LANES)]
    scratch = [pltpu.VMEM((32, LANES), jnp.float32)] + field_scratch(1)
    if not last:
        out_shape += [f32(SUMS, LANES), f32(FACE, LANES), f32(FACE, LANES)]
        scratch += scatter_scratch()
    return pl.pallas_call(
        functools.partial(turn_kernel, step),
        out_shape=tuple(out_shape),
        in_specs=[VMEM] * len(args),
        out_specs=tuple([VMEM] * len(out_shape)),
        scratch_shapes=scratch,
        compiler_params=pltpu.CompilerParams(vmem_limit_bytes=VMEM_LIMIT),
        name="turn",
    )(*args)


def swaps(count_x, count_y):
    x_odd, x_even, y_odd, y_even = [], [], [], []
    for i in range(count_x):
        for j in range(count_y):
            here = i * count_y + j
            up = i + 1 if i % 2 == 1 else i - 1
            x_odd.append((here, up * count_y + j if 0 <= up < count_x else i * count_y + (j ^ 1)))
            x_even.append((here, (i ^ 1) * count_y + j))
            y_odd.append((here, i * count_y + ((j + 1 if j % 2 == 1 else j - 1) % count_y)))
            y_even.append((here, i * count_y + (j ^ 1)))
    return x_odd, x_even, y_odd, y_even


def edge_message(step, axes, sums, got_b, got_a):
    i = lax.axis_index("gx")
    odd = i % 2 == 1
    rows = slice(4 * PLANE, FACE)
    low = jnp.where(i > 0, jnp.where(odd, got_b[rows], got_a[rows]), 0.0)
    high = jnp.where(i < lax.axis_size("gx") - 1, jnp.where(odd, got_a[rows], got_b[rows]), 0.0)
    edge = sums[4 * EDGE:4 * EDGE + EDGES] + jnp.concatenate([jnp.zeros_like(low), low, high])
    if step > 0:
        return edge
    parts = [edge]
    for s in range(STEPS):
        own = axes[s, :, 0].astype(jnp.float32)
        row = FACE + s * CELLS_Y
        parts += [own[1:2], own[0:1], jnp.where(odd, got_a[row:row + 1], got_b[row:row + 1]), own[1:2]]
    return jnp.concatenate(parts)


def per_device(perms, velocities, bins, offsets, axes, live):
    names = ("gx", "gy")
    x_odd, x_even, y_odd, y_even = perms
    inputs = (offsets, velocities.reshape(3, ROWS, LANES), bins.reshape(3, STEPS, ROWS, LANES), axes, jnp.asarray(axis_table()))
    vel, code, axes, table, sums, a, b = scatter_call(live, *[pltpu.with_memory_space_constraint(x, pltpu.HBM) for x in inputs])
    for step in range(STEPS):
        got_b = lax.ppermute(b, names, x_even)
        got_a = lax.ppermute(a, names, x_odd)
        if step == 0:
            first_b, first_a = got_b, got_a
        words = inner_call(step, code, axes, sums)
        edge = edge_message(step, axes, sums, got_b, got_a)
        got_d = lax.ppermute(edge, names, y_even)
        got_c = lax.ppermute(edge, names, y_odd)
        if step == 0:
            first_edge, first_c, first_d = edge, got_c, got_d
        words = inner_call(step, code, axes, sums, got_b, got_a, first_b, first_a, words)
        done = turn_call(step, vel, code, axes, table, words, edge, got_c, got_d, first_edge, first_c, first_d)
        if step < STEPS - 1:
            vel, sums, a, b = done
        else:
            vel = done[0]
    return vel.reshape(velocities.shape)


def solution(mesh):
    placed = (
        P(None, "gx", "gy", None),
        P(None, None, "gx", "gy", None),
        P(),
        P(None, "gx", "gy", None),
        P("gx", "gy"),
    )
    perms = swaps(mesh.shape["gx"], mesh.shape["gy"])
    return jax.shard_map(
        functools.partial(per_device, perms), mesh=mesh, in_specs=placed, out_specs=P(None, "gx", "gy", None), check_vma=False
    )
```

time: 41.2 us -> 38.6 us (0.937)
  waiting for transfers between devices: 7.99 us -> 4.05 us
  Pallas kernels: 15.5 us -> 18.2 us
  starting transfers between devices: 16.6 us -> 15.4 us
    pallas_call x0 -> x4, Pallas kernels: none -> 7.23 us  [inner_call(): pl.pallas_call(functools.partial(inner_kernel, step), out_shape=i32(2, RO...]
    pallas_call x2, Pallas kernels: 11.1 us -> 6.49 us  [turn_call(): pl.pallas_call(functools.partial(turn_kernel, step), out_shape=tuple(out_...]
    ppermute x4, waiting for transfers between devices: 3.95 us -> 0.01 us  [the longest x2 0.01 us: per_device(): got_d = lax.ppermute(edge, names, y_even)]
    ppermute x4, starting transfers between devices: 5.2 us -> 3.96 us  [the longest x2 3.78 us: per_device(): got_c = lax.ppermute(edge, names, y_odd)]
  transfers between devices with their start and end apart: 8 -> 8, of which waited for: 4 -> 2; matrix products, arithmetic and copies ran while one was open for 0% -> 0% of each run, Pallas kernels for 0% -> 19%
where the time goes in v3:
time: 38.6 us; the launch traced here: 38.5 us
  Pallas kernels  18.2 us (47%)
  starting transfers between devices  15.4 us (40%)
  waiting for transfers between devices  4.05 us (10%)
  between operations  0.77 us (2%)
    ppermute x2, starting transfers between devices, per_device(): got_a = lax.ppermute(a, names, x_odd)  9.35 us
    pallas_call x4, Pallas kernels, inner_call(): pl.pallas_call(functools.partial(inner_kernel, step), out_shape=i32(2, RO...  7.23 us
    pallas_call x2, Pallas kernels, turn_call(): pl.pallas_call(functools.partial(turn_kernel, step), out_shape=tuple(out_...  6.49 us
    pallas_call x1, Pallas kernels, scatter_call(): pl.pallas_call(scatter_kernel, out_shape=out_shape, in_specs=[SMEM] + [HB...  4.43 us
    ppermute x2, waiting for transfers between devices, per_device(): got_a = lax.ppermute(a, names, x_odd)  4.03 us
    ppermute x2, starting transfers between devices, per_device(): got_c = lax.ppermute(edge, names, y_odd)  3.78 us
    ppermute x2, starting transfers between devices, per_device(): got_b = lax.ppermute(b, names, x_even)  2.11 us
  transfers between devices with their start and end apart: 8, of which 2 were waited for; matrix products, arithmetic and copies ran while one was open for 0% of the time, Pallas kernels for 19%

profile of v3, /device:TPU:24, one launch (start us, length us, event | category | flops | bytes accessed | tf_op | source)
XLA Modules:
  0.0 38.5 jit_solution(8570501710577320808)
XLA Ops:
  0.7 4.4 %scatter.1 = (f32[3,160,128]{2,1,0:T(8,128)S(1)}, s32[2,160,128]{2,1,0:T(8,128)S(1)}, s32[2,2,16,128]{3,2,1,0:T(8,128)S(1)}, f32[3,8,128]{2,1,0:T(8,128)S(1)}, f...) custom-call(s32[1,1]{1,0:T(1,128)S(6)} %copy.9.live_ref, s32[2,3]{1,0:T(2,128)} %offsets_hbm.1, ...), custom_call_target="tpu_custom_call" | custom-call | tf_op jit(solution)/shard_map/scatter/pallas_call | solution.py:318
  5.1 2.0 %collective-permute-start = (f32[104,128]{1,0:T(8,128)S(1)}, f32[104,128]{1,0:T(8,128)S(1)}, u32[]{:S(2)}, u32[]{:S(2)}) collective-permute-start(f32[104,128]{1,0:T(8,128)S(1)} %get-tuple-element.21), channel_id=1, source_target_pairs={{0,8},{1,9},{2,10},{3,11},{4,12},{5,13},{6,14},{7,15},{8,0},{9,1},... | collective-permute-start | bytes 159752 | tf_op jit(solution)/shard_map/ppermute | solution.py:409
  7.1 5.1 %collective-permute-start.1 = (f32[104,128]{1,0:T(8,128)S(1)}, f32[104,128]{1,0:T(8,128)S(1)}, u32[]{:S(2)}, u32[]{:S(2)}) collective-permute-start(f32[104,128]{1,0:T(8,128)S(1)} %get-tuple-element.22), channel_id=1, source_target_pairs={{0,1},{1,0},{2,3},{3,2},{4,5},{5,4},{6,7},{7,6},{8,16},{9,17},{10,... | collective-permute-start | bytes 159752 | tf_op jit(solution)/shard_map/ppermute | solution.py:410
  12.2 0.0 collective-permute-done.rest_0_.rest_2_
  12.3 2.1 %collective-permute-done.1.rest_1_.rest_3_ = f32[104,128]{1,0:T(8,128)S(1)} collective-permute-done((f32[104,128]{1,0:T(8,128)S(1)}, f32[104,128]{1,0:T(8,128)S(1)}, u32[]{:S(2)}, u32[]{:S(2)}) %collective-permute-start.1) | collective-permute-done | bytes 53280 | tf_op jit(solution)/shard_map/ppermute | solution.py:410
  14.4 0.1 collective-permute-start.3
  14.5 2.8 %collective-permute-start.2 = (f32[32,128]{1,0:T(8,128)S(1)}, f32[32,128]{1,0:T(8,128)S(1)}, u32[]{:S(2)}, u32[]{:S(2)}) collective-permute-start(f32[32,128]{1,0:T(8,128)S(1)} %concatenate.10.edge_ref.first_edge_ref), channel_id=1, source_target_pairs={{0,7},{1,2},{2,1},{3,4},{4,3},{5,6},{6,5},{7,0},{8,15},{9,10},{10,... | collective-permute-start | bytes 49160 | tf_op jit(solution)/shard_map/ppermute | solution.py:416
  17.4 1.4 %inner.4.rest_4_ = s32[2,160,128]{2,1,0:T(8,128)S(1)} custom-call(s32[2,160,128]{2,1,0:T(8,128)S(1)} %get-tuple-element.17.code_ref, s32[2,2,16,128]{3,2,1,0:T(8,128)S(1)} %get-tuple-element.18.axes_ref, f32[224,128]{1,0:T(8,128)S(1)} %get-tuple-element.20.sums_ref), custom_call_target="tpu_custom_call" | custom-call | bytes 8000000 | tf_op jit(solution)/shard_map/inner/pallas_call | solution.py:343
  18.8 2.2 %inner.5.words_ref = s32[2,160,128]{2,1,0:T(8,128)S(1)} custom-call(s32[2,160,128]{2,1,0:T(8,128)S(1)} %get-tuple-element.17.code_ref, s32[2,2,16,128]{3,2,1,0:T(8,128)S(1)} %get-tuple-element.18.axes_ref, f32[224,128]{1,0:T(8,128)S(1)} %get-tuple-element.20.sums_ref, f32[104,128]{1,0:T(8,128)S(1)} %collective-permute-done.rest_0_.rest_2_, ...), custom_call_target="tpu_custom_call" | custom-call | bytes 8000000 | tf_op jit(solution)/shard_map/inner/pallas_call | solution.py:343
  21.0 0.0 collective-permute-done.3.d_ref.first_d_ref
  21.0 0.0 collective-permute-done.2.c_ref.first_c_ref
  21.0 4.5 %turn.2 = (f32[3,160,128]{2,1,0:T(8,128)S(1)}, f32[224,128]{1,0:T(8,128)S(1)}, f32[72,128]{1,0:T(8,128)S(1)}, f32[72,128]{1,0:T(8,128)S(1)}) custom-call(f32[3,160,128]{2,1,0:T(8,128)S(1)} %get-tuple-element.16.vel_ref, s32[2,160,128]{2,1,0:T(8,128)S(1)} %get-tuple-element.17.code_ref, s32[2,2,16,128]{3,2,1,0:T(8,128)S(1)} %get-tuple-element.18.axes_ref, ...), custom_call_target="tpu_custom_call" | custom-call | tf_op jit(solution)/shard_map/turn/pallas_call | solution.py:362
  25.5 0.1 collective-permute-start.4
  25.6 4.2 %collective-permute-start.5 = (f32[72,128]{1,0:T(8,128)S(1)}, f32[72,128]{1,0:T(8,128)S(1)}, u32[]{:S(2)}, u32[]{:S(2)}) collective-permute-start(f32[72,128]{1,0:T(8,128)S(1)} %get-tuple-element.26), channel_id=1, source_target_pairs={{0,1},{1,0},{2,3},{3,2},{4,5},{5,4},{6,7},{7,6},{8,16},{9,17},{10,... | collective-permute-start | bytes 110600 | tf_op jit(solution)/shard_map/ppermute | solution.py:410
  29.9 0.0 collective-permute-done.4.rest_0_
  29.9 1.9 %collective-permute-done.5.rest_1_ = f32[72,128]{1,0:T(8,128)S(1)} collective-permute-done((f32[72,128]{1,0:T(8,128)S(1)}, f32[72,128]{1,0:T(8,128)S(1)}, u32[]{:S(2)}, u32[]{:S(2)}) %collective-permute-start.5) | collective-permute-done | bytes 36896 | tf_op jit(solution)/shard_map/ppermute | solution.py:410
  31.8 0.1 collective-permute-start.7
  31.9 0.9 %collective-permute-start.6 = (f32[24,128]{1,0:T(8,128)S(1)}, f32[24,128]{1,0:T(8,128)S(1)}, u32[]{:S(2)}, u32[]{:S(2)}) collective-permute-start(f32[24,128]{1,0:T(8,128)S(1)} %fusion.3.edge_ref), channel_id=1, source_target_pairs={{0,7},{1,2},{2,1},{3,4},{4,3},{5,6},{6,5},{7,0},{8,15},{9,10},{10,... | collective-permute-start | bytes 36872 | tf_op jit(solution)/shard_map/ppermute | solution.py:416
  32.8 1.4 %inner.6.rest_4_ = s32[2,160,128]{2,1,0:T(8,128)S(1)} custom-call(s32[2,160,128]{2,1,0:T(8,128)S(1)} %get-tuple-element.17.code_ref, s32[2,2,16,128]{3,2,1,0:T(8,128)S(1)} %get-tuple-element.18.axes_ref, f32[224,128]{1,0:T(8,128)S(1)} %get-tuple-element.24.sums_ref), custom_call_target="tpu_custom_call" | custom-call | bytes 8000000 | tf_op jit(solution)/shard_map/inner/pallas_call | solution.py:343
  34.3 2.2 %inner.7.words_ref = s32[2,160,128]{2,1,0:T(8,128)S(1)} custom-call(s32[2,160,128]{2,1,0:T(8,128)S(1)} %get-tuple-element.17.code_ref, s32[2,2,16,128]{3,2,1,0:T(8,128)S(1)} %get-tuple-element.18.axes_ref, f32[224,128]{1,0:T(8,128)S(1)} %get-tuple-element.24.sums_ref, f32[72,128]{1,0:T(8,128)S(1)} %collective-permute-done.4.rest_0_, ...), custom_call_target="tpu_custom_call" | custom-call | bytes 8000000 | tf_op jit(solution)/shard_map/inner/pallas_call | solution.py:343
  36.5 0.0 collective-permute-done.7.d_ref
  36.5 0.0 collective-permute-done.6.c_ref
  36.5 2.0 %turn.3 = f32[3,160,128]{2,1,0:T(8,128)} custom-call(f32[3,160,128]{2,1,0:T(8,128)S(1)} %get-tuple-element.23.vel_ref, s32[2,160,128]{2,1,0:T(8,128)S(1)} %get-tuple-element.17.code_ref, s32[2,2,16,128]{3,2,1,0:T(8,128)S(1)} %get-tuple-element.18.axes_ref, f32[3,8,128]{2,1,0:T(8,128)S(1)} %get-tuple-element.19.table_ref, s32[2,160,128]{2,1,0:T(8,128)S(1)} %inner.7.words_ref, ...), custom_call_target="tpu_custom_call" | custom-call | tf_op jit(solution)/shard_map/turn/pallas_call | solution.py:362
  (9 shorter events, 0.1 us)
Async XLA Ops:
  5.1 7.2 %collective-permute-start = (f32[104,128]{1,0:T(8,128)S(1)}, f32[104,128]{1,0:T(8,128)S(1)}, u32[]{:S(2)}, u32[]{:S(2)}) collective-permute-start(f32[104,128]{1,0:T(8,128)S(1)} %get-tuple-element.21), channel_id=1, source_target_pairs={{0,8},{1,9},{2,10},{3,11},{4,12},{5,13},{6,14},{7,15},{8,0},{9,1},... | collective-permute-start | bytes 159752 | tf_op jit(solution)/shard_map/ppermute | solution.py:409
  7.1 7.2 %collective-permute-start.1 = (f32[104,128]{1,0:T(8,128)S(1)}, f32[104,128]{1,0:T(8,128)S(1)}, u32[]{:S(2)}, u32[]{:S(2)}) collective-permute-start(f32[104,128]{1,0:T(8,128)S(1)} %get-tuple-element.22), channel_id=1, source_target_pairs={{0,1},{1,0},{2,3},{3,2},{4,5},{5,4},{6,7},{7,6},{8,16},{9,17},{10,... | collective-permute-start | bytes 159752 | tf_op jit(solution)/shard_map/ppermute | solution.py:410
  14.4 6.6 %collective-permute-start.3 = (f32[32,128]{1,0:T(8,128)S(1)}, f32[32,128]{1,0:T(8,128)S(1)}, u32[]{:S(2)}, u32[]{:S(2)}) collective-permute-start(f32[32,128]{1,0:T(8,128)S(1)} %concatenate.10.edge_ref.first_edge_ref), channel_id=1, source_target_pairs={{0,1},{1,0},{2,3},{3,2},{4,5},{5,4},{6,7},{7,6},{8,9},{9,8},{10,11... | collective-permute-start | bytes 49160 | tf_op jit(solution)/shard_map/ppermute | solution.py:415
  14.5 6.5 %collective-permute-start.2 = (f32[32,128]{1,0:T(8,128)S(1)}, f32[32,128]{1,0:T(8,128)S(1)}, u32[]{:S(2)}, u32[]{:S(2)}) collective-permute-start(f32[32,128]{1,0:T(8,128)S(1)} %concatenate.10.edge_ref.first_edge_ref), channel_id=1, source_target_pairs={{0,7},{1,2},{2,1},{3,4},{4,3},{5,6},{6,5},{7,0},{8,15},{9,10},{10,... | collective-permute-start | bytes 49160 | tf_op jit(solution)/shard_map/ppermute | solution.py:416
  25.5 4.3 %collective-permute-start.4 = (f32[72,128]{1,0:T(8,128)S(1)}, f32[72,128]{1,0:T(8,128)S(1)}, u32[]{:S(2)}, u32[]{:S(2)}) collective-permute-start(f32[72,128]{1,0:T(8,128)S(1)} %get-tuple-element.25), channel_id=1, source_target_pairs={{0,8},{1,9},{2,10},{3,11},{4,12},{5,13},{6,14},{7,15},{8,0},{9,1},... | collective-permute-start | bytes 110600 | tf_op jit(solution)/shard_map/ppermute | solution.py:409
  25.6 6.2 %collective-permute-start.5 = (f32[72,128]{1,0:T(8,128)S(1)}, f32[72,128]{1,0:T(8,128)S(1)}, u32[]{:S(2)}, u32[]{:S(2)}) collective-permute-start(f32[72,128]{1,0:T(8,128)S(1)} %get-tuple-element.26), channel_id=1, source_target_pairs={{0,1},{1,0},{2,3},{3,2},{4,5},{5,4},{6,7},{7,6},{8,16},{9,17},{10,... | collective-permute-start | bytes 110600 | tf_op jit(solution)/shard_map/ppermute | solution.py:410
  31.8 4.7 %collective-permute-start.7 = (f32[24,128]{1,0:T(8,128)S(1)}, f32[24,128]{1,0:T(8,128)S(1)}, u32[]{:S(2)}, u32[]{:S(2)}) collective-permute-start(f32[24,128]{1,0:T(8,128)S(1)} %fusion.3.edge_ref), channel_id=1, source_target_pairs={{0,1},{1,0},{2,3},{3,2},{4,5},{5,4},{6,7},{7,6},{8,9},{9,8},{10,11... | collective-permute-start | bytes 36872 | tf_op jit(solution)/shard_map/ppermute | solution.py:415
  31.9 4.6 %collective-permute-start.6 = (f32[24,128]{1,0:T(8,128)S(1)}, f32[24,128]{1,0:T(8,128)S(1)}, u32[]{:S(2)}, u32[]{:S(2)}) collective-permute-start(f32[24,128]{1,0:T(8,128)S(1)} %fusion.3.edge_ref), channel_id=1, source_target_pairs={{0,7},{1,2},{2,1},{3,4},{4,3},{5,6},{6,5},{7,0},{8,15},{9,10},{10,... | collective-permute-start | bytes 36872 | tf_op jit(solution)/shard_map/ppermute | solution.py:416

commit v4 on v3

--- a/solution.py
+++ b/solution.py
@@ -91,11 +91,11 @@
     return jnp.concatenate([jnp.where(pair == ids[t], data, zero) for t in range(WIDE // 16)], axis=0)
 
 
-def scatter_rows(acc_ref, vel_ref, key_ref, pair_ref, base, count):
-    rows = [pl.ds(base + r, 1) for r in range(count)]
+def scatter_rows(acc_ref, vel_ref, key_ref, pair_ref):
+    rows = [slice(r, r + 1) for r in range(ROWS)]
     spread = jnp.concatenate([spread_row(vel_ref, pair_ref, row) for row in rows], axis=1)
     hot = jnp.concatenate([hot_row(key_ref, row) for row in rows], axis=1)
-    acc_ref[...] += lax.dot_general(spread, hot, (((1,), (1,)), ((), ())), preferred_element_type=jnp.float32)
+    acc_ref[...] = lax.dot_general(hot, spread, (((1,), (1,)), ((), ())), preferred_element_type=jnp.float32).T
 
 
 def finish_sums(acc_ref, sums_ref):
@@ -132,7 +132,6 @@
     ]
     for copy in copies:
         copy.start()
-    acc_ref[...] = jnp.zeros_like(acc_ref)
     at_wall = lax.axis_index("gx") == lax.axis_size("gx") - 1
     for copy in copies[:2]:
         copy.wait()
@@ -140,18 +139,16 @@
     code = cell_code(bins_ref.at[0], 0, offsets_ref, live, at_wall)
     code_ref[0] = code
     fill_keys(code, key_ref, pair_ref)
-    copies[2].wait()
-
-    scatter_rows(acc_ref, vel_ref, key_ref, pair_ref, 0, ROWS)
-    finish_sums(acc_ref, sums_ref)
-    write_faces(sums_ref, a_ref, b_ref)
-    for copy in copies[3:]:
+    for copy in copies[2:]:
         copy.wait()
     code_ref[1] = cell_code(bins_ref.at[1], 1, offsets_ref, live, at_wall)
     for step in range(STEPS):
         own = axes_ref[step, 0].astype(jnp.float32)
         a_ref[FACE + step * CELLS_Y:FACE + (step + 1) * CELLS_Y, :] = own
         b_ref[FACE + step * CELLS_Y:FACE + (step + 1) * CELLS_Y, :] = own
+    scatter_rows(acc_ref, vel_ref, key_ref, pair_ref)
+    finish_sums(acc_ref, sums_ref)
+    write_faces(sums_ref, a_ref, b_ref)
 
 
 def pack_fields(total_ref, index_ref, first_ref, second_ref, start, groups):
@@ -248,7 +245,6 @@
         next_ref, na_ref, nb_ref = rest[1:4]
         key_ref, pair_ref, acc_ref = rest[-3:]
         fill_keys(code_ref[step + 1], key_ref, pair_ref)
-        acc_ref[...] = jnp.zeros_like(acc_ref)
     odd = lax.axis_index("gy") % 2 == 1
     sub = row_ids((8, LANES))
     total_ref[...] = jnp.zeros_like(total_ref)
@@ -266,10 +262,10 @@
     pack_fields(total_ref, index_ref, first_ref, second_ref, 0, 1)
 
     def body(turn, carry):
-        base = pl.multiple_of(turn * BLOCK, BLOCK)
+        base = turn * BLOCK
         gather_rows(code_ref.at[step], first_ref, second_ref, got_ref, base, BLOCK, GROUPS - 1, 1)
         for b in range(BLOCK // 8):
-            rows = pl.ds(pl.multiple_of(base + 8 * b, 8), 8)
+            rows = pl.ds(base + 8 * b, 8)
             code = code_ref[step, rows, :]
             words = [jnp.where(code < EDGE * DEPTH, words_ref[w, rows, :], word) for w, word in enumerate(choose_rows(code, got_ref, b))]
             mean, index = unpack_fields(*words)
@@ -284,9 +280,10 @@
                 out_ref[c, rows, :] = jnp.where(code < DEAD, turned, vel[c])
         return carry
 
-    lax.fori_loop(0, ROWS // BLOCK, body, 0)
+    for turn in range(ROWS // BLOCK):
+        body(turn, 0)
     if not last:
-        scatter_rows(acc_ref, out_ref, key_ref, pair_ref, 0, ROWS)
+        scatter_rows(acc_ref, out_ref, key_ref, pair_ref)
         finish_sums(acc_ref, next_ref)
         write_faces(next_ref, na_ref, nb_ref)
 
@@ -411,6 +408,7 @@
         if step == 0:
             first_b, first_a = got_b, got_a
         words = inner_call(step, code, axes, sums)
+        got_b, got_a, words = lax.optimization_barrier((got_b, got_a, words))
         edge = edge_message(step, axes, sums, got_b, got_a)
         got_d = lax.ppermute(edge, names, y_even)
         got_c = lax.ppermute(edge, names, y_odd)

time: 38.6 us -> 35.5 us (0.920)
  waiting for transfers between devices: 4.05 us -> 1.86 us
  Pallas kernels: 18.2 us -> 16.7 us
  starting transfers between devices: 15.4 us -> 16 us
    ppermute x2, waiting for transfers between devices: 4.03 us -> 1.13 us  [per_device(): got_a = lax.ppermute(a, names, x_odd)]
    pallas_call x2, Pallas kernels: 6.49 us -> 5.19 us  [turn_call(): pl.pallas_call(functools.partial(turn_kernel, step), out_shape=tuple(out_...]
    ppermute x2, waiting for transfers between devices: 0.01 us -> 0.71 us  [per_device(): got_c = lax.ppermute(edge, names, y_odd)]
    ppermute x2, starting transfers between devices: 3.78 us -> 4.36 us  [per_device(): got_c = lax.ppermute(edge, names, y_odd)]
  transfers between devices with their start and end apart: 8 -> 8, of which waited for: 2 -> 3; matrix products, arithmetic and copies ran while one was open for 0% -> 0% of each run, Pallas kernels for 19% -> 20%
where the time goes in v4:
time: 35.5 us; the launch traced here: 35.4 us
  Pallas kernels  16.7 us (47%)
  starting transfers between devices  16 us (45%)
  waiting for transfers between devices  1.86 us (5%)
  between operations  0.79 us (2%)
    ppermute x2, starting transfers between devices, per_device(): got_a = lax.ppermute(a, names, x_odd)  9.36 us
    pallas_call x4, Pallas kernels, inner_call(): pl.pallas_call(functools.partial(inner_kernel, step), out_shape=i32(2, RO...  7.21 us
    pallas_call x2, Pallas kernels, turn_call(): pl.pallas_call(functools.partial(turn_kernel, step), out_shape=tuple(out_...  5.19 us
    ppermute x2, starting transfers between devices, per_device(): got_c = lax.ppermute(edge, names, y_odd)  4.36 us
    pallas_call x1, Pallas kernels, scatter_call(): pl.pallas_call(scatter_kernel, out_shape=out_shape, in_specs=[SMEM] + [HB...  4.31 us
    ppermute x2, starting transfers between devices, per_device(): got_b = lax.ppermute(b, names, x_even)  2.09 us
    ppermute x2, waiting for transfers between devices, per_device(): got_a = lax.ppermute(a, names, x_odd)  1.13 us
    ppermute x2, waiting for transfers between devices, per_device(): got_c = lax.ppermute(edge, names, y_odd)  0.71 us
  transfers between devices with their start and end apart: 8, of which 3 were waited for; matrix products, arithmetic and copies ran while one was open for 0% of the time, Pallas kernels for 20%

profile of v4, /device:TPU:24, one launch (start us, length us, event | category | flops | bytes accessed | tf_op | source)
XLA Modules:
  0.0 35.4 jit_solution(12252544005050287405)
XLA Ops:
  0.7 4.3 %scatter.1 = (f32[3,160,128]{2,1,0:T(8,128)S(1)}, s32[2,160,128]{2,1,0:T(8,128)S(1)}, s32[2,2,16,128]{3,2,1,0:T(8,128)S(1)}, f32[3,8,128]{2,1,0:T(8,128)S(1)}, f...) custom-call(s32[1,1]{1,0:T(1,128)S(6)} %copy.9.live_ref, s32[2,3]{1,0:T(2,128)} %offsets_hbm.1, ...), custom_call_target="tpu_custom_call" | custom-call | tf_op jit(solution)/shard_map/scatter/pallas_call | solution.py:315
  5.0 2.0 %collective-permute-start = (f32[104,128]{1,0:T(8,128)S(1)}, f32[104,128]{1,0:T(8,128)S(1)}, u32[]{:S(2)}, u32[]{:S(2)}) collective-permute-start(f32[104,128]{1,0:T(8,128)S(1)} %get-tuple-element.27), channel_id=1, source_target_pairs={{0,8},{1,9},{2,10},{3,11},{4,12},{5,13},{6,14},{7,15},{8,0},{9,1},... | collective-permute-start | bytes 159752 | tf_op jit(solution)/shard_map/ppermute | solution.py:406
  7.0 5.1 %collective-permute-start.1 = (f32[104,128]{1,0:T(8,128)S(1)}, f32[104,128]{1,0:T(8,128)S(1)}, u32[]{:S(2)}, u32[]{:S(2)}) collective-permute-start(f32[104,128]{1,0:T(8,128)S(1)} %get-tuple-element.28), channel_id=1, source_target_pairs={{0,1},{1,0},{2,3},{3,2},{4,5},{5,4},{6,7},{7,6},{8,16},{9,17},{10,... | collective-permute-start | bytes 159752 | tf_op jit(solution)/shard_map/ppermute | solution.py:407
  12.1 1.4 %inner.4.rest_4_ = s32[2,160,128]{2,1,0:T(8,128)S(1)} custom-call(s32[2,160,128]{2,1,0:T(8,128)S(1)} %get-tuple-element.23.code_ref, s32[2,2,16,128]{3,2,1,0:T(8,128)S(1)} %get-tuple-element.24.axes_ref, f32[224,128]{1,0:T(8,128)S(1)} %get-tuple-element.26.sums_ref), custom_call_target="tpu_custom_call" | custom-call | bytes 8000000 | tf_op jit(solution)/shard_map/inner/pallas_call | solution.py:340
  13.6 0.0 collective-permute-done.rest_0_.rest_2_
  13.6 0.6 %collective-permute-done.1.rest_1_.rest_3_ = f32[104,128]{1,0:T(8,128)S(1)} collective-permute-done((f32[104,128]{1,0:T(8,128)S(1)}, f32[104,128]{1,0:T(8,128)S(1)}, u32[]{:S(2)}, u32[]{:S(2)}) %collective-permute-start.1) | collective-permute-done | bytes 53280 | tf_op jit(solution)/shard_map/ppermute | solution.py:407
  14.3 0.1 collective-permute-start.3
  14.4 2.8 %collective-permute-start.2 = (f32[32,128]{1,0:T(8,128)S(1)}, f32[32,128]{1,0:T(8,128)S(1)}, u32[]{:S(2)}, u32[]{:S(2)}) collective-permute-start(f32[32,128]{1,0:T(8,128)S(1)} %concatenate.10.edge_ref.first_edge_ref), channel_id=1, source_target_pairs={{0,7},{1,2},{2,1},{3,4},{4,3},{5,6},{6,5},{7,0},{8,15},{9,10},{10,... | collective-permute-start | bytes 49160 | tf_op jit(solution)/shard_map/ppermute | solution.py:414
  17.2 2.2 %inner.5.words_ref = s32[2,160,128]{2,1,0:T(8,128)S(1)} custom-call(s32[2,160,128]{2,1,0:T(8,128)S(1)} %get-tuple-element.23.code_ref, s32[2,2,16,128]{3,2,1,0:T(8,128)S(1)} %get-tuple-element.24.axes_ref, f32[224,128]{1,0:T(8,128)S(1)} %get-tuple-element.26.sums_ref, f32[104,128]{1,0:T(8,128)S(1)} %collective-permute-done.rest_0_.rest_2_, ...), custom_call_target="tpu_custom_call" | custom-call | bytes 8000000 | tf_op jit(solution)/shard_map/inner/pallas_call | solution.py:340
  19.4 0.0 collective-permute-done.3.d_ref.first_d_ref
  19.4 0.0 collective-permute-done.2.c_ref.first_c_ref
  19.4 3.3 %turn.2 = (f32[3,160,128]{2,1,0:T(8,128)S(1)}, f32[224,128]{1,0:T(8,128)S(1)}, f32[72,128]{1,0:T(8,128)S(1)}, f32[72,128]{1,0:T(8,128)S(1)}) custom-call(f32[3,160,128]{2,1,0:T(8,128)S(1)} %get-tuple-element.22.vel_ref, s32[2,160,128]{2,1,0:T(8,128)S(1)} %get-tuple-element.23.code_ref, s32[2,2,16,128]{3,2,1,0:T(8,128)S(1)} %get-tuple-element.24.axes_ref, ...), custom_call_target="tpu_custom_call" | custom-call | tf_op jit(solution)/shard_map/turn/pallas_call | solution.py:359
  22.8 0.1 collective-permute-start.4
  22.9 4.2 %collective-permute-start.5 = (f32[72,128]{1,0:T(8,128)S(1)}, f32[72,128]{1,0:T(8,128)S(1)}, u32[]{:S(2)}, u32[]{:S(2)}) collective-permute-start(f32[72,128]{1,0:T(8,128)S(1)} %get-tuple-element.35), channel_id=1, source_target_pairs={{0,1},{1,0},{2,3},{3,2},{4,5},{5,4},{6,7},{7,6},{8,16},{9,17},{10,... | collective-permute-start | bytes 110600 | tf_op jit(solution)/shard_map/ppermute | solution.py:407
  27.1 1.4 %inner.6.rest_4_ = s32[2,160,128]{2,1,0:T(8,128)S(1)} custom-call(s32[2,160,128]{2,1,0:T(8,128)S(1)} %get-tuple-element.23.code_ref, s32[2,2,16,128]{3,2,1,0:T(8,128)S(1)} %get-tuple-element.24.axes_ref, f32[224,128]{1,0:T(8,128)S(1)} %get-tuple-element.33.sums_ref), custom_call_target="tpu_custom_call" | custom-call | bytes 8000000 | tf_op jit(solution)/shard_map/inner/pallas_call | solution.py:340
  28.5 0.0 collective-permute-done.4.rest_0_
  28.5 0.5 %collective-permute-done.5.rest_1_ = f32[72,128]{1,0:T(8,128)S(1)} collective-permute-done((f32[72,128]{1,0:T(8,128)S(1)}, f32[72,128]{1,0:T(8,128)S(1)}, u32[]{:S(2)}, u32[]{:S(2)}) %collective-permute-start.5) | collective-permute-done | bytes 36896 | tf_op jit(solution)/shard_map/ppermute | solution.py:407
  29.0 0.1 collective-permute-start.7
  29.1 1.5 %collective-permute-start.6 = (f32[24,128]{1,0:T(8,128)S(1)}, f32[24,128]{1,0:T(8,128)S(1)}, u32[]{:S(2)}, u32[]{:S(2)}) collective-permute-start(f32[24,128]{1,0:T(8,128)S(1)} %fusion.3.edge_ref), channel_id=1, source_target_pairs={{0,7},{1,2},{2,1},{3,4},{4,3},{5,6},{6,5},{7,0},{8,15},{9,10},{10,... | collective-permute-start | bytes 36872 | tf_op jit(solution)/shard_map/ppermute | solution.py:414
  30.7 2.2 %inner.7.words_ref = s32[2,160,128]{2,1,0:T(8,128)S(1)} custom-call(s32[2,160,128]{2,1,0:T(8,128)S(1)} %get-tuple-element.23.code_ref, s32[2,2,16,128]{3,2,1,0:T(8,128)S(1)} %get-tuple-element.24.axes_ref, f32[224,128]{1,0:T(8,128)S(1)} %get-tuple-element.33.sums_ref, f32[72,128]{1,0:T(8,128)S(1)} %collective-permute-done.4.rest_0_, ...), custom_call_target="tpu_custom_call" | custom-call | bytes 8000000 | tf_op jit(solution)/shard_map/inner/pallas_call | solution.py:340
  32.8 0.0 collective-permute-done.7.d_ref
  32.8 0.7 %collective-permute-done.6.c_ref = f32[24,128]{1,0:T(8,128)S(1)} collective-permute-done((f32[24,128]{1,0:T(8,128)S(1)}, f32[24,128]{1,0:T(8,128)S(1)}, u32[]{:S(2)}, u32[]{:S(2)}) %collective-permute-start.6) | collective-permute-done | bytes 12320 | tf_op jit(solution)/shard_map/ppermute | solution.py:414
  33.6 1.9 %turn.3 = f32[3,160,128]{2,1,0:T(8,128)} custom-call(f32[3,160,128]{2,1,0:T(8,128)S(1)} %get-tuple-element.32.vel_ref, s32[2,160,128]{2,1,0:T(8,128)S(1)} %get-tuple-element.23.code_ref, s32[2,2,16,128]{3,2,1,0:T(8,128)S(1)} %get-tuple-element.24.axes_ref, f32[3,8,128]{2,1,0:T(8,128)S(1)} %get-tuple-element.25.table_ref, s32[2,160,128]{2,1,0:T(8,128)S(1)} %inner.7.words_ref, ...), custom_call_target="tpu_custom_call" | custom-call | tf_op jit(solution)/shard_map/turn/pallas_call | solution.py:359
  (9 shorter events, 0.1 us)
Async XLA Ops:
  5.0 8.6 %collective-permute-start = (f32[104,128]{1,0:T(8,128)S(1)}, f32[104,128]{1,0:T(8,128)S(1)}, u32[]{:S(2)}, u32[]{:S(2)}) collective-permute-start(f32[104,128]{1,0:T(8,128)S(1)} %get-tuple-element.27), channel_id=1, source_target_pairs={{0,8},{1,9},{2,10},{3,11},{4,12},{5,13},{6,14},{7,15},{8,0},{9,1},... | collective-permute-start | bytes 159752 | tf_op jit(solution)/shard_map/ppermute | solution.py:406
  7.0 7.2 %collective-permute-start.1 = (f32[104,128]{1,0:T(8,128)S(1)}, f32[104,128]{1,0:T(8,128)S(1)}, u32[]{:S(2)}, u32[]{:S(2)}) collective-permute-start(f32[104,128]{1,0:T(8,128)S(1)} %get-tuple-element.28), channel_id=1, source_target_pairs={{0,1},{1,0},{2,3},{3,2},{4,5},{5,4},{6,7},{7,6},{8,16},{9,17},{10,... | collective-permute-start | bytes 159752 | tf_op jit(solution)/shard_map/ppermute | solution.py:407
  14.3 5.1 %collective-permute-start.3 = (f32[32,128]{1,0:T(8,128)S(1)}, f32[32,128]{1,0:T(8,128)S(1)}, u32[]{:S(2)}, u32[]{:S(2)}) collective-permute-start(f32[32,128]{1,0:T(8,128)S(1)} %concatenate.10.edge_ref.first_edge_ref), channel_id=1, source_target_pairs={{0,1},{1,0},{2,3},{3,2},{4,5},{5,4},{6,7},{7,6},{8,9},{9,8},{10,11... | collective-permute-start | bytes 49160 | tf_op jit(solution)/shard_map/ppermute | solution.py:413
  14.4 5.0 %collective-permute-start.2 = (f32[32,128]{1,0:T(8,128)S(1)}, f32[32,128]{1,0:T(8,128)S(1)}, u32[]{:S(2)}, u32[]{:S(2)}) collective-permute-start(f32[32,128]{1,0:T(8,128)S(1)} %concatenate.10.edge_ref.first_edge_ref), channel_id=1, source_target_pairs={{0,7},{1,2},{2,1},{3,4},{4,3},{5,6},{6,5},{7,0},{8,15},{9,10},{10,... | collective-permute-start | bytes 49160 | tf_op jit(solution)/shard_map/ppermute | solution.py:414
  22.8 5.8 %collective-permute-start.4 = (f32[72,128]{1,0:T(8,128)S(1)}, f32[72,128]{1,0:T(8,128)S(1)}, u32[]{:S(2)}, u32[]{:S(2)}) collective-permute-start(f32[72,128]{1,0:T(8,128)S(1)} %get-tuple-element.34), channel_id=1, source_target_pairs={{0,8},{1,9},{2,10},{3,11},{4,12},{5,13},{6,14},{7,15},{8,0},{9,1},... | collective-permute-start | bytes 110600 | tf_op jit(solution)/shard_map/ppermute | solution.py:406
  22.9 6.2 %collective-permute-start.5 = (f32[72,128]{1,0:T(8,128)S(1)}, f32[72,128]{1,0:T(8,128)S(1)}, u32[]{:S(2)}, u32[]{:S(2)}) collective-permute-start(f32[72,128]{1,0:T(8,128)S(1)} %get-tuple-element.35), channel_id=1, source_target_pairs={{0,1},{1,0},{2,3},{3,2},{4,5},{5,4},{6,7},{7,6},{8,16},{9,17},{10,... | collective-permute-start | bytes 110600 | tf_op jit(solution)/shard_map/ppermute | solution.py:407
  29.0 3.8 %collective-permute-start.7 = (f32[24,128]{1,0:T(8,128)S(1)}, f32[24,128]{1,0:T(8,128)S(1)}, u32[]{:S(2)}, u32[]{:S(2)}) collective-permute-start(f32[24,128]{1,0:T(8,128)S(1)} %fusion.3.edge_ref), channel_id=1, source_target_pairs={{0,1},{1,0},{2,3},{3,2},{4,5},{5,4},{6,7},{7,6},{8,9},{9,8},{10,11... | collective-permute-start | bytes 36872 | tf_op jit(solution)/shard_map/ppermute | solution.py:413
  29.1 4.4 %collective-permute-start.6 = (f32[24,128]{1,0:T(8,128)S(1)}, f32[24,128]{1,0:T(8,128)S(1)}, u32[]{:S(2)}, u32[]{:S(2)}) collective-permute-start(f32[24,128]{1,0:T(8,128)S(1)} %fusion.3.edge_ref), channel_id=1, source_target_pairs={{0,7},{1,2},{2,1},{3,4},{4,3},{5,6},{6,5},{7,0},{8,15},{9,10},{10,... | collective-permute-start | bytes 36872 | tf_op jit(solution)/shard_map/ppermute | solution.py:414

commit v5 on v4

--- a/solution.py
+++ b/solution.py
@@ -25,7 +25,7 @@
 EDGES = 24
 WIDE = 8 * 28
 AXROWS = STEPS * CELLS_Y
-BLOCK = 80
+FIRST = 112
 LOWEST = 121
 DEAD = 64 * DEPTH
 VMEM_LIMIT = 40 * 1024 * 1024
@@ -91,11 +91,25 @@
     return jnp.concatenate([jnp.where(pair == ids[t], data, zero) for t in range(WIDE // 16)], axis=0)
 
 
-def scatter_rows(acc_ref, vel_ref, key_ref, pair_ref):
-    rows = [slice(r, r + 1) for r in range(ROWS)]
+def scatter_rows(acc_ref, vel_ref, key_ref, pair_ref, count):
+    rows = [slice(r, r + 1) for r in range(count)]
     spread = jnp.concatenate([spread_row(vel_ref, pair_ref, row) for row in rows], axis=1)
     hot = jnp.concatenate([hot_row(key_ref, row) for row in rows], axis=1)
     acc_ref[...] = lax.dot_general(hot, spread, (((1,), (1,)), ((), ())), preferred_element_type=jnp.float32).T
+
+
+def each_part(live_ref, body, otherwise=None):
+    more = live_ref[0, 0] > FIRST * LANES
+
+    @pl.when(more)
+    def _():
+        body(ROWS)
+
+    @pl.when(jnp.logical_not(more))
+    def _():
+        body(FIRST)
+        if otherwise is not None:
+            otherwise()
 
 
 def finish_sums(acc_ref, sums_ref):
@@ -146,7 +160,7 @@
         own = axes_ref[step, 0].astype(jnp.float32)
         a_ref[FACE + step * CELLS_Y:FACE + (step + 1) * CELLS_Y, :] = own
         b_ref[FACE + step * CELLS_Y:FACE + (step + 1) * CELLS_Y, :] = own
-    scatter_rows(acc_ref, vel_ref, key_ref, pair_ref)
+    each_part(live_ref, functools.partial(scatter_rows, acc_ref, vel_ref, key_ref, pair_ref))
     finish_sums(acc_ref, sums_ref)
     write_faces(sums_ref, a_ref, b_ref)
 
@@ -176,9 +190,9 @@
     return jnp.take_along_axis(table, index, axis=1, mode="promise_in_bounds")
 
 
-def gather_rows(code_ref, first_ref, second_ref, got_ref, base, count, start, groups):
+def gather_rows(code_ref, first_ref, second_ref, got_ref, count, start, groups):
     for r in range(count):
-        code = jnp.broadcast_to(code_ref[pl.ds(base + r, 1), :], (8, LANES))
+        code = jnp.broadcast_to(code_ref[r:r + 1, :], (8, LANES))
         z = code & (DEPTH - 1)
         group = code >> 10
         got = None
@@ -202,7 +216,7 @@
     return words
 
 
-def inner_kernel(step, code_ref, axes_ref, sums_ref, *rest):
+def inner_kernel(step, live_ref, code_ref, axes_ref, sums_ref, *rest):
     middle = len(rest) == 6
     if middle:
         start, groups = 0, 2
@@ -225,20 +239,18 @@
         index_ref[PLANE:PLANE + CELLS_Y - 1, :] = jnp.where(odd, first_a_ref[rows, :], first_b_ref[rows, :]).astype(jnp.int32)
     pack_fields(total_ref, index_ref, first_ref, second_ref, 0, groups)
 
-    def body(turn, carry):
-        base = pl.multiple_of(turn * BLOCK, BLOCK)
-        gather_rows(code_ref.at[step], first_ref, second_ref, got_ref, base, BLOCK, start, groups)
-        for b in range(BLOCK // 8):
-            rows = pl.ds(pl.multiple_of(base + 8 * b, 8), 8)
+    def part(count):
+        gather_rows(code_ref.at[step], first_ref, second_ref, got_ref, count, start, groups)
+        for b in range(count // 8):
+            rows = slice(8 * b, 8 * b + 8)
             code = code_ref[step, rows, :]
             for w, word in enumerate(choose_rows(code, got_ref, b)):
                 out_ref[w, rows, :] = word if middle else jnp.where(code < start * 8 * DEPTH, before_ref[w, rows, :], word)
-        return carry
-
-    lax.fori_loop(0, ROWS // BLOCK, body, 0)
-
-
-def turn_kernel(step, vel_ref, code_ref, axes_ref, table_ref, words_ref, edge_ref, c_ref, d_ref, first_edge_ref, first_c_ref, first_d_ref, *rest):
+
+    each_part(live_ref, part)
+
+
+def turn_kernel(step, live_ref, vel_ref, code_ref, axes_ref, table_ref, words_ref, edge_ref, c_ref, d_ref, first_edge_ref, first_c_ref, first_d_ref, *rest):
     last = step == STEPS - 1
     out_ref, total_ref, index_ref, first_ref, second_ref, got_ref = rest[:1] + rest[-8 + 3 * last:][:5]
     if not last:
@@ -261,11 +273,10 @@
         index_ref[2 * plane + 1:2 * plane + 2, :] = index_high[plane:plane + 1, :]
     pack_fields(total_ref, index_ref, first_ref, second_ref, 0, 1)
 
-    def body(turn, carry):
-        base = turn * BLOCK
-        gather_rows(code_ref.at[step], first_ref, second_ref, got_ref, base, BLOCK, GROUPS - 1, 1)
-        for b in range(BLOCK // 8):
-            rows = pl.ds(base + 8 * b, 8)
+    def part(count):
+        gather_rows(code_ref.at[step], first_ref, second_ref, got_ref, count, GROUPS - 1, 1)
+        for b in range(count // 8):
+            rows = slice(8 * b, 8 * b + 8)
             code = code_ref[step, rows, :]
             words = [jnp.where(code < EDGE * DEPTH, words_ref[w, rows, :], word) for w, word in enumerate(choose_rows(code, got_ref, b))]
             mean, index = unpack_fields(*words)
@@ -278,12 +289,14 @@
                 cross = axis[d] * rel[e] - axis[e] * rel[d]
                 turned = mean[c] + turn_cos * rel[c] + turn_sin * cross + along * axis[c]
                 out_ref[c, rows, :] = jnp.where(code < DEAD, turned, vel[c])
-        return carry
-
-    for turn in range(ROWS // BLOCK):
-        body(turn, 0)
+        if not last:
+            scatter_rows(acc_ref, out_ref, key_ref, pair_ref, count)
+
+    def keep():
+        out_ref[:, FIRST:, :] = vel_ref[:, FIRST:, :]
+
+    each_part(live_ref, part, keep)
     if not last:
-        scatter_rows(acc_ref, out_ref, key_ref, pair_ref)
         finish_sums(acc_ref, next_ref)
         write_faces(next_ref, na_ref, nb_ref)
 
@@ -331,16 +344,16 @@
         pltpu.VMEM((8 * groups, LANES), jnp.int32),
         pltpu.VMEM((8 * groups, LANES), jnp.int32),
         pltpu.VMEM((8 * groups, LANES), jnp.int32),
-        pltpu.VMEM((2, 8 * BLOCK, LANES), jnp.int32),
+        pltpu.VMEM((2, 8 * ROWS, LANES), jnp.int32),
     ]
 
 
 def inner_call(step, *args):
-    groups = 2 if len(args) == 3 else 4
+    groups = 2 if len(args) == 4 else 4
     return pl.pallas_call(
         functools.partial(inner_kernel, step),
         out_shape=i32(2, ROWS, LANES),
-        in_specs=[VMEM] * len(args),
+        in_specs=[SMEM] + [VMEM] * (len(args) - 1),
         out_specs=VMEM,
         scratch_shapes=field_scratch(groups) + [pltpu.VMEM((32 * groups, LANES), jnp.float32)],
         compiler_params=pltpu.CompilerParams(vmem_limit_bytes=VMEM_LIMIT),
@@ -359,7 +372,7 @@
     return pl.pallas_call(
         functools.partial(turn_kernel, step),
         out_shape=tuple(out_shape),
-        in_specs=[VMEM] * len(args),
+        in_specs=[SMEM] + [VMEM] * (len(args) - 1),
         out_specs=tuple([VMEM] * len(out_shape)),
         scratch_shapes=scratch,
         compiler_params=pltpu.CompilerParams(vmem_limit_bytes=VMEM_LIMIT),
@@ -407,15 +420,15 @@
         got_a = lax.ppermute(a, names, x_odd)
         if step == 0:
             first_b, first_a = got_b, got_a
-        words = inner_call(step, code, axes, sums)
+        words = inner_call(step, live, code, axes, sums)
         got_b, got_a, words = lax.optimization_barrier((got_b, got_a, words))
         edge = edge_message(step, axes, sums, got_b, got_a)
         got_d = lax.ppermute(edge, names, y_even)
         got_c = lax.ppermute(edge, names, y_odd)
         if step == 0:
             first_edge, first_c, first_d = edge, got_c, got_d
-        words = inner_call(step, code, axes, sums, got_b, got_a, first_b, first_a, words)
-        done = turn_call(step, vel, code, axes, table, words, edge, got_c, got_d, first_edge, first_c, first_d)
+        words = inner_call(step, live, code, axes, sums, got_b, got_a, first_b, first_a, words)
+        done = turn_call(step, live, vel, code, axes, table, words, edge, got_c, got_d, first_edge, first_c, first_d)
         if step < STEPS - 1:
             vel, sums, a, b = done
         else:

time: 35.5 us -> 33.9 us (0.955)
  Pallas kernels: 16.7 us -> 12.7 us
  waiting for transfers between devices: 1.86 us -> 4.53 us
    pallas_call x4, Pallas kernels: 7.21 us -> 4.97 us  [inner_call(): pl.pallas_call(functools.partial(inner_kernel, step), out_shape=i32(2, RO...]
    ppermute x2, starting transfers between devices: 2.09 us -> 3.74 us  [per_device(): got_b = lax.ppermute(b, names, x_even)]
    ppermute x2, starting transfers between devices: 9.36 us -> 7.7 us  [per_device(): got_a = lax.ppermute(a, names, x_odd)]
    ppermute x2, waiting for transfers between devices: 1.13 us -> 2.78 us  [per_device(): got_a = lax.ppermute(a, names, x_odd)]
    ppermute x2, waiting for transfers between devices: 0.71 us -> 1.74 us  [per_device(): got_c = lax.ppermute(edge, names, y_odd)]
    pallas_call x2, Pallas kernels: 5.19 us -> 4.24 us  [turn_call(): pl.pallas_call(functools.partial(turn_kernel, step), out_shape=tuple(out_...]
    pallas_call x1, Pallas kernels: 4.31 us -> 3.52 us  [scatter_call(): pl.pallas_call(scatter_kernel, out_shape=out_shape, in_specs=[SMEM] + [HB...]
  transfers between devices with their start and end apart: 8 -> 8, of which waited for: 3 -> 4; matrix products, arithmetic and copies ran while one was open for 0% -> 0% of each run, Pallas kernels for 20% -> 15%
where the time goes in v5:
time: 33.9 us; the launch traced here: 33.8 us
  starting transfers between devices  15.7 us (46%)
  Pallas kernels  12.7 us (37%)
  waiting for transfers between devices  4.53 us (13%)
  between operations  0.78 us (2%)
    ppermute x2, starting transfers between devices, per_device(): got_a = lax.ppermute(a, names, x_odd)  7.7 us
    pallas_call x4, Pallas kernels, inner_call(): pl.pallas_call(functools.partial(inner_kernel, step), out_shape=i32(2, RO...  4.97 us
    pallas_call x2, Pallas kernels, turn_call(): pl.pallas_call(functools.partial(turn_kernel, step), out_shape=tuple(out_...  4.24 us
    ppermute x2, starting transfers between devices, per_device(): got_c = lax.ppermute(edge, names, y_odd)  4.11 us
    ppermute x2, starting transfers between devices, per_device(): got_b = lax.ppermute(b, names, x_even)  3.74 us
    pallas_call x1, Pallas kernels, scatter_call(): pl.pallas_call(scatter_kernel, out_shape=out_shape, in_specs=[SMEM] + [HB...  3.52 us
    ppermute x2, waiting for transfers between devices, per_device(): got_a = lax.ppermute(a, names, x_odd)  2.78 us
    ppermute x2, waiting for transfers between devices, per_device(): got_c = lax.ppermute(edge, names, y_odd)  1.74 us
  transfers between devices with their start and end apart: 8, of which 4 were waited for; matrix products, arithmetic and copies ran while one was open for 0% of the time, Pallas kernels for 15%

profile of v5, /device:TPU:24, one launch (start us, length us, event | category | flops | bytes accessed | tf_op | source)
XLA Modules:
  0.0 33.8 jit_solution(7820979857166670900)
XLA Ops:
  0.7 3.5 %scatter.1 = (f32[3,160,128]{2,1,0:T(8,128)S(1)}, s32[2,160,128]{2,1,0:T(8,128)S(1)}, s32[2,2,16,128]{3,2,1,0:T(8,128)S(1)}, f32[3,8,128]{2,1,0:T(8,128)S(1)}, f...) custom-call(s32[1,1]{1,0:T(1,128)S(6)} %copy.9.live_ref, s32[2,3]{1,0:T(2,128)} %offsets_hbm.1, ...), custom_call_target="tpu_custom_call" | custom-call | tf_op jit(solution)/shard_map/scatter/pallas_call | solution.py:328
  4.2 2.8 %collective-permute-start = (f32[104,128]{1,0:T(8,128)S(1)}, f32[104,128]{1,0:T(8,128)S(1)}, u32[]{:S(2)}, u32[]{:S(2)}) collective-permute-start(f32[104,128]{1,0:T(8,128)S(1)} %get-tuple-element.27), channel_id=1, source_target_pairs={{0,8},{1,9},{2,10},{3,11},{4,12},{5,13},{6,14},{7,15},{8,0},{9,1},... | collective-permute-start | bytes 159752 | tf_op jit(solution)/shard_map/ppermute | solution.py:419
  7.0 4.3 %collective-permute-start.1 = (f32[104,128]{1,0:T(8,128)S(1)}, f32[104,128]{1,0:T(8,128)S(1)}, u32[]{:S(2)}, u32[]{:S(2)}) collective-permute-start(f32[104,128]{1,0:T(8,128)S(1)} %get-tuple-element.28), channel_id=1, source_target_pairs={{0,1},{1,0},{2,3},{3,2},{4,5},{5,4},{6,7},{7,6},{8,16},{9,17},{10,... | collective-permute-start | bytes 159752 | tf_op jit(solution)/shard_map/ppermute | solution.py:420
  11.3 1.0 %inner.4.rest_4_ = s32[2,160,128]{2,1,0:T(8,128)S(1)} custom-call(s32[1,1]{1,0:T(1,128)S(6)} %copy.9.live_ref, s32[2,160,128]{2,1,0:T(8,128)S(1)} %get-tuple-element.23.code_ref, s32[2,2,16,128]{3,2,1,0:T(8,128)S(1)} %get-tuple-element.24.axes_ref, f32[224,128]{1,0:T(8,128)S(1)} %get-tuple-element.26.sums_ref), custom_call_target="tpu_custom_call" | custom-call | bytes 8000000 | tf_op jit(solution)/shard_map/inner/pallas_call | solution.py:353
  12.3 0.0 collective-permute-done.rest_0_.rest_2_
  12.3 1.1 %collective-permute-done.1.rest_1_.rest_3_ = f32[104,128]{1,0:T(8,128)S(1)} collective-permute-done((f32[104,128]{1,0:T(8,128)S(1)}, f32[104,128]{1,0:T(8,128)S(1)}, u32[]{:S(2)}, u32[]{:S(2)}) %collective-permute-start.1) | collective-permute-done | bytes 53280 | tf_op jit(solution)/shard_map/ppermute | solution.py:420
  13.5 0.1 collective-permute-start.3
  13.6 2.9 %collective-permute-start.2 = (f32[32,128]{1,0:T(8,128)S(1)}, f32[32,128]{1,0:T(8,128)S(1)}, u32[]{:S(2)}, u32[]{:S(2)}) collective-permute-start(f32[32,128]{1,0:T(8,128)S(1)} %concatenate.10.edge_ref.first_edge_ref), channel_id=1, source_target_pairs={{0,7},{1,2},{2,1},{3,4},{4,3},{5,6},{6,5},{7,0},{8,15},{9,10},{10,... | collective-permute-start | bytes 49160 | tf_op jit(solution)/shard_map/ppermute | solution.py:427
  16.4 1.5 %inner.5.words_ref = s32[2,160,128]{2,1,0:T(8,128)S(1)} custom-call(s32[1,1]{1,0:T(1,128)S(6)} %copy.9.live_ref, s32[2,160,128]{2,1,0:T(8,128)S(1)} %get-tuple-element.23.code_ref, s32[2,2,16,128]{3,2,1,0:T(8,128)S(1)} %get-tuple-element.24.axes_ref, f32[224,128]{1,0:T(8,128)S(1)} %get-tuple-element.26.sums_ref, ...), custom_call_target="tpu_custom_call" | custom-call | bytes 8000000 | tf_op jit(solution)/shard_map/inner/pallas_call | solution.py:353
  18.0 0.0 collective-permute-done.3.d_ref.first_d_ref
  18.0 0.1 collective-permute-done.2.c_ref.first_c_ref
  18.1 2.7 %turn.2 = (f32[3,160,128]{2,1,0:T(8,128)S(1)}, f32[224,128]{1,0:T(8,128)S(1)}, f32[72,128]{1,0:T(8,128)S(1)}, f32[72,128]{1,0:T(8,128)S(1)}) custom-call(s32[1,1]{1,0:T(1,128)S(6)} %copy.9.live_ref, f32[3,160,128]{2,1,0:T(8,128)S(1)} %get-tuple-element.22.vel_ref, s32[2,160,128]{2,1,0:T(8,128)S(1)} %get-tuple-element.23.code_ref, ...), custom_call_target="tpu_custom_call" | custom-call | tf_op jit(solution)/shard_map/turn/pallas_call | solution.py:372
  20.8 0.9 %collective-permute-start.4 = (f32[72,128]{1,0:T(8,128)S(1)}, f32[72,128]{1,0:T(8,128)S(1)}, u32[]{:S(2)}, u32[]{:S(2)}) collective-permute-start(f32[72,128]{1,0:T(8,128)S(1)} %get-tuple-element.34), channel_id=1, source_target_pairs={{0,8},{1,9},{2,10},{3,11},{4,12},{5,13},{6,14},{7,15},{8,0},{9,1},... | collective-permute-start | bytes 110600 | tf_op jit(solution)/shard_map/ppermute | solution.py:419
  21.7 3.4 %collective-permute-start.5 = (f32[72,128]{1,0:T(8,128)S(1)}, f32[72,128]{1,0:T(8,128)S(1)}, u32[]{:S(2)}, u32[]{:S(2)}) collective-permute-start(f32[72,128]{1,0:T(8,128)S(1)} %get-tuple-element.35), channel_id=1, source_target_pairs={{0,1},{1,0},{2,3},{3,2},{4,5},{5,4},{6,7},{7,6},{8,16},{9,17},{10,... | collective-permute-start | bytes 110600 | tf_op jit(solution)/shard_map/ppermute | solution.py:420
  25.1 1.0 %inner.6.rest_4_ = s32[2,160,128]{2,1,0:T(8,128)S(1)} custom-call(s32[1,1]{1,0:T(1,128)S(6)} %copy.9.live_ref, s32[2,160,128]{2,1,0:T(8,128)S(1)} %get-tuple-element.23.code_ref, s32[2,2,16,128]{3,2,1,0:T(8,128)S(1)} %get-tuple-element.24.axes_ref, f32[224,128]{1,0:T(8,128)S(1)} %get-tuple-element.33.sums_ref), custom_call_target="tpu_custom_call" | custom-call | bytes 8000000 | tf_op jit(solution)/shard_map/inner/pallas_call | solution.py:353
  26.1 0.0 collective-permute-done.4.rest_0_
  26.1 1.7 %collective-permute-done.5.rest_1_ = f32[72,128]{1,0:T(8,128)S(1)} collective-permute-done((f32[72,128]{1,0:T(8,128)S(1)}, f32[72,128]{1,0:T(8,128)S(1)}, u32[]{:S(2)}, u32[]{:S(2)}) %collective-permute-start.5) | collective-permute-done | bytes 36896 | tf_op jit(solution)/shard_map/ppermute | solution.py:420
  27.8 0.1 collective-permute-start.7
  27.9 1.2 %collective-permute-start.6 = (f32[24,128]{1,0:T(8,128)S(1)}, f32[24,128]{1,0:T(8,128)S(1)}, u32[]{:S(2)}, u32[]{:S(2)}) collective-permute-start(f32[24,128]{1,0:T(8,128)S(1)} %fusion.3.edge_ref), channel_id=1, source_target_pairs={{0,7},{1,2},{2,1},{3,4},{4,3},{5,6},{6,5},{7,0},{8,15},{9,10},{10,... | collective-permute-start | bytes 36872 | tf_op jit(solution)/shard_map/ppermute | solution.py:427
  29.1 1.5 %inner.7.words_ref = s32[2,160,128]{2,1,0:T(8,128)S(1)} custom-call(s32[1,1]{1,0:T(1,128)S(6)} %copy.9.live_ref, s32[2,160,128]{2,1,0:T(8,128)S(1)} %get-tuple-element.23.code_ref, s32[2,2,16,128]{3,2,1,0:T(8,128)S(1)} %get-tuple-element.24.axes_ref, f32[224,128]{1,0:T(8,128)S(1)} %get-tuple-element.33.sums_ref, ...), custom_call_target="tpu_custom_call" | custom-call | bytes 8000000 | tf_op jit(solution)/shard_map/inner/pallas_call | solution.py:353
  30.6 0.0 collective-permute-done.7.d_ref
  30.6 1.7 %collective-permute-done.6.c_ref = f32[24,128]{1,0:T(8,128)S(1)} collective-permute-done((f32[24,128]{1,0:T(8,128)S(1)}, f32[24,128]{1,0:T(8,128)S(1)}, u32[]{:S(2)}, u32[]{:S(2)}) %collective-permute-start.6) | collective-permute-done | bytes 12320 | tf_op jit(solution)/shard_map/ppermute | solution.py:427
  32.3 1.5 %turn.3 = f32[3,160,128]{2,1,0:T(8,128)} custom-call(s32[1,1]{1,0:T(1,128)S(6)} %copy.9.live_ref, f32[3,160,128]{2,1,0:T(8,128)S(1)} %get-tuple-element.32.vel_ref, s32[2,160,128]{2,1,0:T(8,128)S(1)} %get-tuple-element.23.code_ref, s32[2,2,16,128]{3,2,1,0:T(8,128)S(1)} %get-tuple-element.24.axes_ref, f32[3,8,128]{2,1,0:T(8,128)S(1)} %get-tuple-element.25.table_ref, ...), custom_call_target="tpu_custom_call" | custom-call | tf_op jit(solution)/shard_map/turn/pallas_call | solution.py:372
  (9 shorter events, 0.1 us)
Async XLA Ops:
  4.2 8.1 %collective-permute-start = (f32[104,128]{1,0:T(8,128)S(1)}, f32[104,128]{1,0:T(8,128)S(1)}, u32[]{:S(2)}, u32[]{:S(2)}) collective-permute-start(f32[104,128]{1,0:T(8,128)S(1)} %get-tuple-element.27), channel_id=1, source_target_pairs={{0,8},{1,9},{2,10},{3,11},{4,12},{5,13},{6,14},{7,15},{8,0},{9,1},... | collective-permute-start | bytes 159752 | tf_op jit(solution)/shard_map/ppermute | solution.py:419
  7.0 6.4 %collective-permute-start.1 = (f32[104,128]{1,0:T(8,128)S(1)}, f32[104,128]{1,0:T(8,128)S(1)}, u32[]{:S(2)}, u32[]{:S(2)}) collective-permute-start(f32[104,128]{1,0:T(8,128)S(1)} %get-tuple-element.28), channel_id=1, source_target_pairs={{0,1},{1,0},{2,3},{3,2},{4,5},{5,4},{6,7},{7,6},{8,16},{9,17},{10,... | collective-permute-start | bytes 159752 | tf_op jit(solution)/shard_map/ppermute | solution.py:420
  13.5 4.5 %collective-permute-start.3 = (f32[32,128]{1,0:T(8,128)S(1)}, f32[32,128]{1,0:T(8,128)S(1)}, u32[]{:S(2)}, u32[]{:S(2)}) collective-permute-start(f32[32,128]{1,0:T(8,128)S(1)} %concatenate.10.edge_ref.first_edge_ref), channel_id=1, source_target_pairs={{0,1},{1,0},{2,3},{3,2},{4,5},{5,4},{6,7},{7,6},{8,9},{9,8},{10,11... | collective-permute-start | bytes 49160 | tf_op jit(solution)/shard_map/ppermute | solution.py:426
  13.6 4.5 %collective-permute-start.2 = (f32[32,128]{1,0:T(8,128)S(1)}, f32[32,128]{1,0:T(8,128)S(1)}, u32[]{:S(2)}, u32[]{:S(2)}) collective-permute-start(f32[32,128]{1,0:T(8,128)S(1)} %concatenate.10.edge_ref.first_edge_ref), channel_id=1, source_target_pairs={{0,7},{1,2},{2,1},{3,4},{4,3},{5,6},{6,5},{7,0},{8,15},{9,10},{10,... | collective-permute-start | bytes 49160 | tf_op jit(solution)/shard_map/ppermute | solution.py:427
  20.8 5.3 %collective-permute-start.4 = (f32[72,128]{1,0:T(8,128)S(1)}, f32[72,128]{1,0:T(8,128)S(1)}, u32[]{:S(2)}, u32[]{:S(2)}) collective-permute-start(f32[72,128]{1,0:T(8,128)S(1)} %get-tuple-element.34), channel_id=1, source_target_pairs={{0,8},{1,9},{2,10},{3,11},{4,12},{5,13},{6,14},{7,15},{8,0},{9,1},... | collective-permute-start | bytes 110600 | tf_op jit(solution)/shard_map/ppermute | solution.py:419
  21.7 6.1 %collective-permute-start.5 = (f32[72,128]{1,0:T(8,128)S(1)}, f32[72,128]{1,0:T(8,128)S(1)}, u32[]{:S(2)}, u32[]{:S(2)}) collective-permute-start(f32[72,128]{1,0:T(8,128)S(1)} %get-tuple-element.35), channel_id=1, source_target_pairs={{0,1},{1,0},{2,3},{3,2},{4,5},{5,4},{6,7},{7,6},{8,16},{9,17},{10,... | collective-permute-start | bytes 110600 | tf_op jit(solution)/shard_map/ppermute | solution.py:420
  27.8 2.9 %collective-permute-start.7 = (f32[24,128]{1,0:T(8,128)S(1)}, f32[24,128]{1,0:T(8,128)S(1)}, u32[]{:S(2)}, u32[]{:S(2)}) collective-permute-start(f32[24,128]{1,0:T(8,128)S(1)} %fusion.3.edge_ref), channel_id=1, source_target_pairs={{0,1},{1,0},{2,3},{3,2},{4,5},{5,4},{6,7},{7,6},{8,9},{9,8},{10,11... | collective-permute-start | bytes 36872 | tf_op jit(solution)/shard_map/ppermute | solution.py:426
  27.9 4.4 %collective-permute-start.6 = (f32[24,128]{1,0:T(8,128)S(1)}, f32[24,128]{1,0:T(8,128)S(1)}, u32[]{:S(2)}, u32[]{:S(2)}) collective-permute-start(f32[24,128]{1,0:T(8,128)S(1)} %fusion.3.edge_ref), channel_id=1, source_target_pairs={{0,7},{1,2},{2,1},{3,4},{4,3},{5,6},{6,5},{7,0},{8,15},{9,10},{10,... | collective-permute-start | bytes 36872 | tf_op jit(solution)/shard_map/ppermute | solution.py:427

commit v6 on v5

--- a/solution.py
+++ b/solution.py
@@ -250,7 +250,7 @@
     each_part(live_ref, part)
 
 
-def turn_kernel(step, live_ref, vel_ref, code_ref, axes_ref, table_ref, words_ref, edge_ref, c_ref, d_ref, first_edge_ref, first_c_ref, first_d_ref, *rest):
+def turn_kernel(step, live_ref, vel_ref, code_ref, axes_ref, table_ref, words_ref, edge_ref, d_ref, c_ref, first_edge_ref, first_d_ref, first_c_ref, *rest):
     last = step == STEPS - 1
     out_ref, total_ref, index_ref, first_ref, second_ref, got_ref = rest[:1] + rest[-8 + 3 * last:][:5]
     if not last:
@@ -428,7 +428,7 @@
         if step == 0:
             first_edge, first_c, first_d = edge, got_c, got_d
         words = inner_call(step, live, code, axes, sums, got_b, got_a, first_b, first_a, words)
-        done = turn_call(step, live, vel, code, axes, table, words, edge, got_c, got_d, first_edge, first_c, first_d)
+        done = turn_call(step, live, vel, code, axes, table, words, edge, got_d, got_c, first_edge, first_d, first_c)
         if step < STEPS - 1:
             vel, sums, a, b = done
         else:

time: 33.9 us -> 33.5 us (0.988)
  starting transfers between devices: 15.7 us -> 14.2 us
  waiting for transfers between devices: 4.53 us -> 5.42 us
    ppermute x2, starting transfers between devices: 4.11 us -> 1.23 us  [per_device(): got_c = lax.ppermute(edge, names, y_odd)]
    ppermute x2, waiting for transfers between devices: 1.74 us -> 3.14 us  [per_device(): got_c = lax.ppermute(edge, names, y_odd)]
    ppermute x2, starting transfers between devices: 0.18 us -> 1.48 us  [per_device(): got_d = lax.ppermute(edge, names, y_even)]
    ppermute x2, starting transfers between devices: 3.74 us -> 3.23 us  [per_device(): got_b = lax.ppermute(b, names, x_even)]
    ppermute x2, waiting for transfers between devices: 2.78 us -> 2.27 us  [per_device(): got_a = lax.ppermute(a, names, x_odd)]
    ppermute x2, starting transfers between devices: 7.7 us -> 8.21 us  [per_device(): got_a = lax.ppermute(a, names, x_odd)]
where the time goes in v6:
time: 33.5 us; the launch traced here: 33.1 us
  starting transfers between devices  14.2 us (42%)
  Pallas kernels  12.7 us (38%)
  waiting for transfers between devices  5.42 us (16%)
  between operations  0.75 us (2%)
    ppermute x2, starting transfers between devices, per_device(): got_a = lax.ppermute(a, names, x_odd)  8.21 us
    pallas_call x4, Pallas kernels, inner_call(): pl.pallas_call(functools.partial(inner_kernel, step), out_shape=i32(2, RO...  4.97 us
    pallas_call x2, Pallas kernels, turn_call(): pl.pallas_call(functools.partial(turn_kernel, step), out_shape=tuple(out_...  4.24 us
    pallas_call x1, Pallas kernels, scatter_call(): pl.pallas_call(scatter_kernel, out_shape=out_shape, in_specs=[SMEM] + [HB...  3.52 us
    ppermute x2, starting transfers between devices, per_device(): got_b = lax.ppermute(b, names, x_even)  3.23 us
    ppermute x2, waiting for transfers between devices, per_device(): got_c = lax.ppermute(edge, names, y_odd)  3.14 us
    ppermute x2, waiting for transfers between devices, per_device(): got_a = lax.ppermute(a, names, x_odd)  2.27 us
    ppermute x2, starting transfers between devices, per_device(): got_d = lax.ppermute(edge, names, y_even)  1.48 us
  transfers between devices with their start and end apart: 8, of which 4 were waited for; matrix products, arithmetic and copies ran while one was open for 0% of the time, Pallas kernels for 15%

profile of v6, /device:TPU:24, one launch (start us, length us, event | category | flops | bytes accessed | tf_op | source)
XLA Modules:
  0.0 33.1 jit_solution(15426542125473814874)
XLA Ops:
  0.7 3.5 %scatter.1 = (f32[3,160,128]{2,1,0:T(8,128)S(1)}, s32[2,160,128]{2,1,0:T(8,128)S(1)}, s32[2,2,16,128]{3,2,1,0:T(8,128)S(1)}, f32[3,8,128]{2,1,0:T(8,128)S(1)}, f...) custom-call(s32[1,1]{1,0:T(1,128)S(6)} %copy.9.live_ref, s32[2,3]{1,0:T(2,128)} %offsets_hbm.1, ...), custom_call_target="tpu_custom_call" | custom-call | tf_op jit(solution)/shard_map/scatter/pallas_call | solution.py:328
  4.2 2.8 %collective-permute-start = (f32[104,128]{1,0:T(8,128)S(1)}, f32[104,128]{1,0:T(8,128)S(1)}, u32[]{:S(2)}, u32[]{:S(2)}) collective-permute-start(f32[104,128]{1,0:T(8,128)S(1)} %get-tuple-element.27), channel_id=1, source_target_pairs={{0,8},{1,9},{2,10},{3,11},{4,12},{5,13},{6,14},{7,15},{8,0},{9,1},... | collective-permute-start | bytes 159752 | tf_op jit(solution)/shard_map/ppermute | solution.py:419
  7.0 4.3 %collective-permute-start.1 = (f32[104,128]{1,0:T(8,128)S(1)}, f32[104,128]{1,0:T(8,128)S(1)}, u32[]{:S(2)}, u32[]{:S(2)}) collective-permute-start(f32[104,128]{1,0:T(8,128)S(1)} %get-tuple-element.28), channel_id=1, source_target_pairs={{0,1},{1,0},{2,3},{3,2},{4,5},{5,4},{6,7},{7,6},{8,16},{9,17},{10,... | collective-permute-start | bytes 159752 | tf_op jit(solution)/shard_map/ppermute | solution.py:420
  11.3 1.0 %inner.4.rest_4_ = s32[2,160,128]{2,1,0:T(8,128)S(1)} custom-call(s32[1,1]{1,0:T(1,128)S(6)} %copy.9.live_ref, s32[2,160,128]{2,1,0:T(8,128)S(1)} %get-tuple-element.23.code_ref, s32[2,2,16,128]{3,2,1,0:T(8,128)S(1)} %get-tuple-element.24.axes_ref, f32[224,128]{1,0:T(8,128)S(1)} %get-tuple-element.26.sums_ref), custom_call_target="tpu_custom_call" | custom-call | bytes 8000000 | tf_op jit(solution)/shard_map/inner/pallas_call | solution.py:353
  12.3 0.0 collective-permute-done.rest_0_.rest_2_
  12.3 1.1 %collective-permute-done.1.rest_1_.rest_3_ = f32[104,128]{1,0:T(8,128)S(1)} collective-permute-done((f32[104,128]{1,0:T(8,128)S(1)}, f32[104,128]{1,0:T(8,128)S(1)}, u32[]{:S(2)}, u32[]{:S(2)}) %collective-permute-start.1) | collective-permute-done | bytes 53280 | tf_op jit(solution)/shard_map/ppermute | solution.py:420
  13.5 1.1 %collective-permute-start.3 = (f32[32,128]{1,0:T(8,128)S(1)}, f32[32,128]{1,0:T(8,128)S(1)}, u32[]{:S(2)}, u32[]{:S(2)}) collective-permute-start(f32[32,128]{1,0:T(8,128)S(1)} %concatenate.10.edge_ref.first_edge_ref), channel_id=1, source_target_pairs={{0,7},{1,2},{2,1},{3,4},{4,3},{5,6},{6,5},{7,0},{8,15},{9,10},{10,... | collective-permute-start | bytes 49160 | tf_op jit(solution)/shard_map/ppermute | solution.py:427
  14.6 0.6 %collective-permute-start.2 = (f32[32,128]{1,0:T(8,128)S(1)}, f32[32,128]{1,0:T(8,128)S(1)}, u32[]{:S(2)}, u32[]{:S(2)}) collective-permute-start(f32[32,128]{1,0:T(8,128)S(1)} %concatenate.10.edge_ref.first_edge_ref), channel_id=1, source_target_pairs={{0,1},{1,0},{2,3},{3,2},{4,5},{5,4},{6,7},{7,6},{8,9},{9,8},{10,11... | collective-permute-start | bytes 49160 | tf_op jit(solution)/shard_map/ppermute | solution.py:426
  15.2 1.5 %inner.5.words_ref = s32[2,160,128]{2,1,0:T(8,128)S(1)} custom-call(s32[1,1]{1,0:T(1,128)S(6)} %copy.9.live_ref, s32[2,160,128]{2,1,0:T(8,128)S(1)} %get-tuple-element.23.code_ref, s32[2,2,16,128]{3,2,1,0:T(8,128)S(1)} %get-tuple-element.24.axes_ref, f32[224,128]{1,0:T(8,128)S(1)} %get-tuple-element.26.sums_ref, ...), custom_call_target="tpu_custom_call" | custom-call | bytes 8000000 | tf_op jit(solution)/shard_map/inner/pallas_call | solution.py:353
  16.7 1.3 %collective-permute-done.3.c_ref.first_c_ref = f32[32,128]{1,0:T(8,128)S(1)} collective-permute-done((f32[32,128]{1,0:T(8,128)S(1)}, f32[32,128]{1,0:T(8,128)S(1)}, u32[]{:S(2)}, u32[]{:S(2)}) %collective-permute-start.3) | collective-permute-done | bytes 16416 | tf_op jit(solution)/shard_map/ppermute | solution.py:427
  17.9 0.0 collective-permute-done.2.d_ref.first_d_ref
  18.0 2.7 %turn.2 = (f32[3,160,128]{2,1,0:T(8,128)S(1)}, f32[224,128]{1,0:T(8,128)S(1)}, f32[72,128]{1,0:T(8,128)S(1)}, f32[72,128]{1,0:T(8,128)S(1)}) custom-call(s32[1,1]{1,0:T(1,128)S(6)} %copy.9.live_ref, f32[3,160,128]{2,1,0:T(8,128)S(1)} %get-tuple-element.22.vel_ref, s32[2,160,128]{2,1,0:T(8,128)S(1)} %get-tuple-element.23.code_ref, ...), custom_call_target="tpu_custom_call" | custom-call | tf_op jit(solution)/shard_map/turn/pallas_call | solution.py:372
  20.7 0.4 %collective-permute-start.4 = (f32[72,128]{1,0:T(8,128)S(1)}, f32[72,128]{1,0:T(8,128)S(1)}, u32[]{:S(2)}, u32[]{:S(2)}) collective-permute-start(f32[72,128]{1,0:T(8,128)S(1)} %get-tuple-element.34), channel_id=1, source_target_pairs={{0,8},{1,9},{2,10},{3,11},{4,12},{5,13},{6,14},{7,15},{8,0},{9,1},... | collective-permute-start | bytes 110600 | tf_op jit(solution)/shard_map/ppermute | solution.py:419
  21.1 3.9 %collective-permute-start.5 = (f32[72,128]{1,0:T(8,128)S(1)}, f32[72,128]{1,0:T(8,128)S(1)}, u32[]{:S(2)}, u32[]{:S(2)}) collective-permute-start(f32[72,128]{1,0:T(8,128)S(1)} %get-tuple-element.35), channel_id=1, source_target_pairs={{0,1},{1,0},{2,3},{3,2},{4,5},{5,4},{6,7},{7,6},{8,16},{9,17},{10,... | collective-permute-start | bytes 110600 | tf_op jit(solution)/shard_map/ppermute | solution.py:420
  25.0 1.0 %inner.6.rest_4_ = s32[2,160,128]{2,1,0:T(8,128)S(1)} custom-call(s32[1,1]{1,0:T(1,128)S(6)} %copy.9.live_ref, s32[2,160,128]{2,1,0:T(8,128)S(1)} %get-tuple-element.23.code_ref, s32[2,2,16,128]{3,2,1,0:T(8,128)S(1)} %get-tuple-element.24.axes_ref, f32[224,128]{1,0:T(8,128)S(1)} %get-tuple-element.33.sums_ref), custom_call_target="tpu_custom_call" | custom-call | bytes 8000000 | tf_op jit(solution)/shard_map/inner/pallas_call | solution.py:353
  26.0 0.0 collective-permute-done.4.rest_0_
  26.0 1.2 %collective-permute-done.5.rest_1_ = f32[72,128]{1,0:T(8,128)S(1)} collective-permute-done((f32[72,128]{1,0:T(8,128)S(1)}, f32[72,128]{1,0:T(8,128)S(1)}, u32[]{:S(2)}, u32[]{:S(2)}) %collective-permute-start.5) | collective-permute-done | bytes 36896 | tf_op jit(solution)/shard_map/ppermute | solution.py:420
  27.2 0.1 collective-permute-start.7
  27.3 0.9 %collective-permute-start.6 = (f32[24,128]{1,0:T(8,128)S(1)}, f32[24,128]{1,0:T(8,128)S(1)}, u32[]{:S(2)}, u32[]{:S(2)}) collective-permute-start(f32[24,128]{1,0:T(8,128)S(1)} %fusion.3.edge_ref), channel_id=1, source_target_pairs={{0,1},{1,0},{2,3},{3,2},{4,5},{5,4},{6,7},{7,6},{8,9},{9,8},{10,11... | collective-permute-start | bytes 36872 | tf_op jit(solution)/shard_map/ppermute | solution.py:426
  28.2 1.5 %inner.7.words_ref = s32[2,160,128]{2,1,0:T(8,128)S(1)} custom-call(s32[1,1]{1,0:T(1,128)S(6)} %copy.9.live_ref, s32[2,160,128]{2,1,0:T(8,128)S(1)} %get-tuple-element.23.code_ref, s32[2,2,16,128]{3,2,1,0:T(8,128)S(1)} %get-tuple-element.24.axes_ref, f32[224,128]{1,0:T(8,128)S(1)} %get-tuple-element.33.sums_ref, ...), custom_call_target="tpu_custom_call" | custom-call | bytes 8000000 | tf_op jit(solution)/shard_map/inner/pallas_call | solution.py:353
  29.7 1.9 %collective-permute-done.7.c_ref = f32[24,128]{1,0:T(8,128)S(1)} collective-permute-done((f32[24,128]{1,0:T(8,128)S(1)}, f32[24,128]{1,0:T(8,128)S(1)}, u32[]{:S(2)}, u32[]{:S(2)}) %collective-permute-start.7) | collective-permute-done | bytes 12320 | tf_op jit(solution)/shard_map/ppermute | solution.py:427
  31.6 0.0 collective-permute-done.6.d_ref
  31.6 1.5 %turn.3 = f32[3,160,128]{2,1,0:T(8,128)} custom-call(s32[1,1]{1,0:T(1,128)S(6)} %copy.9.live_ref, f32[3,160,128]{2,1,0:T(8,128)S(1)} %get-tuple-element.32.vel_ref, s32[2,160,128]{2,1,0:T(8,128)S(1)} %get-tuple-element.23.code_ref, s32[2,2,16,128]{3,2,1,0:T(8,128)S(1)} %get-tuple-element.24.axes_ref, f32[3,8,128]{2,1,0:T(8,128)S(1)} %get-tuple-element.25.table_ref, ...), custom_call_target="tpu_custom_call" | custom-call | tf_op jit(solution)/shard_map/turn/pallas_call | solution.py:372
  (9 shorter events, 0.1 us)
Async XLA Ops:
  4.2 8.1 %collective-permute-start = (f32[104,128]{1,0:T(8,128)S(1)}, f32[104,128]{1,0:T(8,128)S(1)}, u32[]{:S(2)}, u32[]{:S(2)}) collective-permute-start(f32[104,128]{1,0:T(8,128)S(1)} %get-tuple-element.27), channel_id=1, source_target_pairs={{0,8},{1,9},{2,10},{3,11},{4,12},{5,13},{6,14},{7,15},{8,0},{9,1},... | collective-permute-start | bytes 159752 | tf_op jit(solution)/shard_map/ppermute | solution.py:419
  7.0 6.4 %collective-permute-start.1 = (f32[104,128]{1,0:T(8,128)S(1)}, f32[104,128]{1,0:T(8,128)S(1)}, u32[]{:S(2)}, u32[]{:S(2)}) collective-permute-start(f32[104,128]{1,0:T(8,128)S(1)} %get-tuple-element.28), channel_id=1, source_target_pairs={{0,1},{1,0},{2,3},{3,2},{4,5},{5,4},{6,7},{7,6},{8,16},{9,17},{10,... | collective-permute-start | bytes 159752 | tf_op jit(solution)/shard_map/ppermute | solution.py:420
  13.5 4.5 %collective-permute-start.3 = (f32[32,128]{1,0:T(8,128)S(1)}, f32[32,128]{1,0:T(8,128)S(1)}, u32[]{:S(2)}, u32[]{:S(2)}) collective-permute-start(f32[32,128]{1,0:T(8,128)S(1)} %concatenate.10.edge_ref.first_edge_ref), channel_id=1, source_target_pairs={{0,7},{1,2},{2,1},{3,4},{4,3},{5,6},{6,5},{7,0},{8,15},{9,10},{10,... | collective-permute-start | bytes 49160 | tf_op jit(solution)/shard_map/ppermute | solution.py:427
  14.6 3.3 %collective-permute-start.2 = (f32[32,128]{1,0:T(8,128)S(1)}, f32[32,128]{1,0:T(8,128)S(1)}, u32[]{:S(2)}, u32[]{:S(2)}) collective-permute-start(f32[32,128]{1,0:T(8,128)S(1)} %concatenate.10.edge_ref.first_edge_ref), channel_id=1, source_target_pairs={{0,1},{1,0},{2,3},{3,2},{4,5},{5,4},{6,7},{7,6},{8,9},{9,8},{10,11... | collective-permute-start | bytes 49160 | tf_op jit(solution)/shard_map/ppermute | solution.py:426
  20.7 5.3 %collective-permute-start.4 = (f32[72,128]{1,0:T(8,128)S(1)}, f32[72,128]{1,0:T(8,128)S(1)}, u32[]{:S(2)}, u32[]{:S(2)}) collective-permute-start(f32[72,128]{1,0:T(8,128)S(1)} %get-tuple-element.34), channel_id=1, source_target_pairs={{0,8},{1,9},{2,10},{3,11},{4,12},{5,13},{6,14},{7,15},{8,0},{9,1},... | collective-permute-start | bytes 110600 | tf_op jit(solution)/shard_map/ppermute | solution.py:419
  21.1 6.1 %collective-permute-start.5 = (f32[72,128]{1,0:T(8,128)S(1)}, f32[72,128]{1,0:T(8,128)S(1)}, u32[]{:S(2)}, u32[]{:S(2)}) collective-permute-start(f32[72,128]{1,0:T(8,128)S(1)} %get-tuple-element.35), channel_id=1, source_target_pairs={{0,1},{1,0},{2,3},{3,2},{4,5},{5,4},{6,7},{7,6},{8,16},{9,17},{10,... | collective-permute-start | bytes 110600 | tf_op jit(solution)/shard_map/ppermute | solution.py:420
  27.2 4.4 %collective-permute-start.7 = (f32[24,128]{1,0:T(8,128)S(1)}, f32[24,128]{1,0:T(8,128)S(1)}, u32[]{:S(2)}, u32[]{:S(2)}) collective-permute-start(f32[24,128]{1,0:T(8,128)S(1)} %fusion.3.edge_ref), channel_id=1, source_target_pairs={{0,7},{1,2},{2,1},{3,4},{4,3},{5,6},{6,5},{7,0},{8,15},{9,10},{10,... | collective-permute-start | bytes 36872 | tf_op jit(solution)/shard_map/ppermute | solution.py:427
  27.3 4.3 %collective-permute-start.6 = (f32[24,128]{1,0:T(8,128)S(1)}, f32[24,128]{1,0:T(8,128)S(1)}, u32[]{:S(2)}, u32[]{:S(2)}) collective-permute-start(f32[24,128]{1,0:T(8,128)S(1)} %fusion.3.edge_ref), channel_id=1, source_target_pairs={{0,1},{1,0},{2,3},{3,2},{4,5},{5,4},{6,7},{7,6},{8,9},{9,8},{10,11... | collective-permute-start | bytes 36872 | tf_op jit(solution)/shard_map/ppermute | solution.py:426
